TPU v7x, 256 devices: a whole 4x4x8 slice. The times are simulated.
256 devices in a mesh: lang: 8 (over z), shard: 32 (over y, x, core).
Axes of the slice: x: 4, y: 4, z: 8, core: 2. Of those that a mesh axis runs over, the one named last changes fastest.
Arguments:
- memory: bfloat16 [256, 16, 4096], P(('lang', 'shard')), may hold values from -6 to 6
- lang_id: int32 [256], P(('lang', 'shard')), may hold values from 0 to 7, as said below
- src_len: int32 [256], P(('lang', 'shard')), may hold values from 4 to 16
- tgt_len: int32 [256], P(('lang', 'shard')), may hold values from 32 to 128
- queries: bfloat16 [8, 64, 128, 4096], P('lang', 'shard'), may hold values from -64 to 64
- key_weight: bfloat16 [8, 4096, 4096], P('lang', None, 'shard'), may hold values from -1 to 1
- value_weight: bfloat16 [8, 4096, 4096], P('lang', None, 'shard'), may hold values from -0.09375 to 0.09375
- grad_context: bfloat16 [8, 64, 128, 4096], P('lang', 'shard'), may hold values from -6 to 6
Outputs:
- context: bfloat16 [8, 64, 128, 4096], P('lang', 'shard')
- grad_queries: bfloat16 [8, 64, 128, 4096], P('lang', 'shard')
- grad_memory: bfloat16 [256, 16, 4096], P(('lang', 'shard'))
- grad_key_weight: bfloat16 [8, 4096, 4096], P('lang', None, 'shard')
- grad_value_weight: bfloat16 [8, 4096, 4096], P('lang', None, 'shard')
Inputs may be any that keep to these rules, and one draw needn't show every extreme that they name: `lang_id`: among the 8 sentences of one column b (indices a * 32 + b), no language is named more than 2 times, and in every column some language is named exactly 2 times.
All inputs are finite; a program needn't handle non-finite values.
Results may differ from a plain program's by a relative error of at most 0.025.
The roundings to bfloat16 on the way count: a program that leaves them out, or rounds other values in their place, can miss the bound.
Values may be sent and summed in bfloat16 or wider, within the bound.
No kernel may reach another device: no remote copies, remote signals or barrier semaphores. Data moves between devices by JAX's collectives and lax.ppermute only.
A program may use at most 128 MiB of HBM per device.

v0:
```python
import functools

import jax
import jax.numpy as jnp
from jax import lax
from jax.experimental import pallas as pl
from jax.experimental.pallas import tpu as pltpu
from jax.sharding import Mesh, PartitionSpec as P

HEAD = 128
SRC = 16
TGT = 128
WIDTH = 4096
HALF = WIDTH // 2
PLANES = 8
SIDE = 4
CHIPS = SIDE * SIDE
ROWS = 32
GROUP = 8
MASKED = -1e30
BF = jnp.bfloat16
F32 = jnp.float32
PLANE = ("y", "x")
FAR_FIRST = (0, 4, 3, 5, 2, 6, 1, 7)
TAKEN = ((0, 0), (1, 0), (0, 2), (1, 2), (0, 1), (1, 1), (0, 3), (1, 3))
VMEM = pl.BlockSpec(memory_space=pltpu.VMEM)
SMEM = pl.BlockSpec(memory_space=pltpu.SMEM)
ANY = pl.BlockSpec(memory_space=pl.ANY)


def params(mib):
    return pltpu.CompilerParams(vmem_limit_bytes=mib << 20)


def cost(products, mib):
    return pl.CostEstimate(flops=2 * products, bytes_accessed=mib << 20, transcendentals=0)


def shift(value, axis, step):
    n = lax.axis_size(axis)
    return lax.ppermute(value, axis, [(i, (i + step) % n) for i in range(n)])


def dot(a, b, ca, cb):
    return lax.dot_general(a, b, (((ca,), (cb,)), ((), ())), preferred_element_type=F32)


def route_kernel(place_ref, *refs):
    sentences, (left_ref, right_ref, rank_ref, lens_ref) = refs[:PLANES], refs[PLANES:]
    sentences = [sentences[FAR_FIRST.index(d)] for d in range(PLANES)]
    plane = place_ref[0]
    plane_f = plane.astype(F32)
    match, rank = [], []
    for ref in sentences:
        lang = ref[:, WIDTH : WIDTH + HEAD].astype(F32)
        match.append(jnp.where(lang == plane_f, 1.0, 0.0))
    origin = [lax.rem(plane - d + PLANES, PLANES) for d in range(PLANES)]
    for d in range(PLANES):
        before = jnp.zeros((SRC, HEAD), F32)
        for e in range(PLANES):
            if e != d:
                before += jnp.where(origin[e] < origin[d], match[e], 0.0)
        rank.append(jnp.where(match[d] > 0.5, before, -1.0))
        rank_ref[d] = rank[d][:8]
    for r in range(2):
        src = jnp.zeros((8, HEAD), F32)
        tgt = jnp.zeros((8, HEAD), F32)
        total = jnp.zeros((SRC, WIDTH), BF)
        for d, ref in enumerate(sentences):
            here = rank[d] == float(r)
            src = jnp.where(here[:8], ref[:8, WIDTH + HEAD : WIDTH + 2 * HEAD].astype(F32), src)
            tgt = jnp.where(here[:8], ref[:8, WIDTH + 2 * HEAD :].astype(F32), tgt)
            wide = jnp.where(here[:, :1], 1.0, 0.0).astype(BF)
            total = jnp.where(wide > 0.5, ref[:, :WIDTH], total)
        lens_ref[r] = src
        lens_ref[2 + r] = tgt
        left_ref[r * SRC : (r + 1) * SRC] = total[:, :HALF]
        right_ref[r * SRC : (r + 1) * SRC] = total[:, HALF:]


def join_kernel(*refs):
    parts, outs, sems = refs[: 2 * SIDE], refs[2 * SIDE : 2 * SIDE + 2], refs[2 * SIDE + 2]
    copies = [
        pltpu.make_async_copy(part, outs[half].at[pl.ds(d * ROWS, ROWS)], sems.at[i])
        for i, (part, (half, d)) in enumerate(zip(parts, TAKEN))
    ]
    for copy in copies:
        copy.start()
    for copy in copies:
        copy.wait()


def shift_both(values, axes, sign, order):
    moved = [[terms[0], None, None, None] for terms in values]
    for half, d in order:
        if d:
            moved[half][d] = shift(values[half][d], axes[half], sign * d)
    return moved


def project_kernel(place_ref, *refs):
    blocks, (own_ref, other_ref, out_ref) = refs[: 2 * SIDE], refs[2 * SIDE : 2 * SIDE + 3]
    blocks = [blocks[TAKEN.index(divmod(i, SIDE))] for i in range(2 * SIDE)]
    rows, weight, part, weight_sems, row_sems = refs[2 * SIDE + 3 :]
    weight_copies, row_copies = [], []
    for half in range(2):
        for i, ref in enumerate((own_ref, other_ref)):
            weight_copies.append(
                pltpu.make_async_copy(
                    ref.at[pl.ds(half * HALF, HALF)],
                    weight.at[half, i],
                    weight_sems.at[2 * half + i],
                )
            )
    for i in range(2 * SIDE):
        span = pl.ds((i % SIDE) * SIDE * ROWS, SIDE * ROWS)
        row_copies.append(
            pltpu.make_async_copy(blocks[i], rows.at[i // SIDE, span], row_sems.at[i])
        )
    for half in range(2):
        for copy in weight_copies[2 * half : 2 * half + 2] + row_copies[SIDE * half : SIDE * half + SIDE]:
            copy.start()
    for half in range(2):
        for copy in weight_copies[2 * half : 2 * half + 2] + row_copies[SIDE * half : SIDE * half + SIDE]:
            copy.wait()
        for i in range(2):
            part[half, :, i * 2 * HEAD : (i + 1) * 2 * HEAD] = dot(rows[half], weight[half, i], 1, 0)
    y, x = place_ref[1], place_ref[2]
    for dy in range(SIDE):
        for dx in range(SIDE):
            a, b = (dy * SIDE + dx) * ROWS, (dx * SIDE + dy) * ROWS
            total = part[0, a : a + ROWS] + part[1, b : b + ROWS]
            chip = lax.rem(y - dy + SIDE, SIDE) * SIDE + lax.rem(x - dx + SIDE, SIDE)
            out_ref[chip] = total.astype(BF)


def attend_kernel(place_ref, lens_ref, q_ref, g_ref, kv_ref, ctx_ref, gq_ref, gkv_ref, keys, values):
    swapped = place_ref[4] == 1
    scaling = HEAD ** (-0.5)
    split = (GROUP, SRC, TGT)

    @pl.when(pl.program_id(0) == 0)
    def _():
        keys[...] = jnp.zeros_like(keys)
        values[...] = jnp.zeros_like(values)

    for s in range(2):
        slot = slice(s * SRC, (s + 1) * SRC)
        for h in range(GROUP):
            rows, cols = slice(h * SRC, (h + 1) * SRC), slice(h * HEAD, (h + 1) * HEAD)
            own, other = (h % 2) * 2 * HEAD, (1 - h % 2) * 2 * HEAD
            for start, block in ((0, keys), (HEAD, values)):
                block[s, rows, cols] = jnp.where(
                    swapped,
                    kv_ref[h // 2, slot, other + start : other + start + HEAD],
                    kv_ref[h // 2, slot, own + start : own + start + HEAD],
                )
    grads = []
    for s in range(2):
        src = jnp.maximum(lens_ref[s][:1], 1.0)[None]
        tgt = lens_ref[2 + s][:1, :1]
        q = q_ref[s]
        scores = (dot(keys[s], q, 1, 1) * scaling).reshape(split)
        key_index = lax.broadcasted_iota(jnp.int32, split, 1).astype(F32)
        scores = jnp.where(key_index < src, scores, MASKED)
        shifted = jnp.exp(scores - jnp.max(scores, axis=1, keepdims=True))
        attention = shifted / jnp.sum(shifted, axis=1, keepdims=True)
        attention_bf = attention.reshape(GROUP * SRC, TGT).astype(BF)
        row_index = lax.broadcasted_iota(jnp.int32, (TGT, 1), 0).astype(F32)
        valid = row_index < tgt
        valid_bf = jnp.where(valid, 1.0, 0.0).astype(BF)
        context = dot(attention_bf, values[s], 0, 0)
        ctx_ref[s] = jnp.where(valid, context, 0.0).astype(BF)
        g = g_ref[s]
        grad_masked = jnp.where(valid_bf > 0.5, g, jnp.zeros_like(g))
        grad_values = dot(attention_bf, grad_masked, 1, 0)
        grad_attention = dot(values[s], grad_masked, 1, 1).reshape(split)
        row_dot = jnp.sum(attention * grad_attention, axis=1, keepdims=True)
        grad_scores = (attention * (grad_attention - row_dot)).reshape(GROUP * SRC, TGT).astype(BF)
        gq_ref[s] = (dot(grad_scores, keys[s], 0, 0) * scaling).astype(BF)
        grad_keys = dot(grad_scores, q, 1, 0) * scaling
        grads.append((grad_keys, grad_values))
    for s in range(2):
        slot = slice(s * SRC, (s + 1) * SRC)
        for p in range(GROUP // 2):
            for start, grad in ((0, grads[s][0]), (HEAD, grads[s][1])):
                low, high = (
                    grad[h * SRC : (h + 1) * SRC, h * HEAD : (h + 1) * HEAD].astype(BF)
                    for h in (2 * p, 2 * p + 1)
                )
                gkv_ref[p, slot, start : start + HEAD] = jnp.where(swapped, high, low)
                start += 2 * HEAD
                gkv_ref[p, slot, start : start + HEAD] = jnp.where(swapped, low, high)


def chip_at(place_ref, dy, dx):
    y, x = place_ref[1], place_ref[2]
    return lax.rem(y - dy + SIDE, SIDE) * SIDE + lax.rem(x - dx + SIDE, SIDE)


def reorder_kernel(place_ref, grads_ref, by_y_ref, by_x_ref):
    for dy in range(SIDE):
        for dx in range(SIDE):
            block = grads_ref[chip_at(place_ref, dy, dx)]
            by_y_ref[dy * SIDE + dx] = block
            by_x_ref[dx * SIDE + dy] = block


def partial_kernel(along_y, place_ref, grads_ref, own_ref, other_ref, *refs):
    outs, grads = refs[:SIDE], refs[SIDE]

    @pl.when(pl.program_id(0) == 0)
    def _():
        for d in range(SIDE):
            for e in range(SIDE):
                chip = chip_at(place_ref, *((d, e) if along_y else (e, d)))
                start = (d * SIDE + e) * ROWS
                grads[start : start + ROWS] = grads_ref[chip]

    total = dot(grads[:, : 2 * HEAD], own_ref[...], 1, 1)
    total += dot(grads[:, 2 * HEAD :], other_ref[...], 1, 1)
    for d, out in enumerate(outs):
        out[...] = total[d * SIDE * ROWS : (d + 1) * SIDE * ROWS].astype(BF)


def weight_kernel(by_y_ref, by_x_ref, *refs):
    blocks, (own_ref, other_ref) = refs[: 2 * SIDE], refs[2 * SIDE :]
    step = pl.program_id(0)
    for half, grads in enumerate((by_y_ref, by_x_ref)):

        @pl.when((step >= half * SIDE) & (step < (half + 1) * SIDE))
        def _():
            rows = jnp.concatenate([ref[...] for ref in blocks[half * SIDE : (half + 1) * SIDE]], axis=0)
            total = dot(rows, grads[...], 0, 0).astype(BF)
            own_ref[...] = total[:, : 2 * HEAD]
            other_ref[...] = total[:, 2 * HEAD :]


def give_back_kernel(rank_ref, a_ref, b_ref, *outs):
    for d, out in enumerate(outs):
        first = jnp.where(rank_ref[d][:1, :1] < 0.5, 1.0, 0.0).astype(BF)
        for i, ref in enumerate((a_ref, b_ref)):
            cols = slice(i * HALF, (i + 1) * HALF)
            out[:, cols] = jnp.where(first > 0.5, ref[:SRC], ref[SRC:])


def pick_kernel(place_ref, *refs):
    candidates, out_ref = refs[:PLANES], refs[PLANES]
    for d, ref in zip(FAR_FIRST, candidates):

        @pl.when(place_ref[3] == d)
        def _():
            out_ref[...] = ref[...]


def local(memory, lang_id, src_len, tgt_len, queries, key_weight, value_weight, grad_context):
    plane, y, x = lax.axis_index("lang"), lax.axis_index("y"), lax.axis_index("x")
    core = lax.axis_index("core")
    ahead = lax.rem(lang_id[0] - plane + PLANES, PLANES)
    place = jnp.stack([plane, y, x, ahead, core]).astype(jnp.int32)

    def spread(number):
        return jnp.broadcast_to(number.astype(BF), (SRC, HEAD))

    with jax.named_scope("sentences_over_lang"):
        sentence = jnp.concatenate(
            [memory[0], spread(lang_id[0]), spread(src_len[0]), spread(tgt_len[0])], axis=1
        )
        column = [sentence] + [shift(sentence, "lang", d) for d in FAR_FIRST[1:]]

    with jax.named_scope("weights_of_chip"):
        key_own, value_own, _ = lax.optimization_barrier((key_weight[0], value_weight[0], sentence))
        own_weight = jnp.concatenate([key_own, value_own], axis=1)
        other_weight = shift(own_weight, "core", 1)

    with jax.named_scope("route"):
        left, right, rank, lens = pl.pallas_call(
            route_kernel,
            out_shape=(
                jax.ShapeDtypeStruct((ROWS, HALF), BF),
                jax.ShapeDtypeStruct((ROWS, HALF), BF),
                jax.ShapeDtypeStruct((PLANES, 8, HEAD), F32),
                jax.ShapeDtypeStruct((4, 8, HEAD), F32),
            ),
            in_specs=[SMEM] + [VMEM] * PLANES,
            out_specs=(VMEM,) * 4,
            compiler_params=params(16),
        )(place, *column)

    with jax.named_scope("gather_rows"):
        left, right, own_weight, other_weight = lax.optimization_barrier(
            (left, right, own_weight, other_weight)
        )
        parts = shift_both([[left] * SIDE, [right] * SIDE], ("x", "y"), 1, TAKEN)
        lines = pl.pallas_call(
            join_kernel,
            out_shape=(jax.ShapeDtypeStruct((SIDE * ROWS, HALF), BF),) * 2,
            in_specs=[ANY] * (2 * SIDE),
            out_specs=(ANY, ANY),
            scratch_shapes=[pltpu.SemaphoreType.DMA((2 * SIDE,))],
            compiler_params=params(1),
        )(*[parts[half][d] for half, d in TAKEN])
        blocks = shift_both([[line] * SIDE for line in lines], ("y", "x"), 1, TAKEN)
        blocks = [*blocks[0], *blocks[1]]

    with jax.named_scope("project"):
        projected = pl.pallas_call(
            project_kernel,
            out_shape=jax.ShapeDtypeStruct((CHIPS, ROWS, 4 * HEAD), BF),
            in_specs=[SMEM] + [ANY] * (2 * SIDE + 2),
            out_specs=VMEM,
            scratch_shapes=[
                pltpu.VMEM((2, CHIPS * ROWS, HALF), BF),
                pltpu.VMEM((2, 2, HALF, 2 * HEAD), BF),
                pltpu.VMEM((2, CHIPS * ROWS, 4 * HEAD), F32),
                pltpu.SemaphoreType.DMA((4,)),
                pltpu.SemaphoreType.DMA((2 * SIDE,)),
            ],
            compiler_params=params(40),
        )(place, *[blocks[half * SIDE + d] for half, d in TAKEN], own_weight, other_weight)

    with jax.named_scope("rows_to_slots"):
        slot_rows = lax.all_to_all(projected, PLANE, 0, 0, tiled=True)

    with jax.named_scope("attend"):
        groups = WIDTH // (GROUP * HEAD)
        wide = pl.BlockSpec((2, TGT, GROUP * HEAD), lambda g: (0, 0, g))
        narrow = pl.BlockSpec((GROUP // 2, ROWS, 4 * HEAD), lambda g: (g, 0, 0))
        context, grad_queries, slot_grads = pl.pallas_call(
            attend_kernel,
            grid=(groups,),
            out_shape=(
                jax.ShapeDtypeStruct((2, TGT, WIDTH), BF),
                jax.ShapeDtypeStruct((2, TGT, WIDTH), BF),
                jax.ShapeDtypeStruct((CHIPS, ROWS, 4 * HEAD), BF),
            ),
            in_specs=[SMEM, VMEM, wide, wide, narrow],
            out_specs=(wide, wide, narrow),
            scratch_shapes=[
                pltpu.VMEM((2, GROUP * SRC, GROUP * HEAD), BF),
                pltpu.VMEM((2, GROUP * SRC, GROUP * HEAD), BF),
            ],
            compiler_params=params(58),
        )(place, lens, queries[0], grad_context[0], slot_rows)

    with jax.named_scope("grads_to_heads"):
        head_grads = lax.all_to_all(slot_grads, PLANE, 0, 0, tiled=True)

    with jax.named_scope("sum_rows"):
        tile = HALF // SIDE
        partial = []
        for half, first in enumerate(("x", "y")):
            weight_spec = pl.BlockSpec((tile, 2 * HEAD), lambda t, half=half: (half * SIDE + t, 0))
            terms = pl.pallas_call(
                functools.partial(partial_kernel, first == "y"),
                grid=(SIDE,),
                out_shape=(jax.ShapeDtypeStruct((SIDE * ROWS, HALF), BF),) * SIDE,
                in_specs=[SMEM, VMEM, weight_spec, weight_spec],
                out_specs=(pl.BlockSpec((SIDE * ROWS, tile), lambda t: (0, t)),) * SIDE,
                scratch_shapes=[pltpu.VMEM((CHIPS * ROWS, 4 * HEAD), BF)],
                compiler_params=params(24),
            )(place, head_grads, own_weight, other_weight)
            partial.append(terms)
        arrived = shift_both(partial, ("x", "y"), -1, TAKEN)

    with jax.named_scope("weight_grads"):
        head_grads, _ = lax.optimization_barrier((head_grads, partial))
        by_y, by_x = pl.pallas_call(
            reorder_kernel,
            out_shape=(jax.ShapeDtypeStruct((CHIPS, ROWS, 4 * HEAD), BF),) * 2,
            in_specs=[SMEM, VMEM],
            out_specs=(VMEM, VMEM),
            compiler_params=params(16),
        )(place, head_grads)
        block_specs = [
            pl.BlockSpec(
                (SIDE * ROWS, tile),
                lambda t, low=half * SIDE: (0, jnp.clip(t - low, 0, SIDE - 1)),
            )
            for half in range(2)
            for _ in range(SIDE)
        ]
        keep, send = pl.pallas_call(
            weight_kernel,
            grid=(2 * SIDE,),
            out_shape=(jax.ShapeDtypeStruct((WIDTH, 2 * HEAD), BF),) * 2,
            in_specs=[VMEM, VMEM] + block_specs,
            out_specs=(pl.BlockSpec((tile, 2 * HEAD), lambda t: (t, 0)),) * 2,
            compiler_params=params(32),
            cost_estimate=cost(CHIPS * ROWS * WIDTH * 4 * HEAD, 16),
        )(by_y.reshape(CHIPS * ROWS, 4 * HEAD), by_x.reshape(CHIPS * ROWS, 4 * HEAD), *blocks)
        both = shift(send, "core", 1)
        weight_grads = [
            (keep[:, cols].astype(F32) + both[:, cols].astype(F32)).astype(BF)
            for cols in (slice(0, HEAD), slice(HEAD, 2 * HEAD))
        ]

    with jax.named_scope("sum_rows"):
        lines = [sum(term.astype(F32) for term in terms).astype(BF) for terms in arrived]
        terms = [[line[d * ROWS : (d + 1) * ROWS] for d in range(SIDE)] for line in lines]
        arrived = shift_both(terms, ("y", "x"), -1, TAKEN)
        summed = [sum(term.astype(F32) for term in terms).astype(BF) for terms in arrived]
        summed, weight_grads = lax.optimization_barrier((summed, weight_grads))

    with jax.named_scope("sentences_back"):
        sends = pl.pallas_call(
            give_back_kernel,
            out_shape=(jax.ShapeDtypeStruct((SRC, WIDTH), BF),) * PLANES,
            in_specs=[VMEM] * 3,
            out_specs=(VMEM,) * PLANES,
            compiler_params=params(16),
        )(rank, *summed)
        candidates = [sends[0]] + [shift(sends[d], "lang", -d) for d in FAR_FIRST[1:]]
        grad_memory = pl.pallas_call(
            pick_kernel,
            out_shape=jax.ShapeDtypeStruct((SRC, WIDTH), BF),
            in_specs=[SMEM] + [VMEM] * PLANES,
            out_specs=VMEM,
            compiler_params=params(16),
        )(place, *candidates)

    return (
        context[None],
        grad_queries[None],
        grad_memory[None],
        weight_grads[0][None],
        weight_grads[1][None],
    )


def solution(mesh):
    planes = mesh.shape["lang"]
    grid = Mesh(mesh.devices.reshape(planes, SIDE, SIDE, 2), ("lang", "y", "x", "core"))
    shard = ("y", "x", "core")
    every = ("lang", "y", "x", "core")
    return jax.shard_map(
        local,
        mesh=grid,
        in_specs=(
            P(every, None, None),
            P(every),
            P(every),
            P(every),
            P("lang", shard, None, None),
            P("lang", None, shard),
            P("lang", None, shard),
            P("lang", shard, None, None),
        ),
        out_specs=(
            P("lang", shard, None, None),
            P("lang", shard, None, None),
            P(every, None, None),
            P("lang", None, shard),
            P("lang", None, shard),
        ),
        check_vma=False,
    )
```

profile of v0, /device:TPU:32, one launch (start us, length us, event | category | flops | bytes accessed | tf_op | source)
XLA Modules:
  0.0 203.7 jit_solution(17346718446736435945)
XLA Ops:
  3.7 1.4 constant_dynamic-update-slice_fusion.1
  5.5 6.4 %collective-permute-start = (bf16[16,4480]{1,0:T(8,128)(2,1)S(1)}, bf16[16,4480]{1,0:T(8,128)(2,1)S(1)}, u32[]{:S(2)}, u32[]{:S(2)}) collective-permute-start(bf16[16,4480]{1,0:T(8,128)(2,1)S(1)} %maximum_maximum_fusion.refs_0_), channel_id=1, source_target_pairs={{0,128},{32,160},{64,192},{96,224},{128,0},{160,32},{192,64},{224,... | collective-permute-start | bytes 430088 | tf_op jit(solution)/shard_map/sentences_over_lang/ppermute | solution.py:41
  11.9 5.0 %collective-permute-start.2 = (bf16[16,4480]{1,0:T(8,128)(2,1)S(1)}, bf16[16,4480]{1,0:T(8,128)(2,1)S(1)}, u32[]{:S(2)}, u32[]{:S(2)}) collective-permute-start(bf16[16,4480]{1,0:T(8,128)(2,1)S(1)} %maximum_maximum_fusion.refs_0_), channel_id=1, source_target_pairs={{0,160},{32,192},{64,224},{96,0},{128,32},{160,64},{192,96},{224,1... | collective-permute-start | bytes 430088 | tf_op jit(solution)/shard_map/sentences_over_lang/ppermute | solution.py:41
  17.2 3.0 %collective-permute-done.refs_1_ = bf16[16,4480]{1,0:T(8,128)(2,1)S(1)} collective-permute-done((bf16[16,4480]{1,0:T(8,128)(2,1)S(1)}, bf16[16,4480]{1,0:T(8,128)(2,1)S(1)}, u32[]{:S(2)}, u32[]{:S(2)}) %collective-permute-start) | collective-permute-done | bytes 143392 | tf_op jit(solution)/shard_map/sentences_over_lang/ppermute | solution.py:41
  20.2 2.1 %collective-permute-start.4 = (bf16[16,4480]{1,0:T(8,128)(2,1)S(1)}, bf16[16,4480]{1,0:T(8,128)(2,1)S(1)}, u32[]{:S(2)}, u32[]{:S(2)}) collective-permute-start(bf16[16,4480]{1,0:T(8,128)(2,1)S(1)} %maximum_maximum_fusion.refs_0_), channel_id=1, source_target_pairs={{0,192},{32,224},{64,0},{96,32},{128,64},{160,96},{192,128},{224,1... | collective-permute-start | bytes 430088 | tf_op jit(solution)/shard_map/sentences_over_lang/ppermute | solution.py:41
  22.3 6.2 %collective-permute-done.1.refs_2_ = bf16[16,4480]{1,0:T(8,128)(2,1)S(1)} collective-permute-done((bf16[16,4480]{1,0:T(8,128)(2,1)S(1)}, bf16[16,4480]{1,0:T(8,128)(2,1)S(1)}, u32[]{:S(2)}, u32[]{:S(2)}) %collective-permute-start.1) | collective-permute-done | bytes 143392 | tf_op jit(solution)/shard_map/sentences_over_lang/ppermute | solution.py:41
  28.5 5.0 %collective-permute-start.5 = (bf16[16,4480]{1,0:T(8,128)(2,1)S(1)}, bf16[16,4480]{1,0:T(8,128)(2,1)S(1)}, u32[]{:S(2)}, u32[]{:S(2)}) collective-permute-start(bf16[16,4480]{1,0:T(8,128)(2,1)S(1)} %maximum_maximum_fusion.refs_0_), channel_id=1, source_target_pairs={{0,32},{32,64},{64,96},{96,128},{128,160},{160,192},{192,224},{224... | collective-permute-start | bytes 430088 | tf_op jit(solution)/shard_map/sentences_over_lang/ppermute | solution.py:41
  33.6 1.3 collective-permute-done.3.refs_4_
  34.9 3.0 %collective-permute-done.5.refs_6_ = bf16[16,4480]{1,0:T(8,128)(2,1)S(1)} collective-permute-done((bf16[16,4480]{1,0:T(8,128)(2,1)S(1)}, bf16[16,4480]{1,0:T(8,128)(2,1)S(1)}, u32[]{:S(2)}, u32[]{:S(2)}) %collective-permute-start.5) | collective-permute-done | bytes 143392 | tf_op jit(solution)/shard_map/sentences_over_lang/ppermute | solution.py:41
  39.4 3.4 %collective-permute-start.8 = (bf16[32,2048]{1,0:T(8,128)(2,1)S(1)}, bf16[32,2048]{1,0:T(8,128)(2,1)S(1)}, u32[]{:S(2)}, u32[]{:S(2)}) collective-permute-start(bf16[32,2048]{1,0:T(8,128)(2,1)S(1)} %get-tuple-element.50.refs_0_), channel_id=1, source_target_pairs={{0,4},{2,6},{4,0},{6,2},{1,5},{3,7},{5,1},{7,3},{8,12},{10,14},{12... | collective-permute-start | bytes 393224 | tf_op jit(solution)/shard_map/gather_rows/ppermute | solution.py:41
  43.4 3.2 %collective-permute-start.9 = (bf16[32,2048]{1,0:T(8,128)(2,1)S(1)}, bf16[32,2048]{1,0:T(8,128)(2,1)S(1)}, u32[]{:S(2)}, u32[]{:S(2)}) collective-permute-start(bf16[32,2048]{1,0:T(8,128)(2,1)S(1)} %get-tuple-element.51.refs_1_), channel_id=1, source_target_pairs={{0,16},{8,24},{16,0},{24,8},{1,17},{9,25},{17,1},{25,9},{2,18},{10... | collective-permute-start | bytes 393224 | tf_op jit(solution)/shard_map/gather_rows/ppermute | solution.py:41
  47.3 2.6 %collective-permute-start.12 = (bf16[32,2048]{1,0:T(8,128)(2,1)S(1)}, bf16[32,2048]{1,0:T(8,128)(2,1)S(1)}, u32[]{:S(2)}, u32[]{:S(2)}) collective-permute-start(bf16[32,2048]{1,0:T(8,128)(2,1)S(1)} %get-tuple-element.50.refs_0_), channel_id=1, source_target_pairs={{0,6},{2,0},{4,2},{6,4},{1,7},{3,1},{5,3},{7,5},{8,14},{10,8},{12,... | collective-permute-start | bytes 393224 | tf_op jit(solution)/shard_map/gather_rows/ppermute | solution.py:41
  49.9 2.6 %collective-permute-start.13 = (bf16[32,2048]{1,0:T(8,128)(2,1)S(1)}, bf16[32,2048]{1,0:T(8,128)(2,1)S(1)}, u32[]{:S(2)}, u32[]{:S(2)}) collective-permute-start(bf16[32,2048]{1,0:T(8,128)(2,1)S(1)} %get-tuple-element.51.refs_1_), channel_id=1, source_target_pairs={{0,24},{8,0},{16,8},{24,16},{1,25},{9,1},{17,9},{25,17},{2,26},{10... | collective-permute-start | bytes 393224 | tf_op jit(solution)/shard_map/gather_rows/ppermute | solution.py:41
  52.8 2.2 %collective-permute-done.13.refs_7_ = bf16[32,2048]{1,0:T(8,128)(2,1)S(1)} collective-permute-done((bf16[32,2048]{1,0:T(8,128)(2,1)S(1)}, bf16[32,2048]{1,0:T(8,128)(2,1)S(1)}, u32[]{:S(2)}, u32[]{:S(2)}) %collective-permute-start.13) | collective-permute-done | bytes 131104 | tf_op jit(solution)/shard_map/gather_rows/ppermute | solution.py:41
  55.0 1.4 gather_rows.1
  56.4 2.0 collective-permute-start.14
  58.4 2.6 %collective-permute-start.16 = (bf16[128,2048]{1,0:T(8,128)(2,1)S(1)}, bf16[128,2048]{1,0:T(8,128)(2,1)S(1)}, u32[]{:S(2)}, u32[]{:S(2)}) collective-permute-start(bf16[128,2048]{1,0:T(8,128)(2,1)S(1)} %get-tuple-element.52.refs_0_), channel_id=1, source_target_pairs={{0,8},{8,16},{16,24},{24,0},{1,9},{9,17},{17,25},{25,1},{2,10},{10... | collective-permute-start | bytes 1572872 | tf_op jit(solution)/shard_map/gather_rows/ppermute | solution.py:41
  61.9 1.6 collective-permute-start.18
  63.5 9.3 %collective-permute-done.14.refs_2_ = bf16[128,2048]{1,0:T(8,128)(2,1)S(1)} collective-permute-done((bf16[128,2048]{1,0:T(8,128)(2,1)S(1)}, bf16[128,2048]{1,0:T(8,128)(2,1)S(1)}, u32[]{:S(2)}, u32[]{:S(2)}) %collective-permute-start.14) | collective-permute-done | bytes 524320 | tf_op jit(solution)/shard_map/gather_rows/ppermute | solution.py:41
  74.0 3.4 %collective-permute-done.15.refs_3_.refs_6_ = bf16[128,2048]{1,0:T(8,128)(2,1)S(1)} collective-permute-done((bf16[128,2048]{1,0:T(8,128)(2,1)S(1)}, bf16[128,2048]{1,0:T(8,128)(2,1)S(1)}, u32[]{:S(2)}, u32[]{:S(2)}) %collective-permute-start.15) | collective-permute-done | bytes 524320 | tf_op jit(solution)/shard_map/gather_rows/ppermute | solution.py:41
  77.4 2.6 %collective-permute-done.16.refs_4_.refs_1_ = bf16[128,2048]{1,0:T(8,128)(2,1)S(1)} collective-permute-done((bf16[128,2048]{1,0:T(8,128)(2,1)S(1)}, bf16[128,2048]{1,0:T(8,128)(2,1)S(1)}, u32[]{:S(2)}, u32[]{:S(2)}) %collective-permute-start.16) | collective-permute-done | bytes 524320 | tf_op jit(solution)/shard_map/gather_rows/ppermute | solution.py:41
  80.0 3.7 %collective-permute-done.17.refs_5_ = bf16[128,2048]{1,0:T(8,128)(2,1)S(1)} collective-permute-done((bf16[128,2048]{1,0:T(8,128)(2,1)S(1)}, bf16[128,2048]{1,0:T(8,128)(2,1)S(1)}, u32[]{:S(2)}, u32[]{:S(2)}) %collective-permute-start.17) | collective-permute-done | bytes 524320 | tf_op jit(solution)/shard_map/gather_rows/ppermute | solution.py:41
  83.7 4.3 %project.1 = bf16[16,32,512]{2,1,0:T(8,128)(2,1)S(1)} custom-call(s32[5]{0:T(128)S(1)} %stack.23.place_ref, bf16[128,2048]{1,0:T(8,128)(2,1)S(1)} %get-tuple-element.52.refs_0_, bf16[128,2048]{1,0:T(8,128)(2,1)S(1)} %get-tuple-element.53.refs_1_.refs_4_, bf16[128,2048]{1,0:T(8,128)(2,1)S(1)} %collective-permute-done.14.refs_2_, ...), custom_call_target="tpu_custom_call" | custom-call | tf_op jit(solution)/shard_map/project/pallas_call | solution.py:307
  88.0 15.3 %all_to_all.10.kv_ref = bf16[16,32,512]{2,1,0:T(8,128)(2,1)} all-to-all(bf16[16,32,512]{2,1,0:T(8,128)(2,1)S(1)} %project.1), channel_id=1, replica_groups=mesh['lang'=8,'y'=4,'x'=4,'core'=2] {'y','x'}, dimensions={0} | all-to-all | bytes 1048576 | tf_op jit(solution)/shard_map/rows_to_slots/all_to_all | solution.py:323
  103.3 9.4 %attend.1 = (bf16[2,128,4096]{2,1,0:T(8,128)(2,1)}, bf16[2,128,4096]{2,1,0:T(8,128)(2,1)}, bf16[16,32,512]{2,1,0:T(8,128)(2,1)}) custom-call(s32[5]{0:T(128)} %copy-done.2, f32[4,8,128]{2,1,0:T(8,128)} %copy-done.4, bf16[2,128,4096]{2,1,0:T(8,128)(2,1)} %bitcast.24, bf16[2,128,4096]{2,1,0:T(8,128)(2,1)} %bitcast.25, bf16[16,32,512]{2,1,0:T(8,128)(2,1)} %all_to_all.10.kv_ref), custom_call_target="tpu_custom_call" | custom-call | tf_op jit(solution)/shard_map/attend/pallas_call | solution.py:329
  112.8 13.9 %all_to_all.11.grads_ref = bf16[16,32,512]{2,1,0:T(8,128)(2,1)S(1)} all-to-all(bf16[16,32,512]{2,1,0:T(8,128)(2,1)} %get-tuple-element.59), channel_id=1, replica_groups=mesh['lang'=8,'y'=4,'x'=4,'core'=2] {'y','x'}, dimensions={0} | all-to-all | bytes 1048576 | tf_op jit(solution)/shard_map/grads_to_heads/all_to_all | solution.py:347
  126.7 3.6 %sum_rows.2 = (bf16[128,2048]{1,0:T(8,128)(2,1)S(1)}, bf16[128,2048]{1,0:T(8,128)(2,1)S(1)}, bf16[128,2048]{1,0:T(8,128)(2,1)S(1)}, bf16[128,2048]{1,0:T(8,128)(2,1)S(1)}) custom-call(s32[5]{0:T(128)S(1)} %copy-done.3, bf16[16,32,512]{2,1,0:T(8,128)(2,1)S(1)} %all_to_all.11.grads_ref, ...), custom_call_target="tpu_custom_call" | custom-call | tf_op jit(solution)/shard_map/sum_rows/pallas_call | solution.py:354
  130.9 1.3 collective-permute-start.21
  132.3 1.4 collective-permute-start.20
  133.7 3.6 %sum_rows.3 = (bf16[128,2048]{1,0:T(8,128)(2,1)S(1)}, bf16[128,2048]{1,0:T(8,128)(2,1)S(1)}, bf16[128,2048]{1,0:T(8,128)(2,1)S(1)}, bf16[128,2048]{1,0:T(8,128)(2,1)S(1)}) custom-call(s32[5]{0:T(128)S(1)} %copy-done.3, bf16[16,32,512]{2,1,0:T(8,128)(2,1)S(1)} %all_to_all.11.grads_ref, ...), custom_call_target="tpu_custom_call" | custom-call | tf_op jit(solution)/shard_map/sum_rows/pallas_call | solution.py:354
  138.1 1.9 collective-permute-start.27
  140.7 4.5 %weight_grads.3 = (bf16[4096,256]{1,0:T(8,128)(2,1)S(1)}, bf16[4096,256]{1,0:T(8,128)(2,1)S(1)}) custom-call(bf16[512,512]{1,0:T(8,128)(2,1)S(1)} %bitcast.22, bf16[512,512]{1,0:T(8,128)(2,1)S(1)} %bitcast.23, bf16[128,2048]{1,0:T(8,128)(2,1)S(1)} %get-tuple-element.52.refs_0_, bf16[128,2048]{1,0:T(8,128)(2,1)S(1)} %collective-permute-done.16.refs_4_.refs_1_, ...), custom_call_target="tpu_custom_call" | custom-call | flops 2147483648 | bytes 16777216 | tf_op jit(solution)/shard_map/weight_grads/pallas_call | solution.py:383
  145.2 8.9 %collective-permute-done.22 = bf16[128,2048]{1,0:T(8,128)(2,1)S(1)} collective-permute-done((bf16[128,2048]{1,0:T(8,128)(2,1)S(1)}, bf16[128,2048]{1,0:T(8,128)(2,1)S(1)}, u32[]{:S(2)}, u32[]{:S(2)}) %collective-permute-start.22) | collective-permute-done | bytes 524320 | tf_op jit(solution)/shard_map/sum_rows/ppermute | solution.py:41
  154.1 1.3 collective-permute-start.26
  156.6 3.7 %collective-permute-done.28 = bf16[128,2048]{1,0:T(8,128)(2,1)S(1)} collective-permute-done((bf16[128,2048]{1,0:T(8,128)(2,1)S(1)}, bf16[128,2048]{1,0:T(8,128)(2,1)S(1)}, u32[]{:S(2)}, u32[]{:S(2)}) %collective-permute-start.28) | collective-permute-done | bytes 524320 | tf_op jit(solution)/shard_map/sum_rows/ppermute | solution.py:41
  161.4 4.3 %collective-permute-done.26 = bf16[128,2048]{1,0:T(8,128)(2,1)S(1)} collective-permute-done((bf16[128,2048]{1,0:T(8,128)(2,1)S(1)}, bf16[128,2048]{1,0:T(8,128)(2,1)S(1)}, u32[]{:S(2)}, u32[]{:S(2)}) %collective-permute-start.26) | collective-permute-done | bytes 524320 | tf_op jit(solution)/shard_map/sum_rows/ppermute | solution.py:41
  166.2 2.5 %collective-permute-start.30 = (bf16[32,2048]{1,0:T(8,128)(2,1)S(1)}, bf16[32,2048]{1,0:T(8,128)(2,1)S(1)}, u32[]{:S(2)}, u32[]{:S(2)}) collective-permute-start(bf16[32,2048]{1,0:T(8,128)(2,1)S(1)} %get-tuple-element.89), channel_id=1, source_target_pairs={{0,4},{2,6},{4,0},{6,2},{1,5},{3,7},{5,1},{7,3},{8,12},{10,14},{12... | collective-permute-start | bytes 393224 | tf_op jit(solution)/shard_map/sum_rows/ppermute | solution.py:41
  169.9 4.2 %collective-permute-done.31 = bf16[32,2048]{1,0:T(8,128)(2,1)S(1)} collective-permute-done((bf16[32,2048]{1,0:T(8,128)(2,1)S(1)}, bf16[32,2048]{1,0:T(8,128)(2,1)S(1)}, u32[]{:S(2)}, u32[]{:S(2)}) %collective-permute-start.31) | collective-permute-done | bytes 131104 | tf_op jit(solution)/shard_map/sum_rows/ppermute | solution.py:41
  174.8 1.9 add_convert_fusion
  176.7 1.5 collective-permute-start.33
  178.2 3.1 %collective-permute-start.34 = (bf16[16,4096]{1,0:T(8,128)(2,1)S(1)}, bf16[16,4096]{1,0:T(8,128)(2,1)S(1)}, u32[]{:S(2)}, u32[]{:S(2)}) collective-permute-start(bf16[16,4096]{1,0:T(8,128)(2,1)S(1)} %get-tuple-element.77), channel_id=1, source_target_pairs={{0,160},{32,192},{64,224},{96,0},{128,32},{160,64},{192,96},{224,1... | collective-permute-start | bytes 393224 | tf_op jit(solution)/shard_map/sentences_back/ppermute | solution.py:41
  181.4 1.9 collective-permute-start.35
  183.3 3.1 %collective-permute-start.36 = (bf16[16,4096]{1,0:T(8,128)(2,1)S(1)}, bf16[16,4096]{1,0:T(8,128)(2,1)S(1)}, u32[]{:S(2)}, u32[]{:S(2)}) collective-permute-start(bf16[16,4096]{1,0:T(8,128)(2,1)S(1)} %get-tuple-element.79), channel_id=1, source_target_pairs={{0,192},{32,224},{64,0},{96,32},{128,64},{160,96},{192,128},{224,1... | collective-permute-start | bytes 393224 | tf_op jit(solution)/shard_map/sentences_back/ppermute | solution.py:41
  186.6 3.3 %collective-permute-done.33.refs_1_ = bf16[16,4096]{1,0:T(8,128)(2,1)S(1)} collective-permute-done((bf16[16,4096]{1,0:T(8,128)(2,1)S(1)}, bf16[16,4096]{1,0:T(8,128)(2,1)S(1)}, u32[]{:S(2)}, u32[]{:S(2)}) %collective-permute-start.33) | collective-permute-done | bytes 131104 | tf_op jit(solution)/shard_map/sentences_back/ppermute | solution.py:41
  189.8 7.4 %collective-permute-done.34.refs_2_ = bf16[16,4096]{1,0:T(8,128)(2,1)S(1)} collective-permute-done((bf16[16,4096]{1,0:T(8,128)(2,1)S(1)}, bf16[16,4096]{1,0:T(8,128)(2,1)S(1)}, u32[]{:S(2)}, u32[]{:S(2)}) %collective-permute-start.34) | collective-permute-done | bytes 131104 | tf_op jit(solution)/shard_map/sentences_back/ppermute | solution.py:41
  197.2 2.9 %collective-permute-done.36.refs_4_ = bf16[16,4096]{1,0:T(8,128)(2,1)S(1)} collective-permute-done((bf16[16,4096]{1,0:T(8,128)(2,1)S(1)}, bf16[16,4096]{1,0:T(8,128)(2,1)S(1)}, u32[]{:S(2)}, u32[]{:S(2)}) %collective-permute-start.36) | collective-permute-done | bytes 131104 | tf_op jit(solution)/shard_map/sentences_back/ppermute | solution.py:41
  200.1 1.2 collective-permute-done.37.refs_5_
  202.4 1.3 sentences_back.3
  (73 shorter events, 14.9 us)
Async XLA Ops:
  0.6 4.5 %copy-start.5 = (bf16[1,4096,128]{2,1,0:T(8,128)(2,1)S(1)}, bf16[1,4096,128]{2,1,0:T(8,128)(2,1)}, u32[]{:S(2)}) copy-start(bf16[1,4096,128]{2,1,0:T(8,128)(2,1)} %param.14) | copy-start | bytes 3145732
  5.4 34.0 %collective-permute-start.7 = (bf16[4096,256]{1,0:T(8,128)(2,1)S(1)}, bf16[4096,256]{1,0:T(8,128)(2,1)}, u32[]{:S(2)}, u32[]{:S(2)}) collective-permute-start(bf16[4096,256]{1,0:T(8,128)(2,1)S(1)} %constant_dynamic-update-slice_fusion.refs_8_.own_ref), channel_id=1, source_target_pairs={{0,1},{1,0},{2,3},{3,2},{4,5},{5,4},{6,7},{7,6},{8,9},{9,8},{10,11... | collective-permute-start | bytes 6291464 | tf_op jit(solution)/shard_map/weights_of_chip/ppermute | solution.py:41
  5.5 14.7 %collective-permute-start = (bf16[16,4480]{1,0:T(8,128)(2,1)S(1)}, bf16[16,4480]{1,0:T(8,128)(2,1)S(1)}, u32[]{:S(2)}, u32[]{:S(2)}) collective-permute-start(bf16[16,4480]{1,0:T(8,128)(2,1)S(1)} %maximum_maximum_fusion.refs_0_), channel_id=1, source_target_pairs={{0,128},{32,160},{64,192},{96,224},{128,0},{160,32},{192,64},{224,... | collective-permute-start | bytes 430088 | tf_op jit(solution)/shard_map/sentences_over_lang/ppermute | solution.py:41
  11.9 16.6 %collective-permute-start.1 = (bf16[16,4480]{1,0:T(8,128)(2,1)S(1)}, bf16[16,4480]{1,0:T(8,128)(2,1)S(1)}, u32[]{:S(2)}, u32[]{:S(2)}) collective-permute-start(bf16[16,4480]{1,0:T(8,128)(2,1)S(1)} %maximum_maximum_fusion.refs_0_), channel_id=1, source_target_pairs={{0,96},{32,128},{64,160},{96,192},{128,224},{160,0},{192,32},{224,... | collective-permute-start | bytes 430088 | tf_op jit(solution)/shard_map/sentences_over_lang/ppermute | solution.py:41
  11.9 21.6 %collective-permute-start.2 = (bf16[16,4480]{1,0:T(8,128)(2,1)S(1)}, bf16[16,4480]{1,0:T(8,128)(2,1)S(1)}, u32[]{:S(2)}, u32[]{:S(2)}) collective-permute-start(bf16[16,4480]{1,0:T(8,128)(2,1)S(1)} %maximum_maximum_fusion.refs_0_), channel_id=1, source_target_pairs={{0,160},{32,192},{64,224},{96,0},{128,32},{160,64},{192,96},{224,1... | collective-permute-start | bytes 430088 | tf_op jit(solution)/shard_map/sentences_over_lang/ppermute | solution.py:41
  16.9 17.9 %collective-permute-start.3 = (bf16[16,4480]{1,0:T(8,128)(2,1)S(1)}, bf16[16,4480]{1,0:T(8,128)(2,1)S(1)}, u32[]{:S(2)}, u32[]{:S(2)}) collective-permute-start(bf16[16,4480]{1,0:T(8,128)(2,1)S(1)} %maximum_maximum_fusion.refs_0_), channel_id=1, source_target_pairs={{0,64},{32,96},{64,128},{96,160},{128,192},{160,224},{192,0},{224,... | collective-permute-start | bytes 430088 | tf_op jit(solution)/shard_map/sentences_over_lang/ppermute | solution.py:41
  20.2 14.6 %collective-permute-start.4 = (bf16[16,4480]{1,0:T(8,128)(2,1)S(1)}, bf16[16,4480]{1,0:T(8,128)(2,1)S(1)}, u32[]{:S(2)}, u32[]{:S(2)}) collective-permute-start(bf16[16,4480]{1,0:T(8,128)(2,1)S(1)} %maximum_maximum_fusion.refs_0_), channel_id=1, source_target_pairs={{0,192},{32,224},{64,0},{96,32},{128,64},{160,96},{192,128},{224,1... | collective-permute-start | bytes 430088 | tf_op jit(solution)/shard_map/sentences_over_lang/ppermute | solution.py:41
  28.5 9.4 %collective-permute-start.5 = (bf16[16,4480]{1,0:T(8,128)(2,1)S(1)}, bf16[16,4480]{1,0:T(8,128)(2,1)S(1)}, u32[]{:S(2)}, u32[]{:S(2)}) collective-permute-start(bf16[16,4480]{1,0:T(8,128)(2,1)S(1)} %maximum_maximum_fusion.refs_0_), channel_id=1, source_target_pairs={{0,32},{32,64},{64,96},{96,128},{128,160},{160,192},{192,224},{224... | collective-permute-start | bytes 430088 | tf_op jit(solution)/shard_map/sentences_over_lang/ppermute | solution.py:41
  33.5 5.1 %collective-permute-start.6 = (bf16[16,4480]{1,0:T(8,128)(2,1)S(1)}, bf16[16,4480]{1,0:T(8,128)(2,1)S(1)}, u32[]{:S(2)}, u32[]{:S(2)}) collective-permute-start(bf16[16,4480]{1,0:T(8,128)(2,1)S(1)} %maximum_maximum_fusion.refs_0_), channel_id=1, source_target_pairs={{0,224},{32,0},{64,32},{96,64},{128,96},{160,128},{192,160},{224,1... | collective-permute-start | bytes 430088 | tf_op jit(solution)/shard_map/sentences_over_lang/ppermute | solution.py:41
  33.6 54.4 %copy-start.2 = (s32[5]{0:T(128)}, s32[5]{0:T(128)S(1)}, u32[]{:S(2)}) copy-start(s32[5]{0:T(128)S(1)} %stack.23.place_ref) | copy-start | bytes 64
  39.4 44.2 %copy-start.4 = (f32[4,8,128]{2,1,0:T(8,128)}, f32[4,8,128]{2,1,0:T(8,128)S(1)}, u32[]{:S(2)}) copy-start(f32[4,8,128]{2,1,0:T(8,128)S(1)} %get-tuple-element.45.lens_ref) | copy-start | bytes 49156
  39.4 10.5 %collective-permute-start.8 = (bf16[32,2048]{1,0:T(8,128)(2,1)S(1)}, bf16[32,2048]{1,0:T(8,128)(2,1)S(1)}, u32[]{:S(2)}, u32[]{:S(2)}) collective-permute-start(bf16[32,2048]{1,0:T(8,128)(2,1)S(1)} %get-tuple-element.50.refs_0_), channel_id=1, source_target_pairs={{0,4},{2,6},{4,0},{6,2},{1,5},{3,7},{5,1},{7,3},{8,12},{10,14},{12... | collective-permute-start | bytes 393224 | tf_op jit(solution)/shard_map/gather_rows/ppermute | solution.py:41
  42.8 9.7 %collective-permute-start.10 = (bf16[32,2048]{1,0:T(8,128)(2,1)S(1)}, bf16[32,2048]{1,0:T(8,128)(2,1)S(1)}, u32[]{:S(2)}, u32[]{:S(2)}) collective-permute-start(bf16[32,2048]{1,0:T(8,128)(2,1)S(1)} %get-tuple-element.50.refs_0_), channel_id=1, source_target_pairs={{0,2},{2,4},{4,6},{6,0},{1,3},{3,5},{5,7},{7,1},{8,10},{10,12},{12... | collective-permute-start | bytes 393224 | tf_op jit(solution)/shard_map/gather_rows/ppermute | solution.py:41
  43.4 9.1 %collective-permute-start.9 = (bf16[32,2048]{1,0:T(8,128)(2,1)S(1)}, bf16[32,2048]{1,0:T(8,128)(2,1)S(1)}, u32[]{:S(2)}, u32[]{:S(2)}) collective-permute-start(bf16[32,2048]{1,0:T(8,128)(2,1)S(1)} %get-tuple-element.51.refs_1_), channel_id=1, source_target_pairs={{0,16},{8,24},{16,0},{24,8},{1,17},{9,25},{17,1},{25,9},{2,18},{10... | collective-permute-start | bytes 393224 | tf_op jit(solution)/shard_map/gather_rows/ppermute | solution.py:41
  46.6 6.2 %collective-permute-start.11 = (bf16[32,2048]{1,0:T(8,128)(2,1)S(1)}, bf16[32,2048]{1,0:T(8,128)(2,1)S(1)}, u32[]{:S(2)}, u32[]{:S(2)}) collective-permute-start(bf16[32,2048]{1,0:T(8,128)(2,1)S(1)} %get-tuple-element.51.refs_1_), channel_id=1, source_target_pairs={{0,8},{8,16},{16,24},{24,0},{1,9},{9,17},{17,25},{25,1},{2,10},{10... | collective-permute-start | bytes 393224 | tf_op jit(solution)/shard_map/gather_rows/ppermute | solution.py:41
  47.3 5.5 %collective-permute-start.12 = (bf16[32,2048]{1,0:T(8,128)(2,1)S(1)}, bf16[32,2048]{1,0:T(8,128)(2,1)S(1)}, u32[]{:S(2)}, u32[]{:S(2)}) collective-permute-start(bf16[32,2048]{1,0:T(8,128)(2,1)S(1)} %get-tuple-element.50.refs_0_), channel_id=1, source_target_pairs={{0,6},{2,0},{4,2},{6,4},{1,7},{3,1},{5,3},{7,5},{8,14},{10,8},{12,... | collective-permute-start | bytes 393224 | tf_op jit(solution)/shard_map/gather_rows/ppermute | solution.py:41
  49.9 5.1 %collective-permute-start.13 = (bf16[32,2048]{1,0:T(8,128)(2,1)S(1)}, bf16[32,2048]{1,0:T(8,128)(2,1)S(1)}, u32[]{:S(2)}, u32[]{:S(2)}) collective-permute-start(bf16[32,2048]{1,0:T(8,128)(2,1)S(1)} %get-tuple-element.51.refs_1_), channel_id=1, source_target_pairs={{0,24},{8,0},{16,8},{24,16},{1,25},{9,1},{17,9},{25,17},{2,26},{10... | collective-permute-start | bytes 393224 | tf_op jit(solution)/shard_map/gather_rows/ppermute | solution.py:41
  56.4 16.5 %collective-permute-start.14 = (bf16[128,2048]{1,0:T(8,128)(2,1)S(1)}, bf16[128,2048]{1,0:T(8,128)(2,1)S(1)}, u32[]{:S(2)}, u32[]{:S(2)}) collective-permute-start(bf16[128,2048]{1,0:T(8,128)(2,1)S(1)} %get-tuple-element.52.refs_0_), channel_id=1, source_target_pairs={{0,16},{8,24},{16,0},{24,8},{1,17},{9,25},{17,1},{25,9},{2,18},{10... | collective-permute-start | bytes 1572872 | tf_op jit(solution)/shard_map/gather_rows/ppermute | solution.py:41
  58.4 21.6 %collective-permute-start.16 = (bf16[128,2048]{1,0:T(8,128)(2,1)S(1)}, bf16[128,2048]{1,0:T(8,128)(2,1)S(1)}, u32[]{:S(2)}, u32[]{:S(2)}) collective-permute-start(bf16[128,2048]{1,0:T(8,128)(2,1)S(1)} %get-tuple-element.52.refs_0_), channel_id=1, source_target_pairs={{0,8},{8,16},{16,24},{24,0},{1,9},{9,17},{17,25},{25,1},{2,10},{10... | collective-permute-start | bytes 1572872 | tf_op jit(solution)/shard_map/gather_rows/ppermute | solution.py:41
  61.0 16.4 %collective-permute-start.15 = (bf16[128,2048]{1,0:T(8,128)(2,1)S(1)}, bf16[128,2048]{1,0:T(8,128)(2,1)S(1)}, u32[]{:S(2)}, u32[]{:S(2)}) collective-permute-start(bf16[128,2048]{1,0:T(8,128)(2,1)S(1)} %get-tuple-element.53.refs_1_.refs_4_), channel_id=1, source_target_pairs={{0,4},{2,6},{4,0},{6,2},{1,5},{3,7},{5,1},{7,3},{8,12},{10,14},{12... | collective-permute-start | bytes 1572872 | tf_op jit(solution)/shard_map/gather_rows/ppermute | solution.py:41
  61.9 21.7 %collective-permute-start.17 = (bf16[128,2048]{1,0:T(8,128)(2,1)S(1)}, bf16[128,2048]{1,0:T(8,128)(2,1)S(1)}, u32[]{:S(2)}, u32[]{:S(2)}) collective-permute-start(bf16[128,2048]{1,0:T(8,128)(2,1)S(1)} %get-tuple-element.53.refs_1_.refs_4_), channel_id=1, source_target_pairs={{0,2},{2,4},{4,6},{6,0},{1,3},{3,5},{5,7},{7,1},{8,10},{10,12},{12... | collective-permute-start | bytes 1572872 | tf_op jit(solution)/shard_map/gather_rows/ppermute | solution.py:41
  61.9 21.7 %collective-permute-start.18 = (bf16[128,2048]{1,0:T(8,128)(2,1)S(1)}, bf16[128,2048]{1,0:T(8,128)(2,1)S(1)}, u32[]{:S(2)}, u32[]{:S(2)}) collective-permute-start(bf16[128,2048]{1,0:T(8,128)(2,1)S(1)} %get-tuple-element.52.refs_0_), channel_id=1, source_target_pairs={{0,24},{8,0},{16,8},{24,16},{1,25},{9,1},{17,9},{25,17},{2,26},{10... | collective-permute-start | bytes 1572872 | tf_op jit(solution)/shard_map/gather_rows/ppermute | solution.py:41
  72.9 10.8 %collective-permute-start.19 = (bf16[128,2048]{1,0:T(8,128)(2,1)S(1)}, bf16[128,2048]{1,0:T(8,128)(2,1)S(1)}, u32[]{:S(2)}, u32[]{:S(2)}) collective-permute-start(bf16[128,2048]{1,0:T(8,128)(2,1)S(1)} %get-tuple-element.53.refs_1_.refs_4_), channel_id=1, source_target_pairs={{0,6},{2,0},{4,2},{6,4},{1,7},{3,1},{5,3},{7,5},{8,14},{10,8},{12,... | collective-permute-start | bytes 1572872 | tf_op jit(solution)/shard_map/gather_rows/ppermute | solution.py:41
  83.6 4.4 %copy-start = (bf16[128,2048]{1,0:T(8,128)(2,1)}, bf16[128,2048]{1,0:T(8,128)(2,1)S(1)}, u32[]{:S(2)}) copy-start(bf16[128,2048]{1,0:T(8,128)(2,1)S(1)} %collective-permute-done.19.refs_7_) | copy-start | bytes 1572868
  103.3 23.4 %copy-start.3 = (s32[5]{0:T(128)S(1)}, s32[5]{0:T(128)}, u32[]{:S(2)}) copy-start(s32[5]{0:T(128)} %copy-done.2) | copy-start | bytes 64
  130.3 23.8 %collective-permute-start.22 = (bf16[128,2048]{1,0:T(8,128)(2,1)S(1)}, bf16[128,2048]{1,0:T(8,128)(2,1)S(1)}, u32[]{:S(2)}, u32[]{:S(2)}) collective-permute-start(bf16[128,2048]{1,0:T(8,128)(2,1)S(1)} %get-tuple-element.63), channel_id=1, source_target_pairs={{0,2},{2,4},{4,6},{6,0},{1,3},{3,5},{5,7},{7,1},{8,10},{10,12},{12... | collective-permute-start | bytes 1572872 | tf_op jit(solution)/shard_map/sum_rows/ppermute | solution.py:41
  130.9 24.5 %collective-permute-start.21 = (bf16[128,2048]{1,0:T(8,128)(2,1)S(1)}, bf16[128,2048]{1,0:T(8,128)(2,1)S(1)}, u32[]{:S(2)}, u32[]{:S(2)}) collective-permute-start(bf16[128,2048]{1,0:T(8,128)(2,1)S(1)} %get-tuple-element.62), channel_id=1, source_target_pairs={{0,4},{2,6},{4,0},{6,2},{1,5},{3,7},{5,1},{7,3},{8,12},{10,14},{12... | collective-permute-start | bytes 1572872 | tf_op jit(solution)/shard_map/sum_rows/ppermute | solution.py:41
  132.3 8.4 %copy-start.1 = (bf16[128,2048]{1,0:T(8,128)(2,1)S(1)}, bf16[128,2048]{1,0:T(8,128)(2,1)}, u32[]{:S(2)}) copy-start(bf16[128,2048]{1,0:T(8,128)(2,1)} %copy-done) | copy-start | bytes 1572868
  132.3 23.1 %collective-permute-start.20 = (bf16[128,2048]{1,0:T(8,128)(2,1)S(1)}, bf16[128,2048]{1,0:T(8,128)(2,1)S(1)}, u32[]{:S(2)}, u32[]{:S(2)}) collective-permute-start(bf16[128,2048]{1,0:T(8,128)(2,1)S(1)} %get-tuple-element.61), channel_id=1, source_target_pairs={{0,6},{2,0},{4,2},{6,4},{1,7},{3,1},{5,3},{7,5},{8,14},{10,8},{12,... | collective-permute-start | bytes 1572872 | tf_op jit(solution)/shard_map/sum_rows/ppermute | solution.py:41
  137.3 22.9 %collective-permute-start.28 = (bf16[128,2048]{1,0:T(8,128)(2,1)S(1)}, bf16[128,2048]{1,0:T(8,128)(2,1)S(1)}, u32[]{:S(2)}, u32[]{:S(2)}) collective-permute-start(bf16[128,2048]{1,0:T(8,128)(2,1)S(1)} %get-tuple-element.67), channel_id=1, source_target_pairs={{0,8},{8,16},{16,24},{24,0},{1,9},{9,17},{17,25},{25,1},{2,10},{10... | collective-permute-start | bytes 1572872 | tf_op jit(solution)/shard_map/sum_rows/ppermute | solution.py:41
  138.1 23.3 %collective-permute-start.27 = (bf16[128,2048]{1,0:T(8,128)(2,1)S(1)}, bf16[128,2048]{1,0:T(8,128)(2,1)S(1)}, u32[]{:S(2)}, u32[]{:S(2)}) collective-permute-start(bf16[128,2048]{1,0:T(8,128)(2,1)S(1)} %get-tuple-element.66), channel_id=1, source_target_pairs={{0,16},{8,24},{16,0},{24,8},{1,17},{9,25},{17,1},{25,9},{2,18},{10... | collective-permute-start | bytes 1572872 | tf_op jit(solution)/shard_map/sum_rows/ppermute | solution.py:41
  154.1 11.6 %collective-permute-start.26 = (bf16[128,2048]{1,0:T(8,128)(2,1)S(1)}, bf16[128,2048]{1,0:T(8,128)(2,1)S(1)}, u32[]{:S(2)}, u32[]{:S(2)}) collective-permute-start(bf16[128,2048]{1,0:T(8,128)(2,1)S(1)} %get-tuple-element.65), channel_id=1, source_target_pairs={{0,24},{8,0},{16,8},{24,16},{1,25},{9,1},{17,9},{25,17},{2,26},{10... | collective-permute-start | bytes 1572872 | tf_op jit(solution)/shard_map/sum_rows/ppermute | solution.py:41
  155.4 19.3 %collective-permute-start.32 = (bf16[4096,256]{1,0:T(8,128)(2,1)S(1)}, bf16[4096,256]{1,0:T(8,128)(2,1)S(1)}, u32[]{:S(2)}, u32[]{:S(2)}) collective-permute-start(bf16[4096,256]{1,0:T(8,128)(2,1)S(1)} %get-tuple-element.72), channel_id=1, source_target_pairs={{0,1},{1,0},{2,3},{3,2},{4,5},{5,4},{6,7},{7,6},{8,9},{9,8},{10,11... | collective-permute-start | bytes 6291464 | tf_op jit(solution)/shard_map/weight_grads/ppermute | solution.py:41
  155.8 10.4 %collective-permute-start.25 = (bf16[32,2048]{1,0:T(8,128)(2,1)S(1)}, bf16[32,2048]{1,0:T(8,128)(2,1)S(1)}, u32[]{:S(2)}, u32[]{:S(2)}) collective-permute-start(bf16[32,2048]{1,0:T(8,128)(2,1)S(1)} %get-tuple-element.91), channel_id=1, source_target_pairs={{0,8},{8,16},{16,24},{24,0},{1,9},{9,17},{17,25},{25,1},{2,10},{10... | collective-permute-start | bytes 393224 | tf_op jit(solution)/shard_map/sum_rows/ppermute | solution.py:41
  160.3 8.5 %collective-permute-start.24 = (bf16[32,2048]{1,0:T(8,128)(2,1)S(1)}, bf16[32,2048]{1,0:T(8,128)(2,1)S(1)}, u32[]{:S(2)}, u32[]{:S(2)}) collective-permute-start(bf16[32,2048]{1,0:T(8,128)(2,1)S(1)} %get-tuple-element.92), channel_id=1, source_target_pairs={{0,16},{8,24},{16,0},{24,8},{1,17},{9,25},{17,1},{25,9},{2,18},{10... | collective-permute-start | bytes 393224 | tf_op jit(solution)/shard_map/sum_rows/ppermute | solution.py:41
  161.4 8.4 %collective-permute-start.23 = (bf16[32,2048]{1,0:T(8,128)(2,1)S(1)}, bf16[32,2048]{1,0:T(8,128)(2,1)S(1)}, u32[]{:S(2)}, u32[]{:S(2)}) collective-permute-start(bf16[32,2048]{1,0:T(8,128)(2,1)S(1)} %get-tuple-element.90), channel_id=1, source_target_pairs={{0,24},{8,0},{16,8},{24,16},{1,25},{9,1},{17,9},{25,17},{2,26},{10... | collective-permute-start | bytes 393224 | tf_op jit(solution)/shard_map/sum_rows/ppermute | solution.py:41
  166.1 8.0 %collective-permute-start.31 = (bf16[32,2048]{1,0:T(8,128)(2,1)S(1)}, bf16[32,2048]{1,0:T(8,128)(2,1)S(1)}, u32[]{:S(2)}, u32[]{:S(2)}) collective-permute-start(bf16[32,2048]{1,0:T(8,128)(2,1)S(1)} %get-tuple-element.88), channel_id=1, source_target_pairs={{0,2},{2,4},{4,6},{6,0},{1,3},{3,5},{5,7},{7,1},{8,10},{10,12},{12... | collective-permute-start | bytes 393224 | tf_op jit(solution)/shard_map/sum_rows/ppermute | solution.py:41
  166.2 7.9 %collective-permute-start.30 = (bf16[32,2048]{1,0:T(8,128)(2,1)S(1)}, bf16[32,2048]{1,0:T(8,128)(2,1)S(1)}, u32[]{:S(2)}, u32[]{:S(2)}) collective-permute-start(bf16[32,2048]{1,0:T(8,128)(2,1)S(1)} %get-tuple-element.89), channel_id=1, source_target_pairs={{0,4},{2,6},{4,0},{6,2},{1,5},{3,7},{5,1},{7,3},{8,12},{10,14},{12... | collective-permute-start | bytes 393224 | tf_op jit(solution)/shard_map/sum_rows/ppermute | solution.py:41
  168.8 5.9 %collective-permute-start.29 = (bf16[32,2048]{1,0:T(8,128)(2,1)S(1)}, bf16[32,2048]{1,0:T(8,128)(2,1)S(1)}, u32[]{:S(2)}, u32[]{:S(2)}) collective-permute-start(bf16[32,2048]{1,0:T(8,128)(2,1)S(1)} %get-tuple-element.87), channel_id=1, source_target_pairs={{0,6},{2,0},{4,2},{6,4},{1,7},{3,1},{5,3},{7,5},{8,14},{10,8},{12,... | collective-permute-start | bytes 393224 | tf_op jit(solution)/shard_map/sum_rows/ppermute | solution.py:41
  176.7 13.1 %collective-permute-start.33 = (bf16[16,4096]{1,0:T(8,128)(2,1)S(1)}, bf16[16,4096]{1,0:T(8,128)(2,1)S(1)}, u32[]{:S(2)}, u32[]{:S(2)}) collective-permute-start(bf16[16,4096]{1,0:T(8,128)(2,1)S(1)} %get-tuple-element.76), channel_id=1, source_target_pairs={{0,128},{32,160},{64,192},{96,224},{128,0},{160,32},{192,64},{224,... | collective-permute-start | bytes 393224 | tf_op jit(solution)/shard_map/sentences_back/ppermute | solution.py:41
  178.2 19.0 %collective-permute-start.34 = (bf16[16,4096]{1,0:T(8,128)(2,1)S(1)}, bf16[16,4096]{1,0:T(8,128)(2,1)S(1)}, u32[]{:S(2)}, u32[]{:S(2)}) collective-permute-start(bf16[16,4096]{1,0:T(8,128)(2,1)S(1)} %get-tuple-element.77), channel_id=1, source_target_pairs={{0,160},{32,192},{64,224},{96,0},{128,32},{160,64},{192,96},{224,1... | collective-permute-start | bytes 393224 | tf_op jit(solution)/shard_map/sentences_back/ppermute | solution.py:41
  181.4 15.9 %collective-permute-start.35 = (bf16[16,4096]{1,0:T(8,128)(2,1)S(1)}, bf16[16,4096]{1,0:T(8,128)(2,1)S(1)}, u32[]{:S(2)}, u32[]{:S(2)}) collective-permute-start(bf16[16,4096]{1,0:T(8,128)(2,1)S(1)} %get-tuple-element.78), channel_id=1, source_target_pairs={{0,96},{32,128},{64,160},{96,192},{128,224},{160,0},{192,32},{224,... | collective-permute-start | bytes 393224 | tf_op jit(solution)/shard_map/sentences_back/ppermute | solution.py:41
  183.3 16.8 %collective-permute-start.36 = (bf16[16,4096]{1,0:T(8,128)(2,1)S(1)}, bf16[16,4096]{1,0:T(8,128)(2,1)S(1)}, u32[]{:S(2)}, u32[]{:S(2)}) collective-permute-start(bf16[16,4096]{1,0:T(8,128)(2,1)S(1)} %get-tuple-element.79), channel_id=1, source_target_pairs={{0,192},{32,224},{64,0},{96,32},{128,64},{160,96},{192,128},{224,1... | collective-permute-start | bytes 393224 | tf_op jit(solution)/shard_map/sentences_back/ppermute | solution.py:41
  186.4 14.9 %collective-permute-start.37 = (bf16[16,4096]{1,0:T(8,128)(2,1)S(1)}, bf16[16,4096]{1,0:T(8,128)(2,1)S(1)}, u32[]{:S(2)}, u32[]{:S(2)}) collective-permute-start(bf16[16,4096]{1,0:T(8,128)(2,1)S(1)} %get-tuple-element.80), channel_id=1, source_target_pairs={{0,64},{32,96},{64,128},{96,160},{128,192},{160,224},{192,0},{224,... | collective-permute-start | bytes 393224 | tf_op jit(solution)/shard_map/sentences_back/ppermute | solution.py:41
  189.8 12.0 %collective-permute-start.38 = (bf16[16,4096]{1,0:T(8,128)(2,1)S(1)}, bf16[16,4096]{1,0:T(8,128)(2,1)S(1)}, u32[]{:S(2)}, u32[]{:S(2)}) collective-permute-start(bf16[16,4096]{1,0:T(8,128)(2,1)S(1)} %get-tuple-element.81), channel_id=1, source_target_pairs={{0,224},{32,0},{64,32},{96,64},{128,96},{160,128},{192,160},{224,1... | collective-permute-start | bytes 393224 | tf_op jit(solution)/shard_map/sentences_back/ppermute | solution.py:41
  197.2 5.2 %collective-permute-start.39 = (bf16[16,4096]{1,0:T(8,128)(2,1)S(1)}, bf16[16,4096]{1,0:T(8,128)(2,1)S(1)}, u32[]{:S(2)}, u32[]{:S(2)}) collective-permute-start(bf16[16,4096]{1,0:T(8,128)(2,1)S(1)} %get-tuple-element.82), channel_id=1, source_target_pairs={{0,32},{32,64},{64,96},{96,128},{128,160},{160,192},{192,224},{224... | collective-permute-start | bytes 393224 | tf_op jit(solution)/shard_map/sentences_back/ppermute | solution.py:41
where the time goes:
time: 206 us; the launch traced here: 204 us
  waiting for transfers between devices  74.5 us (36%)
  starting transfers between devices  61.9 us (30%)
  Pallas kernels  29.7 us (14%)
  blocking collectives  29.2 us (14%)
  other arithmetic  3.64 us (2%)
  between operations  2.98 us (1%)
    ppermute x40, waiting for transfers between devices, shift(): return lax.ppermute(value, axis, [(i, (i + step) % n) for i in range(n)])  74.5 us
    ppermute x40, starting transfers between devices, shift(): return lax.ppermute(value, axis, [(i, (i + step) % n) for i in range(n)])  61.9 us
    all_to_all x1, blocking collectives, local(): slot_rows = lax.all_to_all(projected, PLANE, 0, 0, tiled=True)  15.3 us
    all_to_all x1, blocking collectives, local(): head_grads = lax.all_to_all(slot_grads, PLANE, 0, 0, tiled=True)  13.9 us
    pallas_call x1, Pallas kernels, local(): pl.pallas_call(attend_kernel, grid=(groups,), out_shape=(jax.ShapeDtypeSt...  9.45 us
    pallas_call x2, Pallas kernels, local(): pl.pallas_call(functools.partial(partial_kernel, first == 'y'), grid=(SID...  7.19 us
    pallas_call x1, Pallas kernels, local(): pl.pallas_call(weight_kernel, grid=(2 * SIDE,), out_shape=(jax.ShapeDtype...  4.5 us
    pallas_call x1, Pallas kernels, local(): pl.pallas_call(project_kernel, out_shape=jax.ShapeDtypeStruct((CHIPS, ROW...  4.34 us
  transfers between devices with their start and end apart: 40, of which 23 were waited for; matrix products, arithmetic and copies ran while one was open for 0% of the time, Pallas kernels for 5%

commit v1 on v0

v1 whole, which is shorter than its diff:
```python
import functools

import jax
import jax.numpy as jnp
from jax import lax
from jax.experimental import pallas as pl
from jax.experimental.pallas import tpu as pltpu
from jax.sharding import Mesh, PartitionSpec as P

HEAD = 128
SRC = 16
TGT = 128
WIDTH = 4096
PLANES = 8
SIDE = 4
CHIPS = SIDE * SIDE
ROWS = 32
GROUP = 8
MASKED = -1e30
BF = jnp.bfloat16
F32 = jnp.float32
PLANE = ("y", "x")
FAR_FIRST = (0, 4, 3, 5, 2, 6, 1, 7)
LINE = (0, 2, 1, 3)
VMEM = pl.BlockSpec(memory_space=pltpu.VMEM)
SMEM = pl.BlockSpec(memory_space=pltpu.SMEM)
ANY = pl.BlockSpec(memory_space=pl.ANY)


def params(mib):
    return pltpu.CompilerParams(vmem_limit_bytes=mib << 20)


def cost(products, mib):
    return pl.CostEstimate(flops=2 * products, bytes_accessed=mib << 20, transcendentals=0)


def exchange(value):
    return lax.ppermute(value, "core", [(0, 1), (1, 0)])


def shift_lang(value, step):
    pairs = [
        (2 * z + c, 2 * ((z + (step if c == 0 else -step)) % PLANES) + c)
        for z in range(PLANES)
        for c in range(2)
    ]
    return lax.ppermute(value, ("lang", "core"), pairs)


def shift_plane(value, phase, step):
    pairs = []
    for y in range(SIDE):
        for x in range(SIDE):
            for c in range(2):
                along_x = c == phase
                to_y = y if along_x else (y + step) % SIDE
                to_x = (x + step) % SIDE if along_x else x
                pairs.append(((y * SIDE + x) * 2 + c, (to_y * SIDE + to_x) * 2 + c))
    return lax.ppermute(value, ("y", "x", "core"), pairs)


def dot(a, b, ca, cb):
    return lax.dot_general(a, b, (((ca,), (cb,)), ((), ())), preferred_element_type=F32)


def chip_at(place_ref, first, second):
    y, x, core = place_ref[1], place_ref[2], place_ref[4]
    dy = jnp.where(core == 0, second, first)
    dx = jnp.where(core == 0, first, second)
    return lax.rem(y - dy + SIDE, SIDE) * SIDE + lax.rem(x - dx + SIDE, SIDE)


def route_kernel(place_ref, *refs):
    sentences, (routed_ref, rank_ref, lens_ref) = refs[:PLANES], refs[PLANES:]
    sentences = [sentences[FAR_FIRST.index(d)] for d in range(PLANES)]
    plane, core = place_ref[0], place_ref[4]
    plane_f = plane.astype(F32)
    match, rank = [], []
    for ref in sentences:
        lang = ref[:, WIDTH : WIDTH + 1].astype(F32)
        match.append(jnp.where(lang == plane_f, 1.0, 0.0))
    origin = [
        lax.rem(plane + jnp.where(core == 0, PLANES - d, d), PLANES) for d in range(PLANES)
    ]
    for d in range(PLANES):
        before = jnp.zeros((SRC, 1), F32)
        for e in range(PLANES):
            if e != d:
                before += jnp.where(origin[e] < origin[d], match[e], 0.0)
        rank.append(jnp.where(match[d] > 0.5, before, -1.0))
        rank_ref[d] = jnp.broadcast_to(rank[d][:8], (8, HEAD))
    for r in range(2):
        src = jnp.zeros((8, 1), F32)
        tgt = jnp.zeros((8, 1), F32)
        total = jnp.zeros((SRC, WIDTH), BF)
        for d, ref in enumerate(sentences):
            here = rank[d] == float(r)
            src = jnp.where(here[:8], ref[:8, WIDTH + 1 : WIDTH + 2].astype(F32), src)
            tgt = jnp.where(here[:8], ref[:8, WIDTH + 2 : WIDTH + 3].astype(F32), tgt)
            wide = jnp.where(here, 1.0, 0.0).astype(BF)
            total = jnp.where(wide > 0.5, ref[:, :WIDTH], total)
        lens_ref[r] = jnp.broadcast_to(src, (8, HEAD))
        lens_ref[2 + r] = jnp.broadcast_to(tgt, (8, HEAD))
        routed_ref[r * SRC : (r + 1) * SRC] = total


def join_kernel(*refs):
    parts, out, sems = refs[:SIDE], refs[SIDE], refs[SIDE + 1]
    copies = [
        pltpu.make_async_copy(part, out.at[pl.ds(d * ROWS, ROWS)], sems.at[i])
        for i, (part, d) in enumerate(zip(parts, LINE))
    ]
    for copy in copies:
        copy.start()
    for copy in copies:
        copy.wait()


def project_kernel(place_ref, *refs):
    blocks, (own_ref, other_ref, out_ref) = refs[:SIDE], refs[SIDE : SIDE + 3]
    rows, weight, part, sems = refs[SIDE + 3 :]
    step = WIDTH // SIDE
    copies = []
    for k in range(SIDE):
        span = pl.ds(k * step, step)
        chunk = []
        for i, ref in enumerate((own_ref, other_ref)):
            chunk.append(pltpu.make_async_copy(ref.at[span], weight.at[k, i], sems.at[k, i]))
        for i, (ref, d) in enumerate(zip(blocks, LINE)):
            into = rows.at[k, pl.ds(d * SIDE * ROWS, SIDE * ROWS)]
            chunk.append(pltpu.make_async_copy(ref.at[:, span], into, sems.at[k, 2 + i]))
        copies.append(chunk)
        for copy in chunk:
            copy.start()
    for k, chunk in enumerate(copies):
        for copy in chunk:
            copy.wait()
        for i in range(2):
            cols = slice(i * 2 * HEAD, (i + 1) * 2 * HEAD)
            term = dot(rows[k], weight[k, i], 1, 0)
            part[:, cols] = term if k == 0 else part[:, cols] + term
    for second in range(SIDE):
        for first in range(SIDE):
            start = (second * SIDE + first) * ROWS
            chip = chip_at(place_ref, first, second)
            out_ref[chip] = part[start : start + ROWS].astype(BF)


def attend_kernel(place_ref, lens_ref, q_ref, g_ref, kv_ref, ctx_ref, gq_ref, gkv_ref, keys, values):
    swapped = place_ref[4] == 1
    scaling = HEAD ** (-0.5)
    split = (GROUP, SRC, TGT)

    @pl.when(pl.program_id(0) == 0)
    def _():
        keys[...] = jnp.zeros_like(keys)
        values[...] = jnp.zeros_like(values)

    def head(array, h):
        return array[:, h * HEAD : (h + 1) * HEAD]

    for s in range(2):
        slot = slice(s * SRC, (s + 1) * SRC)
        for h in range(GROUP):
            rows, cols = slice(h * SRC, (h + 1) * SRC), slice(h * HEAD, (h + 1) * HEAD)
            own, other = (h % 2) * 2 * HEAD, (1 - h % 2) * 2 * HEAD
            for start, block in ((0, keys), (HEAD, values)):
                block[s, rows, cols] = jnp.where(
                    swapped,
                    kv_ref[h // 2, slot, other + start : other + start + HEAD],
                    kv_ref[h // 2, slot, own + start : own + start + HEAD],
                )
    grads = []
    for s in range(2):
        src = jnp.maximum(lens_ref[s][:1], 1.0)[None]
        tgt = lens_ref[2 + s][:1, :1]
        q, g = q_ref[s], g_ref[s]
        row_index = lax.broadcasted_iota(jnp.int32, (TGT, 1), 0).astype(F32)
        valid = row_index < tgt
        valid_bf = jnp.where(valid, 1.0, 0.0).astype(BF)
        grad_masked = jnp.where(valid_bf > 0.5, g, jnp.zeros_like(g))
        scores = (dot(keys[s], q, 1, 1) * scaling).reshape(split)
        key_index = lax.broadcasted_iota(jnp.int32, split, 1).astype(F32)
        scores = jnp.where(key_index < src, scores, MASKED)
        shifted = jnp.exp(scores - jnp.max(scores, axis=1, keepdims=True))
        attention = shifted / jnp.sum(shifted, axis=1, keepdims=True)
        attention_bf = attention.astype(BF)
        context = dot(attention_bf.reshape(GROUP * SRC, TGT), values[s], 0, 0)
        ctx_ref[s] = jnp.where(valid, context, 0.0).astype(BF)
        grad_attention = dot(values[s], grad_masked, 1, 1).reshape(split)
        row_dot = jnp.sum(attention * grad_attention, axis=1, keepdims=True)
        grad_scores = (attention * (grad_attention - row_dot)).astype(BF)
        grad_queries = dot(grad_scores.reshape(GROUP * SRC, TGT), keys[s], 0, 0)
        gq_ref[s] = (grad_queries * scaling).astype(BF)
        grad_keys = [
            (dot(grad_scores[h], head(q, h), 1, 0) * scaling).astype(BF) for h in range(GROUP)
        ]
        grad_values = [
            dot(attention_bf[h], head(grad_masked, h), 1, 0).astype(BF) for h in range(GROUP)
        ]
        grads.append((grad_keys, grad_values))
    for s in range(2):
        slot = slice(s * SRC, (s + 1) * SRC)
        for p in range(GROUP // 2):
            for start, grad in zip((0, HEAD), grads[s]):
                low, high = grad[2 * p], grad[2 * p + 1]
                gkv_ref[p, slot, start : start + HEAD] = jnp.where(swapped, high, low)
                start += 2 * HEAD
                gkv_ref[p, slot, start : start + HEAD] = jnp.where(swapped, low, high)


def partial_kernel(distances, place_ref, grads_ref, own_ref, other_ref, *refs):
    outs, grads = refs[:-1], refs[-1]
    width = SIDE * ROWS

    @pl.when(pl.program_id(0) == 0)
    def _():
        for i, first in enumerate(distances):
            for second in range(SIDE):
                start = (i * SIDE + second) * ROWS
                grads[start : start + ROWS] = grads_ref[chip_at(place_ref, first, second)]

    total = dot(grads[:, : 2 * HEAD], own_ref[...], 1, 1)
    total += dot(grads[:, 2 * HEAD :], other_ref[...], 1, 1)
    for i, out in enumerate(outs):
        out[...] = total[i * width : (i + 1) * width].astype(BF)


def weight_kernel(place_ref, grads_ref, *refs):
    blocks, (own_ref, other_ref, grads) = refs[:SIDE], refs[SIDE:]

    @pl.when(pl.program_id(0) == 0)
    def _():
        for i, second in enumerate(LINE):
            for first in range(SIDE):
                start = (i * SIDE + first) * ROWS
                grads[start : start + ROWS] = grads_ref[chip_at(place_ref, first, second)]

    rows = jnp.concatenate([ref[...] for ref in blocks], axis=0)
    total = dot(rows, grads[...], 0, 0).astype(BF)
    own_ref[...] = total[:, : 2 * HEAD]
    other_ref[...] = total[:, 2 * HEAD :]


def give_back_kernel(rank_ref, grads_ref, *outs):
    for d, out in zip(FAR_FIRST, outs):
        first = jnp.where(rank_ref[d][:1, :1] < 0.5, 1.0, 0.0).astype(BF)
        out[...] = jnp.where(first > 0.5, grads_ref[:SRC], grads_ref[SRC:])


def pick_kernel(place_ref, *refs):
    candidates, out_ref = refs[:PLANES], refs[PLANES]
    for d, ref in zip(FAR_FIRST, candidates):

        @pl.when(place_ref[3] == d)
        def _():
            out_ref[...] = ref[...]


def local(memory, lang_id, src_len, tgt_len, queries, key_weight, value_weight, grad_context):
    plane, y, x = lax.axis_index("lang"), lax.axis_index("y"), lax.axis_index("x")
    core = lax.axis_index("core")
    ahead = jnp.where(core == 0, lang_id[0] - plane, plane - lang_id[0])
    ahead = lax.rem(ahead + PLANES, PLANES)
    place = jnp.stack([plane, y, x, ahead, core]).astype(jnp.int32)

    with jax.named_scope("sentences_over_lang"):
        lane = lax.broadcasted_iota(jnp.int32, (SRC, HEAD), 1)
        numbers = jnp.where(lane == 0, lang_id[0], jnp.where(lane == 1, src_len[0], tgt_len[0]))
        sentence = jnp.concatenate([memory[0], numbers.astype(BF)], axis=1)

    with jax.named_scope("weights_of_chip"):
        key_own, value_own, _ = lax.optimization_barrier((key_weight[0], value_weight[0], sentence))
        own_weight = jnp.concatenate([key_own, value_own], axis=1)
        other_weight = exchange(own_weight)

    with jax.named_scope("sentences_over_lang"):
        late, other_weight = lax.optimization_barrier((sentence, other_weight))
        column = [sentence] + [shift_lang(sentence, d) for d in FAR_FIRST[1:5]]
        column += [shift_lang(late, d) for d in FAR_FIRST[5:]]

    with jax.named_scope("route"):
        routed, rank, lens = pl.pallas_call(
            route_kernel,
            out_shape=(
                jax.ShapeDtypeStruct((ROWS, WIDTH), BF),
                jax.ShapeDtypeStruct((PLANES, 8, HEAD), F32),
                jax.ShapeDtypeStruct((4, 8, HEAD), F32),
            ),
            in_specs=[SMEM] + [VMEM] * PLANES,
            out_specs=(VMEM,) * 3,
            compiler_params=params(16),
        )(place, *column)

    with jax.named_scope("gather_rows"):
        line = pl.pallas_call(
            join_kernel,
            out_shape=jax.ShapeDtypeStruct((SIDE * ROWS, WIDTH), BF),
            in_specs=[ANY] * SIDE,
            out_specs=ANY,
            scratch_shapes=[pltpu.SemaphoreType.DMA((SIDE,))],
            compiler_params=params(1),
        )(routed, *[shift_plane(routed, 0, d) for d in LINE[1:]])
        blocks = [line] + [shift_plane(line, 1, d) for d in LINE[1:]]

    with jax.named_scope("project"):
        projected = pl.pallas_call(
            project_kernel,
            out_shape=jax.ShapeDtypeStruct((CHIPS, ROWS, 4 * HEAD), BF),
            in_specs=[SMEM] + [ANY] * (SIDE + 2),
            out_specs=VMEM,
            scratch_shapes=[
                pltpu.VMEM((SIDE, CHIPS * ROWS, WIDTH // SIDE), BF),
                pltpu.VMEM((SIDE, 2, WIDTH // SIDE, 2 * HEAD), BF),
                pltpu.VMEM((CHIPS * ROWS, 4 * HEAD), F32),
                pltpu.SemaphoreType.DMA((SIDE, 2 + SIDE)),
            ],
            compiler_params=params(40),
        )(place, *blocks, own_weight, other_weight)

    with jax.named_scope("rows_to_slots"):
        slot_rows = lax.all_to_all(projected, PLANE, 0, 0, tiled=True)

    with jax.named_scope("attend"):
        groups = WIDTH // (GROUP * HEAD)
        wide = pl.BlockSpec((2, TGT, GROUP * HEAD), lambda g: (0, 0, g))
        narrow = pl.BlockSpec((GROUP // 2, ROWS, 4 * HEAD), lambda g: (g, 0, 0))
        context, grad_queries, slot_grads = pl.pallas_call(
            attend_kernel,
            grid=(groups,),
            out_shape=(
                jax.ShapeDtypeStruct((2, TGT, WIDTH), BF),
                jax.ShapeDtypeStruct((2, TGT, WIDTH), BF),
                jax.ShapeDtypeStruct((CHIPS, ROWS, 4 * HEAD), BF),
            ),
            in_specs=[SMEM, VMEM, wide, wide, narrow],
            out_specs=(wide, wide, narrow),
            scratch_shapes=[
                pltpu.VMEM((2, GROUP * SRC, GROUP * HEAD), BF),
                pltpu.VMEM((2, GROUP * SRC, GROUP * HEAD), BF),
            ],
            compiler_params=params(58),
        )(place, lens, queries[0], grad_context[0], slot_rows)

    with jax.named_scope("grads_to_heads"):
        head_grads = lax.all_to_all(slot_grads, PLANE, 0, 0, tiled=True)

    with jax.named_scope("sum_rows"):
        tile = WIDTH // SIDE
        terms = {}
        for distances in ((2, 1), (3, 0)):
            count = len(distances)
            found = pl.pallas_call(
                functools.partial(partial_kernel, distances),
                grid=(WIDTH // tile,),
                out_shape=(jax.ShapeDtypeStruct((SIDE * ROWS, WIDTH), BF),) * count,
                in_specs=[SMEM, VMEM] + [pl.BlockSpec((tile, 2 * HEAD), lambda t: (t, 0))] * 2,
                out_specs=(pl.BlockSpec((SIDE * ROWS, tile), lambda t: (0, t)),) * count,
                scratch_shapes=[pltpu.VMEM((count * SIDE * ROWS, 4 * HEAD), BF)],
                compiler_params=params(24),
                cost_estimate=cost(count * SIDE * ROWS * WIDTH * 4 * HEAD, 7),
            )(place, head_grads, own_weight, other_weight)
            terms.update(zip(distances, found))
        arrived = [terms[0]] + [shift_plane(terms[d], 0, -d) for d in LINE[1:]]
        line = sum(term.astype(F32) for term in arrived).astype(BF)

    with jax.named_scope("weight_grads"):
        head_grads, _ = lax.optimization_barrier((head_grads, terms))
        tile = WIDTH // 8
        keep, send = pl.pallas_call(
            weight_kernel,
            grid=(WIDTH // tile,),
            out_shape=(jax.ShapeDtypeStruct((WIDTH, 2 * HEAD), BF),) * 2,
            in_specs=[SMEM, VMEM]
            + [pl.BlockSpec((SIDE * ROWS, tile), lambda t: (0, t))] * SIDE,
            out_specs=(pl.BlockSpec((tile, 2 * HEAD), lambda t: (t, 0)),) * 2,
            scratch_shapes=[pltpu.VMEM((CHIPS * ROWS, 4 * HEAD), BF)],
            compiler_params=params(32),
            cost_estimate=cost(CHIPS * ROWS * WIDTH * 4 * HEAD, 16),
        )(place, head_grads, *blocks)
        both = exchange(send)
        weight_grads = [
            (keep[:, cols].astype(F32) + both[:, cols].astype(F32)).astype(BF)
            for cols in (slice(0, HEAD), slice(HEAD, 2 * HEAD))
        ]

    with jax.named_scope("sum_rows"):
        pieces = {d: line[d * ROWS : (d + 1) * ROWS] for d in LINE}
        arrived = [pieces[0]] + [shift_plane(pieces[d], 1, -d) for d in LINE[1:]]
        summed = sum(term.astype(F32) for term in arrived).astype(BF)

    with jax.named_scope("sentences_back"):
        sends = pl.pallas_call(
            give_back_kernel,
            out_shape=(jax.ShapeDtypeStruct((SRC, WIDTH), BF),) * PLANES,
            in_specs=[VMEM] * 2,
            out_specs=(VMEM,) * PLANES,
            compiler_params=params(16),
        )(rank, summed)
        late, weight_grads = lax.optimization_barrier((sends[5:], weight_grads))
        sends = [*sends[:5], *late]
        candidates = [sends[0]] + [shift_lang(sends[i], -FAR_FIRST[i]) for i in range(1, PLANES)]
        grad_memory = pl.pallas_call(
            pick_kernel,
            out_shape=jax.ShapeDtypeStruct((SRC, WIDTH), BF),
            in_specs=[SMEM] + [VMEM] * PLANES,
            out_specs=VMEM,
            compiler_params=params(16),
        )(place, *candidates)

    return (
        context[None],
        grad_queries[None],
        grad_memory[None],
        weight_grads[0][None],
        weight_grads[1][None],
    )


def solution(mesh):
    planes = mesh.shape["lang"]
    grid = Mesh(mesh.devices.reshape(planes, SIDE, SIDE, 2), ("lang", "y", "x", "core"))
    shard = ("y", "x", "core")
    every = ("lang", "y", "x", "core")
    return jax.shard_map(
        local,
        mesh=grid,
        in_specs=(
            P(every, None, None),
            P(every),
            P(every),
            P(every),
            P("lang", shard, None, None),
            P("lang", None, shard),
            P("lang", None, shard),
            P("lang", shard, None, None),
        ),
        out_specs=(
            P("lang", shard, None, None),
            P("lang", shard, None, None),
            P(every, None, None),
            P("lang", None, shard),
            P("lang", None, shard),
        ),
        check_vma=False,
    )
```

time: 206 us -> 195 us (0.947)
  waiting for transfers between devices: 74.5 us -> 68.9 us
  Pallas kernels: 29.7 us -> 26.8 us
    ppermute x40 -> x28, waiting for transfers between devices: 74.5 us -> 68.9 us  [the longest x12 56.1 us: shift_plane(): return lax.ppermute(value, ('y', 'x', 'core'), pairs)]
    pallas_call x6 -> x5, Pallas kernels: 14.5 us -> 11.3 us  [the longest x2 5.35 us: local(): pl.pallas_call(functools.partial(partial_kernel, distances), grid=(WIDTH...]
    ppermute x40 -> x28, starting transfers between devices: 61.9 us -> 60.4 us  [the longest x14 42.2 us: shift_lang(): return lax.ppermute(value, ('lang', 'core'), pairs)]
  transfers between devices with their start and end apart: 40 -> 28, of which waited for: 23 -> 15; matrix products, arithmetic and copies ran while one was open for 0% -> 1% of each run, Pallas kernels for 5% -> 4%
where the time goes in v1:
time: 195 us; the launch traced here: 194 us
  waiting for transfers between devices  68.9 us (35%)
  starting transfers between devices  60.4 us (31%)
  blocking collectives  27.8 us (14%)
  Pallas kernels  26.8 us (14%)
  local copies, waits for them, and re-layouts  3.75 us (2%)
  other arithmetic  3.66 us (2%)
  between operations  2.91 us (1%)
    ppermute x12, waiting for transfers between devices, shift_plane(): return lax.ppermute(value, ('y', 'x', 'core'), pairs)  56.1 us
    ppermute x14, starting transfers between devices, shift_lang(): return lax.ppermute(value, ('lang', 'core'), pairs)  42.2 us
    ppermute x12, starting transfers between devices, shift_plane(): return lax.ppermute(value, ('y', 'x', 'core'), pairs)  18 us
    all_to_all x1, blocking collectives, local(): slot_rows = lax.all_to_all(projected, PLANE, 0, 0, tiled=True)  14.1 us
    all_to_all x1, blocking collectives, local(): head_grads = lax.all_to_all(slot_grads, PLANE, 0, 0, tiled=True)  13.6 us
    ppermute x14, waiting for transfers between devices, shift_lang(): return lax.ppermute(value, ('lang', 'core'), pairs)  12.8 us
    pallas_call x1, Pallas kernels, local(): pl.pallas_call(attend_kernel, grid=(groups,), out_shape=(jax.ShapeDtypeSt...  10.2 us
    pallas_call x2, Pallas kernels, local(): pl.pallas_call(functools.partial(partial_kernel, distances), grid=(WIDTH...  5.35 us
  transfers between devices with their start and end apart: 28, of which 15 were waited for; matrix products, arithmetic and copies ran while one was open for 1% of the time, Pallas kernels for 4%

profile of v1, /device:TPU:32, one launch (start us, length us, event | category | flops | bytes accessed | tf_op | source)
XLA Modules:
  0.0 194.2 jit_solution(9942165712112639283)
XLA Ops:
  2.7 0.9 pad_maximum_fusion.refs_0_
  3.6 1.4 constant_dynamic-update-slice_fusion.1
  5.4 3.3 %collective-permute-start.3 = (bf16[16,4224]{1,0:T(8,128)(2,1)S(1)}, bf16[16,4224]{1,0:T(8,128)(2,1)S(1)}, u32[]{:S(2)}, u32[]{:S(2)}) collective-permute-start(bf16[16,4224]{1,0:T(8,128)(2,1)S(1)} %pad_maximum_fusion.refs_0_), channel_id=1, source_target_pairs={{0,64},{1,193},{32,96},{33,225},{64,128},{65,1},{96,160},{97,33},{... | collective-permute-start | bytes 405512 | tf_op jit(solution)/shard_map/sentences_over_lang/ppermute | solution.py:48
  8.8 2.7 %collective-permute-start.2 = (bf16[16,4224]{1,0:T(8,128)(2,1)S(1)}, bf16[16,4224]{1,0:T(8,128)(2,1)S(1)}, u32[]{:S(2)}, u32[]{:S(2)}) collective-permute-start(bf16[16,4224]{1,0:T(8,128)(2,1)S(1)} %pad_maximum_fusion.refs_0_), channel_id=1, source_target_pairs={{0,160},{1,97},{32,192},{33,129},{64,224},{65,161},{96,0},{97,193}... | collective-permute-start | bytes 405512 | tf_op jit(solution)/shard_map/sentences_over_lang/ppermute | solution.py:48
  11.4 2.4 %collective-permute-start.1 = (bf16[16,4224]{1,0:T(8,128)(2,1)S(1)}, bf16[16,4224]{1,0:T(8,128)(2,1)S(1)}, u32[]{:S(2)}, u32[]{:S(2)}) collective-permute-start(bf16[16,4224]{1,0:T(8,128)(2,1)S(1)} %pad_maximum_fusion.refs_0_), channel_id=1, source_target_pairs={{0,96},{1,161},{32,128},{33,193},{64,160},{65,225},{96,192},{97,1}... | collective-permute-start | bytes 405512 | tf_op jit(solution)/shard_map/sentences_over_lang/ppermute | solution.py:48
  13.8 4.5 %collective-permute-start = (bf16[16,4224]{1,0:T(8,128)(2,1)S(1)}, bf16[16,4224]{1,0:T(8,128)(2,1)S(1)}, u32[]{:S(2)}, u32[]{:S(2)}) collective-permute-start(bf16[16,4224]{1,0:T(8,128)(2,1)S(1)} %pad_maximum_fusion.refs_0_), channel_id=1, source_target_pairs={{0,128},{1,129},{32,160},{33,161},{64,192},{65,193},{96,224},{97,2... | collective-permute-start | bytes 405512 | tf_op jit(solution)/shard_map/sentences_over_lang/ppermute | solution.py:48
  18.3 1.3 copy-done
  19.6 2.0 %collective-permute-start.6 = (bf16[16,4224]{1,0:T(8,128)(2,1)S(1)}, bf16[16,4224]{1,0:T(8,128)(2,1)S(1)}, u32[]{:S(2)}, u32[]{:S(2)}) collective-permute-start(bf16[16,4224]{1,0:T(8,128)(2,1)S(1)} %pad_maximum_fusion.refs_0_), channel_id=1, source_target_pairs={{0,32},{1,225},{32,64},{33,1},{64,96},{65,33},{96,128},{97,65},{12... | collective-permute-start | bytes 405512 | tf_op jit(solution)/shard_map/sentences_over_lang/ppermute | solution.py:48
  21.6 7.0 %collective-permute-start.5 = (bf16[16,4224]{1,0:T(8,128)(2,1)S(1)}, bf16[16,4224]{1,0:T(8,128)(2,1)S(1)}, u32[]{:S(2)}, u32[]{:S(2)}) collective-permute-start(bf16[16,4224]{1,0:T(8,128)(2,1)S(1)} %pad_maximum_fusion.refs_0_), channel_id=1, source_target_pairs={{0,192},{1,65},{32,224},{33,97},{64,0},{65,129},{96,32},{97,161},{... | collective-permute-start | bytes 405512 | tf_op jit(solution)/shard_map/sentences_over_lang/ppermute | solution.py:48
  28.7 3.5 %collective-permute-done.refs_1_ = bf16[16,4224]{1,0:T(8,128)(2,1)S(1)} collective-permute-done((bf16[16,4224]{1,0:T(8,128)(2,1)S(1)}, bf16[16,4224]{1,0:T(8,128)(2,1)S(1)}, u32[]{:S(2)}, u32[]{:S(2)}) %collective-permute-start) | collective-permute-done | bytes 135200 | tf_op jit(solution)/shard_map/sentences_over_lang/ppermute | solution.py:48
  32.3 1.1 collective-permute-done.5.refs_5_
  33.3 0.8 route.1
  34.2 0.6 copy-done.10
  34.8 2.8 %collective-permute-start.10 = (bf16[32,4096]{1,0:T(8,128)(2,1)S(1)}, bf16[32,4096]{1,0:T(8,128)(2,1)S(1)}, u32[]{:S(2)}, u32[]{:S(2)}) collective-permute-start(bf16[32,4096]{1,0:T(8,128)(2,1)S(1)} %get-tuple-element.39.refs_0_), channel_id=1, source_target_pairs={{0,6},{1,25},{2,0},{3,27},{4,2},{5,29},{6,4},{7,31},{8,14},{9,1},{... | collective-permute-start | bytes 786440 | tf_op jit(solution)/shard_map/gather_rows/ppermute | solution.py:60
  37.6 2.3 %collective-permute-start.8 = (bf16[32,4096]{1,0:T(8,128)(2,1)S(1)}, bf16[32,4096]{1,0:T(8,128)(2,1)S(1)}, u32[]{:S(2)}, u32[]{:S(2)}) collective-permute-start(bf16[32,4096]{1,0:T(8,128)(2,1)S(1)} %get-tuple-element.39.refs_0_), channel_id=1, source_target_pairs={{0,4},{1,17},{2,6},{3,19},{4,0},{5,21},{6,2},{7,23},{8,12},{9,25},... | collective-permute-start | bytes 786440 | tf_op jit(solution)/shard_map/gather_rows/ppermute | solution.py:60
  39.9 1.6 collective-permute-done.10.refs_3_
  41.5 6.5 %collective-permute-done.9.refs_2_ = bf16[32,4096]{1,0:T(8,128)(2,1)S(1)} collective-permute-done((bf16[32,4096]{1,0:T(8,128)(2,1)S(1)}, bf16[32,4096]{1,0:T(8,128)(2,1)S(1)}, u32[]{:S(2)}, u32[]{:S(2)}) %collective-permute-start.9) | collective-permute-done | bytes 262176 | tf_op jit(solution)/shard_map/gather_rows/ppermute | solution.py:60
  48.1 3.1 %collective-permute-start.13 = (bf16[128,4096]{1,0:T(8,128)(2,1)S(1)}, bf16[128,4096]{1,0:T(8,128)(2,1)S(1)}, u32[]{:S(2)}, u32[]{:S(2)}) collective-permute-start(bf16[128,4096]{1,0:T(8,128)(2,1)S(1)} %gather_rows.1.refs_0_), channel_id=1, source_target_pairs={{0,24},{1,7},{2,26},{3,1},{4,28},{5,3},{6,30},{7,5},{8,0},{9,15},{... | collective-permute-start | bytes 3145736 | tf_op jit(solution)/shard_map/gather_rows/ppermute | solution.py:60
  51.2 2.2 %collective-permute-start.11 = (bf16[128,4096]{1,0:T(8,128)(2,1)S(1)}, bf16[128,4096]{1,0:T(8,128)(2,1)S(1)}, u32[]{:S(2)}, u32[]{:S(2)}) collective-permute-start(bf16[128,4096]{1,0:T(8,128)(2,1)S(1)} %gather_rows.1.refs_0_), channel_id=1, source_target_pairs={{0,16},{1,5},{2,18},{3,7},{4,20},{5,1},{6,22},{7,3},{8,24},{9,13},... | collective-permute-start | bytes 3145736 | tf_op jit(solution)/shard_map/gather_rows/ppermute | solution.py:60
  53.4 21.3 %collective-permute-done.13.refs_3_ = bf16[128,4096]{1,0:T(8,128)(2,1)S(1)} collective-permute-done((bf16[128,4096]{1,0:T(8,128)(2,1)S(1)}, bf16[128,4096]{1,0:T(8,128)(2,1)S(1)}, u32[]{:S(2)}, u32[]{:S(2)}) %collective-permute-start.13) | collective-permute-done | bytes 1048608 | tf_op jit(solution)/shard_map/gather_rows/ppermute | solution.py:60
  74.8 3.7 %collective-permute-done.12.refs_2_ = bf16[128,4096]{1,0:T(8,128)(2,1)S(1)} collective-permute-done((bf16[128,4096]{1,0:T(8,128)(2,1)S(1)}, bf16[128,4096]{1,0:T(8,128)(2,1)S(1)}, u32[]{:S(2)}, u32[]{:S(2)}) %collective-permute-start.12) | collective-permute-done | bytes 1048608 | tf_op jit(solution)/shard_map/gather_rows/ppermute | solution.py:60
  78.5 3.9 %project.1 = bf16[16,32,512]{2,1,0:T(8,128)(2,1)S(1)} custom-call(s32[5]{0:T(128)S(1)} %stack.23.place_ref, bf16[128,4096]{1,0:T(8,128)(2,1)S(1)} %gather_rows.1.refs_0_, bf16[128,4096]{1,0:T(8,128)(2,1)S(1)} %collective-permute-done.11.refs_1_, bf16[128,4096]{1,0:T(8,128)(2,1)S(1)} %collective-permute-done.12.refs_2_, ...), custom_call_target="tpu_custom_call" | custom-call | tf_op jit(solution)/shard_map/project/pallas_call | solution.py:308
  82.4 14.1 %all_to_all.10.kv_ref = bf16[16,32,512]{2,1,0:T(8,128)(2,1)} all-to-all(bf16[16,32,512]{2,1,0:T(8,128)(2,1)S(1)} %project.1), channel_id=1, replica_groups=mesh['lang'=8,'y'=4,'x'=4,'core'=2] {'y','x'}, dimensions={0} | all-to-all | bytes 1048576 | tf_op jit(solution)/shard_map/rows_to_slots/all_to_all | solution.py:323
  96.6 10.2 %attend.1 = (bf16[2,128,4096]{2,1,0:T(8,128)(2,1)}, bf16[2,128,4096]{2,1,0:T(8,128)(2,1)}, bf16[16,32,512]{2,1,0:T(8,128)(2,1)}) custom-call(s32[5]{0:T(128)} %copy-done.8, f32[4,8,128]{2,1,0:T(8,128)} %copy-done.10, bf16[2,128,4096]{2,1,0:T(8,128)(2,1)} %bitcast.23, bf16[2,128,4096]{2,1,0:T(8,128)(2,1)} %bitcast.24, bf16[16,32,512]{2,1,0:T(8,128)(2,1)} %all_to_all.10.kv_ref), custom_call_target="tpu_custom_call" | custom-call | tf_op jit(solution)/shard_map/attend/pallas_call | solution.py:329
  106.8 13.6 %all_to_all.11.grads_ref = bf16[16,32,512]{2,1,0:T(8,128)(2,1)S(1)} all-to-all(bf16[16,32,512]{2,1,0:T(8,128)(2,1)} %get-tuple-element.44), channel_id=1, replica_groups=mesh['lang'=8,'y'=4,'x'=4,'core'=2] {'y','x'}, dimensions={0} | all-to-all | bytes 1048576 | tf_op jit(solution)/shard_map/grads_to_heads/all_to_all | solution.py:347
  120.4 2.7 %sum_rows.3 = (bf16[128,4096]{1,0:T(8,128)(2,1)S(1)}, bf16[128,4096]{1,0:T(8,128)(2,1)S(1)}) custom-call(s32[5]{0:T(128)S(1)} %copy-done.9, bf16[16,32,512]{2,1,0:T(8,128)(2,1)S(1)} %all_to_all.11.grads_ref, bf16[4096,256]{1,0:T(8,128)(2,1)S(1)} %constant_dynamic-update-slice_fusion.refs_4_.own_ref, bf16[4096,256]{1,0:T(8,128)(2,1)S(1)} %copy-done.1), custom_call_target="tpu_custom_call" | custom-call | flops 1073741824 | bytes 7340032 | tf_op jit(solution)/shard_map/sum_rows/pallas_call | solution.py:354
  123.1 0.9 collective-permute-start.14
  124.0 2.5 %collective-permute-start.15 = (bf16[128,4096]{1,0:T(8,128)(2,1)S(1)}, bf16[128,4096]{1,0:T(8,128)(2,1)S(1)}, u32[]{:S(2)}, u32[]{:S(2)}) collective-permute-start(bf16[128,4096]{1,0:T(8,128)(2,1)S(1)} %get-tuple-element.47), channel_id=1, source_target_pairs={{0,6},{1,25},{2,0},{3,27},{4,2},{5,29},{6,4},{7,31},{8,14},{9,1},{... | collective-permute-start | bytes 3145736 | tf_op jit(solution)/shard_map/sum_rows/ppermute | solution.py:60
  126.5 2.7 %sum_rows.2 = (bf16[128,4096]{1,0:T(8,128)(2,1)S(1)}, bf16[128,4096]{1,0:T(8,128)(2,1)S(1)}) custom-call(s32[5]{0:T(128)S(1)} %copy-done.9, bf16[16,32,512]{2,1,0:T(8,128)(2,1)S(1)} %all_to_all.11.grads_ref, bf16[4096,256]{1,0:T(8,128)(2,1)S(1)} %constant_dynamic-update-slice_fusion.refs_4_.own_ref, bf16[4096,256]{1,0:T(8,128)(2,1)S(1)} %copy-done.1), custom_call_target="tpu_custom_call" | custom-call | flops 1073741824 | bytes 7340032 | tf_op jit(solution)/shard_map/sum_rows/pallas_call | solution.py:354
  129.3 5.0 %weight_grads.1 = (bf16[4096,256]{1,0:T(8,128)(2,1)S(1)}, bf16[4096,256]{1,0:T(8,128)(2,1)S(1)}) custom-call(s32[5]{0:T(128)S(1)} %copy-done.9, bf16[16,32,512]{2,1,0:T(8,128)(2,1)S(1)} %all_to_all.11.grads_ref, bf16[128,4096]{1,0:T(8,128)(2,1)S(1)} %gather_rows.1.refs_0_, bf16[128,4096]{1,0:T(8,128)(2,1)S(1)} %copy-done.7, bf16[128,4096]{1,0:T(8,128)(2,1)S(1)} %copy-done.5, ...), custom_call_target="tpu_custom_call" | custom-call | flops 2147483648 | bytes 16777216 | tf_op jit(solution)/shard_map/weight_grads/pallas_call | solution.py:371
  134.4 5.2 %collective-permute-done.14 = bf16[128,4096]{1,0:T(8,128)(2,1)S(1)} collective-permute-done((bf16[128,4096]{1,0:T(8,128)(2,1)S(1)}, bf16[128,4096]{1,0:T(8,128)(2,1)S(1)}, u32[]{:S(2)}, u32[]{:S(2)}) %collective-permute-start.14) | collective-permute-done | bytes 1048608 | tf_op jit(solution)/shard_map/sum_rows/ppermute | solution.py:60
  139.6 9.0 %collective-permute-done.15 = bf16[128,4096]{1,0:T(8,128)(2,1)S(1)} collective-permute-done((bf16[128,4096]{1,0:T(8,128)(2,1)S(1)}, bf16[128,4096]{1,0:T(8,128)(2,1)S(1)}, u32[]{:S(2)}, u32[]{:S(2)}) %collective-permute-start.15) | collective-permute-done | bytes 1048608 | tf_op jit(solution)/shard_map/sum_rows/ppermute | solution.py:60
  148.6 2.1 %collective-permute-done.16 = bf16[128,4096]{1,0:T(8,128)(2,1)S(1)} collective-permute-done((bf16[128,4096]{1,0:T(8,128)(2,1)S(1)}, bf16[128,4096]{1,0:T(8,128)(2,1)S(1)}, u32[]{:S(2)}, u32[]{:S(2)}) %collective-permute-start.16) | collective-permute-done | bytes 1048608 | tf_op jit(solution)/shard_map/sum_rows/ppermute | solution.py:60
  150.7 0.6 add_convert_fusion.2
  151.4 0.9 collective-permute-start.17
  152.3 0.9 collective-permute-start.19
  153.2 2.4 %collective-permute-start.18 = (bf16[32,4096]{1,0:T(8,128)(2,1)S(1)}, bf16[32,4096]{1,0:T(8,128)(2,1)S(1)}, u32[]{:S(2)}, u32[]{:S(2)}) collective-permute-start(bf16[32,4096]{1,0:T(8,128)(2,1)S(1)} %get-tuple-element.69), channel_id=1, source_target_pairs={{0,24},{1,7},{2,26},{3,1},{4,28},{5,3},{6,30},{7,5},{8,0},{9,15},{... | collective-permute-start | bytes 786440 | tf_op jit(solution)/shard_map/sum_rows/ppermute | solution.py:60
  155.6 3.9 %collective-permute-done.17 = bf16[32,4096]{1,0:T(8,128)(2,1)S(1)} collective-permute-done((bf16[32,4096]{1,0:T(8,128)(2,1)S(1)}, bf16[32,4096]{1,0:T(8,128)(2,1)S(1)}, u32[]{:S(2)}, u32[]{:S(2)}) %collective-permute-start.17) | collective-permute-done | bytes 262176 | tf_op jit(solution)/shard_map/sum_rows/ppermute | solution.py:60
  159.5 2.7 %collective-permute-done.19 = bf16[32,4096]{1,0:T(8,128)(2,1)S(1)} collective-permute-done((bf16[32,4096]{1,0:T(8,128)(2,1)S(1)}, bf16[32,4096]{1,0:T(8,128)(2,1)S(1)}, u32[]{:S(2)}, u32[]{:S(2)}) %collective-permute-start.19) | collective-permute-done | bytes 262176 | tf_op jit(solution)/shard_map/sum_rows/ppermute | solution.py:60
  162.5 11.9 %collective-permute-start.20 = (bf16[16,4096]{1,0:T(8,128)(2,1)S(1)}, bf16[16,4096]{1,0:T(8,128)(2,1)S(1)}, u32[]{:S(2)}, u32[]{:S(2)}) collective-permute-start(bf16[16,4096]{1,0:T(8,128)(2,1)S(1)} %get-tuple-element.50), channel_id=1, source_target_pairs={{0,128},{1,129},{32,160},{33,161},{64,192},{65,193},{96,224},{97,2... | collective-permute-start | bytes 393224 | tf_op jit(solution)/shard_map/sentences_back/ppermute | solution.py:48
  174.4 5.0 %collective-permute-start.22 = (bf16[16,4096]{1,0:T(8,128)(2,1)S(1)}, bf16[16,4096]{1,0:T(8,128)(2,1)S(1)}, u32[]{:S(2)}, u32[]{:S(2)}) collective-permute-start(bf16[16,4096]{1,0:T(8,128)(2,1)S(1)} %get-tuple-element.52), channel_id=1, source_target_pairs={{0,96},{1,161},{32,128},{33,193},{64,160},{65,225},{96,192},{97,1}... | collective-permute-start | bytes 393224 | tf_op jit(solution)/shard_map/sentences_back/ppermute | solution.py:48
  179.4 3.1 %collective-permute-start.23 = (bf16[16,4096]{1,0:T(8,128)(2,1)S(1)}, bf16[16,4096]{1,0:T(8,128)(2,1)S(1)}, u32[]{:S(2)}, u32[]{:S(2)}) collective-permute-start(bf16[16,4096]{1,0:T(8,128)(2,1)S(1)} %get-tuple-element.53), channel_id=1, source_target_pairs={{0,192},{1,65},{32,224},{33,97},{64,0},{65,129},{96,32},{97,161},{... | collective-permute-start | bytes 393224 | tf_op jit(solution)/shard_map/sentences_back/ppermute | solution.py:48
  182.5 1.9 %add_convert_fusion = (bf16[4096,128]{1,0:T(8,128)(2,1)}, bf16[4096,128]{1,0:T(8,128)(2,1)}) fusion(bf16[4096,256]{1,0:T(8,128)(2,1)S(1)} %collective-permute-done.24, bf16[4096,256]{1,0:T(8,128)(2,1)S(1)} %get-tuple-element.58), kind=kLoop, calls=%fused_computation | loop fusion | flops 4194304 | bytes 6291456 | tf_op jit(solution)/shard_map/weight_grads/convert_element_type | solution.py:384
  184.5 1.8 collective-permute-done.21.refs_2_
  186.5 1.1 collective-permute-done.23.refs_4_
  187.6 4.0 %collective-permute-done.25.refs_5_ = bf16[16,4096]{1,0:T(8,128)(2,1)S(1)} collective-permute-done((bf16[16,4096]{1,0:T(8,128)(2,1)S(1)}, bf16[16,4096]{1,0:T(8,128)(2,1)S(1)}, u32[]{:S(2)}, u32[]{:S(2)}) %collective-permute-start.25) | collective-permute-done | bytes 131104 | tf_op jit(solution)/shard_map/sentences_back/ppermute | solution.py:48
  191.6 1.3 collective-permute-done.27.refs_7_
  192.9 1.3 sentences_back.3
  (54 shorter events, 1.4 us)
Async XLA Ops:
  0.6 4.4 %copy-start.11 = (bf16[1,4096,128]{2,1,0:T(8,128)(2,1)S(1)}, bf16[1,4096,128]{2,1,0:T(8,128)(2,1)}, u32[]{:S(2)}) copy-start(bf16[1,4096,128]{2,1,0:T(8,128)(2,1)} %param.14) | copy-start | bytes 3145732
  5.3 13.0 %collective-permute-start.4 = (bf16[4096,256]{1,0:T(8,128)(2,1)S(1)}, bf16[4096,256]{1,0:T(8,128)(2,1)S(1)}, u32[]{:S(2)}, u32[]{:S(2)}) collective-permute-start(bf16[4096,256]{1,0:T(8,128)(2,1)S(1)} %constant_dynamic-update-slice_fusion.refs_4_.own_ref), channel_id=1, source_target_pairs={{0,1},{1,0},{2,3},{3,2},{4,5},{5,4},{6,7},{7,6},{8,9},{9,8},{10,11... | collective-permute-start | bytes 6291464 | tf_op jit(solution)/shard_map/weights_of_chip/ppermute | solution.py:39
  5.4 14.2 %collective-permute-start.3 = (bf16[16,4224]{1,0:T(8,128)(2,1)S(1)}, bf16[16,4224]{1,0:T(8,128)(2,1)S(1)}, u32[]{:S(2)}, u32[]{:S(2)}) collective-permute-start(bf16[16,4224]{1,0:T(8,128)(2,1)S(1)} %pad_maximum_fusion.refs_0_), channel_id=1, source_target_pairs={{0,64},{1,193},{32,96},{33,225},{64,128},{65,1},{96,160},{97,33},{... | collective-permute-start | bytes 405512 | tf_op jit(solution)/shard_map/sentences_over_lang/ppermute | solution.py:48
  8.8 12.9 %collective-permute-start.2 = (bf16[16,4224]{1,0:T(8,128)(2,1)S(1)}, bf16[16,4224]{1,0:T(8,128)(2,1)S(1)}, u32[]{:S(2)}, u32[]{:S(2)}) collective-permute-start(bf16[16,4224]{1,0:T(8,128)(2,1)S(1)} %pad_maximum_fusion.refs_0_), channel_id=1, source_target_pairs={{0,160},{1,97},{32,192},{33,129},{64,224},{65,161},{96,0},{97,193}... | collective-permute-start | bytes 405512 | tf_op jit(solution)/shard_map/sentences_over_lang/ppermute | solution.py:48
  11.4 17.3 %collective-permute-start.1 = (bf16[16,4224]{1,0:T(8,128)(2,1)S(1)}, bf16[16,4224]{1,0:T(8,128)(2,1)S(1)}, u32[]{:S(2)}, u32[]{:S(2)}) collective-permute-start(bf16[16,4224]{1,0:T(8,128)(2,1)S(1)} %pad_maximum_fusion.refs_0_), channel_id=1, source_target_pairs={{0,96},{1,161},{32,128},{33,193},{64,160},{65,225},{96,192},{97,1}... | collective-permute-start | bytes 405512 | tf_op jit(solution)/shard_map/sentences_over_lang/ppermute | solution.py:48
  13.8 18.5 %collective-permute-start = (bf16[16,4224]{1,0:T(8,128)(2,1)S(1)}, bf16[16,4224]{1,0:T(8,128)(2,1)S(1)}, u32[]{:S(2)}, u32[]{:S(2)}) collective-permute-start(bf16[16,4224]{1,0:T(8,128)(2,1)S(1)} %pad_maximum_fusion.refs_0_), channel_id=1, source_target_pairs={{0,128},{1,129},{32,160},{33,161},{64,192},{65,193},{96,224},{97,2... | collective-permute-start | bytes 405512 | tf_op jit(solution)/shard_map/sentences_over_lang/ppermute | solution.py:48
  18.3 1.3 copy-start
  19.6 12.7 %collective-permute-start.7 = (bf16[16,4224]{1,0:T(8,128)(2,1)S(1)}, bf16[16,4224]{1,0:T(8,128)(2,1)S(1)}, u32[]{:S(2)}, u32[]{:S(2)}) collective-permute-start(bf16[16,4224]{1,0:T(8,128)(2,1)S(1)} %pad_maximum_fusion.refs_0_), channel_id=1, source_target_pairs={{0,224},{1,33},{32,0},{33,65},{64,32},{65,97},{96,64},{97,129},{12... | collective-permute-start | bytes 405512 | tf_op jit(solution)/shard_map/sentences_over_lang/ppermute | solution.py:48
  19.6 12.7 %collective-permute-start.6 = (bf16[16,4224]{1,0:T(8,128)(2,1)S(1)}, bf16[16,4224]{1,0:T(8,128)(2,1)S(1)}, u32[]{:S(2)}, u32[]{:S(2)}) collective-permute-start(bf16[16,4224]{1,0:T(8,128)(2,1)S(1)} %pad_maximum_fusion.refs_0_), channel_id=1, source_target_pairs={{0,32},{1,225},{32,64},{33,1},{64,96},{65,33},{96,128},{97,65},{12... | collective-permute-start | bytes 405512 | tf_op jit(solution)/shard_map/sentences_over_lang/ppermute | solution.py:48
  21.6 11.7 %collective-permute-start.5 = (bf16[16,4224]{1,0:T(8,128)(2,1)S(1)}, bf16[16,4224]{1,0:T(8,128)(2,1)S(1)}, u32[]{:S(2)}, u32[]{:S(2)}) collective-permute-start(bf16[16,4224]{1,0:T(8,128)(2,1)S(1)} %pad_maximum_fusion.refs_0_), channel_id=1, source_target_pairs={{0,192},{1,65},{32,224},{33,97},{64,0},{65,129},{96,32},{97,161},{... | collective-permute-start | bytes 405512 | tf_op jit(solution)/shard_map/sentences_over_lang/ppermute | solution.py:48
  28.7 53.6 %copy-start.8 = (s32[5]{0:T(128)}, s32[5]{0:T(128)S(1)}, u32[]{:S(2)}) copy-start(s32[5]{0:T(128)S(1)} %stack.23.place_ref) | copy-start | bytes 64
  28.7 49.8 %copy-start.1 = (bf16[4096,256]{1,0:T(8,128)(2,1)S(1)}, bf16[4096,256]{1,0:T(8,128)(2,1)}, u32[]{:S(2)}) copy-start(bf16[4096,256]{1,0:T(8,128)(2,1)} %copy-done) | copy-start | bytes 6291460
  34.2 0.6 copy-start.10
  34.8 6.7 %collective-permute-start.10 = (bf16[32,4096]{1,0:T(8,128)(2,1)S(1)}, bf16[32,4096]{1,0:T(8,128)(2,1)S(1)}, u32[]{:S(2)}, u32[]{:S(2)}) collective-permute-start(bf16[32,4096]{1,0:T(8,128)(2,1)S(1)} %get-tuple-element.39.refs_0_), channel_id=1, source_target_pairs={{0,6},{1,25},{2,0},{3,27},{4,2},{5,29},{6,4},{7,31},{8,14},{9,1},{... | collective-permute-start | bytes 786440 | tf_op jit(solution)/shard_map/gather_rows/ppermute | solution.py:60
  37.6 10.4 %collective-permute-start.9 = (bf16[32,4096]{1,0:T(8,128)(2,1)S(1)}, bf16[32,4096]{1,0:T(8,128)(2,1)S(1)}, u32[]{:S(2)}, u32[]{:S(2)}) collective-permute-start(bf16[32,4096]{1,0:T(8,128)(2,1)S(1)} %get-tuple-element.39.refs_0_), channel_id=1, source_target_pairs={{0,2},{1,9},{2,4},{3,11},{4,6},{5,13},{6,0},{7,15},{8,10},{9,17},{... | collective-permute-start | bytes 786440 | tf_op jit(solution)/shard_map/gather_rows/ppermute | solution.py:60
  37.6 10.4 %collective-permute-start.8 = (bf16[32,4096]{1,0:T(8,128)(2,1)S(1)}, bf16[32,4096]{1,0:T(8,128)(2,1)S(1)}, u32[]{:S(2)}, u32[]{:S(2)}) collective-permute-start(bf16[32,4096]{1,0:T(8,128)(2,1)S(1)} %get-tuple-element.39.refs_0_), channel_id=1, source_target_pairs={{0,4},{1,17},{2,6},{3,19},{4,0},{5,21},{6,2},{7,23},{8,12},{9,25},... | collective-permute-start | bytes 786440 | tf_op jit(solution)/shard_map/gather_rows/ppermute | solution.py:60
  48.1 26.6 %collective-permute-start.13 = (bf16[128,4096]{1,0:T(8,128)(2,1)S(1)}, bf16[128,4096]{1,0:T(8,128)(2,1)S(1)}, u32[]{:S(2)}, u32[]{:S(2)}) collective-permute-start(bf16[128,4096]{1,0:T(8,128)(2,1)S(1)} %gather_rows.1.refs_0_), channel_id=1, source_target_pairs={{0,24},{1,7},{2,26},{3,1},{4,28},{5,3},{6,30},{7,5},{8,0},{9,15},{... | collective-permute-start | bytes 3145736 | tf_op jit(solution)/shard_map/gather_rows/ppermute | solution.py:60
  51.2 27.2 %collective-permute-start.12 = (bf16[128,4096]{1,0:T(8,128)(2,1)S(1)}, bf16[128,4096]{1,0:T(8,128)(2,1)S(1)}, u32[]{:S(2)}, u32[]{:S(2)}) collective-permute-start(bf16[128,4096]{1,0:T(8,128)(2,1)S(1)} %gather_rows.1.refs_0_), channel_id=1, source_target_pairs={{0,8},{1,3},{2,10},{3,5},{4,12},{5,7},{6,14},{7,1},{8,16},{9,11},{... | collective-permute-start | bytes 3145736 | tf_op jit(solution)/shard_map/gather_rows/ppermute | solution.py:60
  51.2 27.2 %collective-permute-start.11 = (bf16[128,4096]{1,0:T(8,128)(2,1)S(1)}, bf16[128,4096]{1,0:T(8,128)(2,1)S(1)}, u32[]{:S(2)}, u32[]{:S(2)}) collective-permute-start(bf16[128,4096]{1,0:T(8,128)(2,1)S(1)} %gather_rows.1.refs_0_), channel_id=1, source_target_pairs={{0,16},{1,5},{2,18},{3,7},{4,20},{5,1},{6,22},{7,3},{8,24},{9,13},... | collective-permute-start | bytes 3145736 | tf_op jit(solution)/shard_map/gather_rows/ppermute | solution.py:60
  74.8 7.6 %copy-start.2 = (bf16[128,4096]{1,0:T(8,128)(2,1)}, bf16[128,4096]{1,0:T(8,128)(2,1)S(1)}, u32[]{:S(2)}) copy-start(bf16[128,4096]{1,0:T(8,128)(2,1)S(1)} %collective-permute-done.13.refs_3_) | copy-start | bytes 3145732
  78.5 3.9 %copy-start.4 = (bf16[128,4096]{1,0:T(8,128)(2,1)}, bf16[128,4096]{1,0:T(8,128)(2,1)S(1)}, u32[]{:S(2)}) copy-start(bf16[128,4096]{1,0:T(8,128)(2,1)S(1)} %collective-permute-done.12.refs_2_) | copy-start | bytes 3145732
  78.5 3.9 %copy-start.6 = (bf16[128,4096]{1,0:T(8,128)(2,1)}, bf16[128,4096]{1,0:T(8,128)(2,1)S(1)}, u32[]{:S(2)}) copy-start(bf16[128,4096]{1,0:T(8,128)(2,1)S(1)} %collective-permute-done.11.refs_1_) | copy-start | bytes 3145732
  96.6 23.8 %copy-start.9 = (s32[5]{0:T(128)S(1)}, s32[5]{0:T(128)}, u32[]{:S(2)}) copy-start(s32[5]{0:T(128)} %copy-done.8) | copy-start | bytes 64
  123.1 16.5 %collective-permute-start.14 = (bf16[128,4096]{1,0:T(8,128)(2,1)S(1)}, bf16[128,4096]{1,0:T(8,128)(2,1)S(1)}, u32[]{:S(2)}, u32[]{:S(2)}) collective-permute-start(bf16[128,4096]{1,0:T(8,128)(2,1)S(1)} %get-tuple-element.46), channel_id=1, source_target_pairs={{0,4},{1,17},{2,6},{3,19},{4,0},{5,21},{6,2},{7,23},{8,12},{9,25},... | collective-permute-start | bytes 3145736 | tf_op jit(solution)/shard_map/sum_rows/ppermute | solution.py:60
  124.0 5.3 %copy-start.3 = (bf16[128,4096]{1,0:T(8,128)(2,1)S(1)}, bf16[128,4096]{1,0:T(8,128)(2,1)}, u32[]{:S(2)}) copy-start(bf16[128,4096]{1,0:T(8,128)(2,1)} %copy-done.2) | copy-start | bytes 3145732
  124.0 5.3 %copy-start.5 = (bf16[128,4096]{1,0:T(8,128)(2,1)S(1)}, bf16[128,4096]{1,0:T(8,128)(2,1)}, u32[]{:S(2)}) copy-start(bf16[128,4096]{1,0:T(8,128)(2,1)} %copy-done.4) | copy-start | bytes 3145732
  124.0 5.3 %copy-start.7 = (bf16[128,4096]{1,0:T(8,128)(2,1)S(1)}, bf16[128,4096]{1,0:T(8,128)(2,1)}, u32[]{:S(2)}) copy-start(bf16[128,4096]{1,0:T(8,128)(2,1)} %copy-done.6) | copy-start | bytes 3145732
  124.0 24.6 %collective-permute-start.15 = (bf16[128,4096]{1,0:T(8,128)(2,1)S(1)}, bf16[128,4096]{1,0:T(8,128)(2,1)S(1)}, u32[]{:S(2)}, u32[]{:S(2)}) collective-permute-start(bf16[128,4096]{1,0:T(8,128)(2,1)S(1)} %get-tuple-element.47), channel_id=1, source_target_pairs={{0,6},{1,25},{2,0},{3,27},{4,2},{5,29},{6,4},{7,31},{8,14},{9,1},{... | collective-permute-start | bytes 3145736 | tf_op jit(solution)/shard_map/sum_rows/ppermute | solution.py:60
  129.2 21.6 %collective-permute-start.16 = (bf16[128,4096]{1,0:T(8,128)(2,1)S(1)}, bf16[128,4096]{1,0:T(8,128)(2,1)S(1)}, u32[]{:S(2)}, u32[]{:S(2)}) collective-permute-start(bf16[128,4096]{1,0:T(8,128)(2,1)S(1)} %get-tuple-element.48), channel_id=1, source_target_pairs={{0,2},{1,9},{2,4},{3,11},{4,6},{5,13},{6,0},{7,15},{8,10},{9,17},{... | collective-permute-start | bytes 3145736 | tf_op jit(solution)/shard_map/sum_rows/ppermute | solution.py:60
  134.3 48.2 %collective-permute-start.24 = (bf16[4096,256]{1,0:T(8,128)(2,1)S(1)}, bf16[4096,256]{1,0:T(8,128)(2,1)S(1)}, u32[]{:S(2)}, u32[]{:S(2)}) collective-permute-start(bf16[4096,256]{1,0:T(8,128)(2,1)S(1)} %get-tuple-element.59), channel_id=1, source_target_pairs={{0,1},{1,0},{2,3},{3,2},{4,5},{5,4},{6,7},{7,6},{8,9},{9,8},{10,11... | collective-permute-start | bytes 6291464 | tf_op jit(solution)/shard_map/weight_grads/ppermute | solution.py:39
  151.4 8.1 %collective-permute-start.17 = (bf16[32,4096]{1,0:T(8,128)(2,1)S(1)}, bf16[32,4096]{1,0:T(8,128)(2,1)S(1)}, u32[]{:S(2)}, u32[]{:S(2)}) collective-permute-start(bf16[32,4096]{1,0:T(8,128)(2,1)S(1)} %get-tuple-element.67), channel_id=1, source_target_pairs={{0,16},{1,5},{2,18},{3,7},{4,20},{5,1},{6,22},{7,3},{8,24},{9,13},... | collective-permute-start | bytes 786440 | tf_op jit(solution)/shard_map/sum_rows/ppermute | solution.py:60
  152.3 9.9 %collective-permute-start.19 = (bf16[32,4096]{1,0:T(8,128)(2,1)S(1)}, bf16[32,4096]{1,0:T(8,128)(2,1)S(1)}, u32[]{:S(2)}, u32[]{:S(2)}) collective-permute-start(bf16[32,4096]{1,0:T(8,128)(2,1)S(1)} %get-tuple-element.68), channel_id=1, source_target_pairs={{0,8},{1,3},{2,10},{3,5},{4,12},{5,7},{6,14},{7,1},{8,16},{9,11},{... | collective-permute-start | bytes 786440 | tf_op jit(solution)/shard_map/sum_rows/ppermute | solution.py:60
  153.2 9.0 %collective-permute-start.18 = (bf16[32,4096]{1,0:T(8,128)(2,1)S(1)}, bf16[32,4096]{1,0:T(8,128)(2,1)S(1)}, u32[]{:S(2)}, u32[]{:S(2)}) collective-permute-start(bf16[32,4096]{1,0:T(8,128)(2,1)S(1)} %get-tuple-element.69), channel_id=1, source_target_pairs={{0,24},{1,7},{2,26},{3,1},{4,28},{5,3},{6,30},{7,5},{8,0},{9,15},{... | collective-permute-start | bytes 786440 | tf_op jit(solution)/shard_map/sum_rows/ppermute | solution.py:60
  162.5 22.0 %collective-permute-start.20 = (bf16[16,4096]{1,0:T(8,128)(2,1)S(1)}, bf16[16,4096]{1,0:T(8,128)(2,1)S(1)}, u32[]{:S(2)}, u32[]{:S(2)}) collective-permute-start(bf16[16,4096]{1,0:T(8,128)(2,1)S(1)} %get-tuple-element.50), channel_id=1, source_target_pairs={{0,128},{1,129},{32,160},{33,161},{64,192},{65,193},{96,224},{97,2... | collective-permute-start | bytes 393224 | tf_op jit(solution)/shard_map/sentences_back/ppermute | solution.py:48
  174.4 11.9 %collective-permute-start.21 = (bf16[16,4096]{1,0:T(8,128)(2,1)S(1)}, bf16[16,4096]{1,0:T(8,128)(2,1)S(1)}, u32[]{:S(2)}, u32[]{:S(2)}) collective-permute-start(bf16[16,4096]{1,0:T(8,128)(2,1)S(1)} %get-tuple-element.51), channel_id=1, source_target_pairs={{0,160},{1,97},{32,192},{33,129},{64,224},{65,161},{96,0},{97,193}... | collective-permute-start | bytes 393224 | tf_op jit(solution)/shard_map/sentences_back/ppermute | solution.py:48
  174.4 12.1 %collective-permute-start.22 = (bf16[16,4096]{1,0:T(8,128)(2,1)S(1)}, bf16[16,4096]{1,0:T(8,128)(2,1)S(1)}, u32[]{:S(2)}, u32[]{:S(2)}) collective-permute-start(bf16[16,4096]{1,0:T(8,128)(2,1)S(1)} %get-tuple-element.52), channel_id=1, source_target_pairs={{0,96},{1,161},{32,128},{33,193},{64,160},{65,225},{96,192},{97,1}... | collective-permute-start | bytes 393224 | tf_op jit(solution)/shard_map/sentences_back/ppermute | solution.py:48
  179.4 8.2 %collective-permute-start.23 = (bf16[16,4096]{1,0:T(8,128)(2,1)S(1)}, bf16[16,4096]{1,0:T(8,128)(2,1)S(1)}, u32[]{:S(2)}, u32[]{:S(2)}) collective-permute-start(bf16[16,4096]{1,0:T(8,128)(2,1)S(1)} %get-tuple-element.53), channel_id=1, source_target_pairs={{0,192},{1,65},{32,224},{33,97},{64,0},{65,129},{96,32},{97,161},{... | collective-permute-start | bytes 393224 | tf_op jit(solution)/shard_map/sentences_back/ppermute | solution.py:48
  184.5 7.2 %collective-permute-start.25 = (bf16[16,4096]{1,0:T(8,128)(2,1)S(1)}, bf16[16,4096]{1,0:T(8,128)(2,1)S(1)}, u32[]{:S(2)}, u32[]{:S(2)}) collective-permute-start(bf16[16,4096]{1,0:T(8,128)(2,1)S(1)} %get-tuple-element.60), channel_id=1, source_target_pairs={{0,64},{1,193},{32,96},{33,225},{64,128},{65,1},{96,160},{97,33},{... | collective-permute-start | bytes 393224 | tf_op jit(solution)/shard_map/sentences_back/ppermute | solution.py:48
  184.5 7.2 %collective-permute-start.26 = (bf16[16,4096]{1,0:T(8,128)(2,1)S(1)}, bf16[16,4096]{1,0:T(8,128)(2,1)S(1)}, u32[]{:S(2)}, u32[]{:S(2)}) collective-permute-start(bf16[16,4096]{1,0:T(8,128)(2,1)S(1)} %get-tuple-element.61), channel_id=1, source_target_pairs={{0,224},{1,33},{32,0},{33,65},{64,32},{65,97},{96,64},{97,129},{12... | collective-permute-start | bytes 393224 | tf_op jit(solution)/shard_map/sentences_back/ppermute | solution.py:48
  186.3 6.7 %collective-permute-start.27 = (bf16[16,4096]{1,0:T(8,128)(2,1)S(1)}, bf16[16,4096]{1,0:T(8,128)(2,1)S(1)}, u32[]{:S(2)}, u32[]{:S(2)}) collective-permute-start(bf16[16,4096]{1,0:T(8,128)(2,1)S(1)} %get-tuple-element.62), channel_id=1, source_target_pairs={{0,32},{1,225},{32,64},{33,1},{64,96},{65,33},{96,128},{97,65},{12... | collective-permute-start | bytes 393224 | tf_op jit(solution)/shard_map/sentences_back/ppermute | solution.py:48

commit v2 on v1

--- a/solution.py
+++ b/solution.py
@@ -21,7 +21,9 @@
 F32 = jnp.float32
 PLANE = ("y", "x")
 FAR_FIRST = (0, 4, 3, 5, 2, 6, 1, 7)
+NEAR_FIRST = (0, 7, 1, 6, 2, 5, 3, 4)
 LINE = (0, 2, 1, 3)
+EARLY, LATE = (0, 3), (1, 2)
 VMEM = pl.BlockSpec(memory_space=pltpu.VMEM)
 SMEM = pl.BlockSpec(memory_space=pltpu.SMEM)
 ANY = pl.BlockSpec(memory_space=pl.ANY)
@@ -73,7 +75,7 @@
 
 def route_kernel(place_ref, *refs):
     sentences, (routed_ref, rank_ref, lens_ref) = refs[:PLANES], refs[PLANES:]
-    sentences = [sentences[FAR_FIRST.index(d)] for d in range(PLANES)]
+    sentences = [sentences[NEAR_FIRST.index(d)] for d in range(PLANES)]
     plane, core = place_ref[0], place_ref[4]
     plane_f = plane.astype(F32)
     match, rank = [], []
@@ -117,19 +119,21 @@
         copy.wait()
 
 
-def project_kernel(place_ref, *refs):
-    blocks, (own_ref, other_ref, out_ref) = refs[:SIDE], refs[SIDE : SIDE + 3]
-    rows, weight, part, sems = refs[SIDE + 3 :]
+def project_kernel(distances, place_ref, *refs):
+    count = len(distances)
+    blocks, weights, out_ref = refs[:count], refs[count : count + 4], refs[count + 4]
+    rows, weight, part, sems = refs[count + 5 :]
     step = WIDTH // SIDE
     copies = []
     for k in range(SIDE):
         span = pl.ds(k * step, step)
         chunk = []
-        for i, ref in enumerate((own_ref, other_ref)):
-            chunk.append(pltpu.make_async_copy(ref.at[span], weight.at[k, i], sems.at[k, i]))
-        for i, (ref, d) in enumerate(zip(blocks, LINE)):
-            into = rows.at[k, pl.ds(d * SIDE * ROWS, SIDE * ROWS)]
-            chunk.append(pltpu.make_async_copy(ref.at[:, span], into, sems.at[k, 2 + i]))
+        for i, ref in enumerate(weights):
+            into = weight.at[k, i // 2, :, pl.ds(i % 2 * HEAD, HEAD)]
+            chunk.append(pltpu.make_async_copy(ref.at[span], into, sems.at[k, i]))
+        for i, ref in enumerate(blocks):
+            into = rows.at[k, pl.ds(i * SIDE * ROWS, SIDE * ROWS)]
+            chunk.append(pltpu.make_async_copy(ref.at[:, span], into, sems.at[k, 4 + i]))
         copies.append(chunk)
         for copy in chunk:
             copy.start()
@@ -140,25 +144,31 @@
             cols = slice(i * 2 * HEAD, (i + 1) * 2 * HEAD)
             term = dot(rows[k], weight[k, i], 1, 0)
             part[:, cols] = term if k == 0 else part[:, cols] + term
-    for second in range(SIDE):
-        for first in range(SIDE):
-            start = (second * SIDE + first) * ROWS
-            chip = chip_at(place_ref, first, second)
-            out_ref[chip] = part[start : start + ROWS].astype(BF)
-
-
-def attend_kernel(place_ref, lens_ref, q_ref, g_ref, kv_ref, ctx_ref, gq_ref, gkv_ref, keys, values):
+    out_ref[...] = part[...].astype(BF)
+
+
+def project_rest_kernel(distances, place_ref, early_ref, *refs):
+    count = len(distances) + 4
+    out_ref, late = refs[count], refs[-1]
+    project_kernel(distances, place_ref, *refs[:count], late, *refs[count + 1 : -1])
+    for found, seconds in ((early_ref, EARLY), (late, distances)):
+        for i, second in enumerate(seconds):
+            for first in range(SIDE):
+                start = (i * SIDE + first) * ROWS
+                out_ref[chip_at(place_ref, first, second)] = found[start : start + ROWS]
+
+
+def head(array, h):
+    return array[:, h * HEAD : (h + 1) * HEAD]
+
+
+def lay_out(place_ref, kv_ref, keys, values):
     swapped = place_ref[4] == 1
-    scaling = HEAD ** (-0.5)
-    split = (GROUP, SRC, TGT)
 
     @pl.when(pl.program_id(0) == 0)
     def _():
         keys[...] = jnp.zeros_like(keys)
         values[...] = jnp.zeros_like(values)
-
-    def head(array, h):
-        return array[:, h * HEAD : (h + 1) * HEAD]
 
     for s in range(2):
         slot = slice(s * SRC, (s + 1) * SRC)
@@ -171,28 +181,37 @@
                     kv_ref[h // 2, slot, other + start : other + start + HEAD],
                     kv_ref[h // 2, slot, own + start : own + start + HEAD],
                 )
+
+
+def valid_rows(lens_ref, s):
+    row_index = lax.broadcasted_iota(jnp.int32, (TGT, 1), 0).astype(F32)
+    return row_index < lens_ref[2 + s][:1, :1]
+
+
+def attend_kernel(
+    place_ref, lens_ref, q_ref, g_ref, kv_ref, gkv_ref, attention_ref, grad_scores_ref, keys, values
+):
+    swapped = place_ref[4] == 1
+    scaling = HEAD ** (-0.5)
+    split = (GROUP, SRC, TGT)
+    lay_out(place_ref, kv_ref, keys, values)
     grads = []
     for s in range(2):
         src = jnp.maximum(lens_ref[s][:1], 1.0)[None]
-        tgt = lens_ref[2 + s][:1, :1]
         q, g = q_ref[s], g_ref[s]
-        row_index = lax.broadcasted_iota(jnp.int32, (TGT, 1), 0).astype(F32)
-        valid = row_index < tgt
-        valid_bf = jnp.where(valid, 1.0, 0.0).astype(BF)
-        grad_masked = jnp.where(valid_bf > 0.5, g, jnp.zeros_like(g))
+        valid = jnp.where(valid_rows(lens_ref, s), 1.0, 0.0).astype(BF)
+        grad_masked = jnp.where(valid > 0.5, g, jnp.zeros_like(g))
         scores = (dot(keys[s], q, 1, 1) * scaling).reshape(split)
         key_index = lax.broadcasted_iota(jnp.int32, split, 1).astype(F32)
         scores = jnp.where(key_index < src, scores, MASKED)
         shifted = jnp.exp(scores - jnp.max(scores, axis=1, keepdims=True))
         attention = shifted / jnp.sum(shifted, axis=1, keepdims=True)
         attention_bf = attention.astype(BF)
-        context = dot(attention_bf.reshape(GROUP * SRC, TGT), values[s], 0, 0)
-        ctx_ref[s] = jnp.where(valid, context, 0.0).astype(BF)
+        attention_ref[s] = attention_bf.reshape(GROUP * SRC, TGT)
         grad_attention = dot(values[s], grad_masked, 1, 1).reshape(split)
         row_dot = jnp.sum(attention * grad_attention, axis=1, keepdims=True)
         grad_scores = (attention * (grad_attention - row_dot)).astype(BF)
-        grad_queries = dot(grad_scores.reshape(GROUP * SRC, TGT), keys[s], 0, 0)
-        gq_ref[s] = (grad_queries * scaling).astype(BF)
+        grad_scores_ref[s] = grad_scores.reshape(GROUP * SRC, TGT)
         grad_keys = [
             (dot(grad_scores[h], head(q, h), 1, 0) * scaling).astype(BF) for h in range(GROUP)
         ]
@@ -210,8 +229,19 @@
                 gkv_ref[p, slot, start : start + HEAD] = jnp.where(swapped, low, high)
 
 
-def partial_kernel(distances, place_ref, grads_ref, own_ref, other_ref, *refs):
-    outs, grads = refs[:-1], refs[-1]
+def outputs_kernel(
+    place_ref, lens_ref, attention_ref, grad_scores_ref, kv_ref, ctx_ref, gq_ref, keys, values
+):
+    scaling = HEAD ** (-0.5)
+    lay_out(place_ref, kv_ref, keys, values)
+    for s in range(2):
+        context = dot(attention_ref[s], values[s], 0, 0)
+        ctx_ref[s] = jnp.where(valid_rows(lens_ref, s), context, 0.0).astype(BF)
+        gq_ref[s] = (dot(grad_scores_ref[s], keys[s], 0, 0) * scaling).astype(BF)
+
+
+def partial_kernel(distances, place_ref, grads_ref, *refs):
+    weights, outs, grads = refs[:4], refs[4:-1], refs[-1]
     width = SIDE * ROWS
 
     @pl.when(pl.program_id(0) == 0)
@@ -221,8 +251,9 @@
                 start = (i * SIDE + second) * ROWS
                 grads[start : start + ROWS] = grads_ref[chip_at(place_ref, first, second)]
 
-    total = dot(grads[:, : 2 * HEAD], own_ref[...], 1, 1)
-    total += dot(grads[:, 2 * HEAD :], other_ref[...], 1, 1)
+    own, other = (jnp.concatenate([weights[i][...], weights[i + 1][...]], axis=1) for i in (0, 2))
+    total = dot(grads[:, : 2 * HEAD], own, 1, 1)
+    total += dot(grads[:, 2 * HEAD :], other, 1, 1)
     for i, out in enumerate(outs):
         out[...] = total[i * width : (i + 1) * width].astype(BF)
 
@@ -270,15 +301,7 @@
         numbers = jnp.where(lane == 0, lang_id[0], jnp.where(lane == 1, src_len[0], tgt_len[0]))
         sentence = jnp.concatenate([memory[0], numbers.astype(BF)], axis=1)
 
-    with jax.named_scope("weights_of_chip"):
-        key_own, value_own, _ = lax.optimization_barrier((key_weight[0], value_weight[0], sentence))
-        own_weight = jnp.concatenate([key_own, value_own], axis=1)
-        other_weight = exchange(own_weight)
-
-    with jax.named_scope("sentences_over_lang"):
-        late, other_weight = lax.optimization_barrier((sentence, other_weight))
-        column = [sentence] + [shift_lang(sentence, d) for d in FAR_FIRST[1:5]]
-        column += [shift_lang(late, d) for d in FAR_FIRST[5:]]
+        column = [sentence] + [shift_lang(sentence, d) for d in FAR_FIRST[1:]]
 
     with jax.named_scope("route"):
         routed, rank, lens = pl.pallas_call(
@@ -291,7 +314,13 @@
             in_specs=[SMEM] + [VMEM] * PLANES,
             out_specs=(VMEM,) * 3,
             compiler_params=params(16),
-        )(place, *column)
+        )(place, *[column[FAR_FIRST.index(d)] for d in NEAR_FIRST])
+
+    with jax.named_scope("weights_of_chip"):
+        key_own, value_own, routed = lax.optimization_barrier(
+            (key_weight[0], value_weight[0], routed)
+        )
+        weights = (key_own, value_own, exchange(key_own), exchange(value_own))
 
     with jax.named_scope("gather_rows"):
         line = pl.pallas_call(
@@ -305,19 +334,32 @@
         blocks = [line] + [shift_plane(line, 1, d) for d in LINE[1:]]
 
     with jax.named_scope("project"):
+        count = SIDE // 2
+        scratch = [
+            pltpu.VMEM((SIDE, count * SIDE * ROWS, WIDTH // SIDE), BF),
+            pltpu.VMEM((SIDE, 2, WIDTH // SIDE, 2 * HEAD), BF),
+            pltpu.VMEM((count * SIDE * ROWS, 4 * HEAD), F32),
+            pltpu.SemaphoreType.DMA((SIDE, 4 + count)),
+        ]
+        block_at = dict(zip(LINE, blocks))
+        early = pl.pallas_call(
+            functools.partial(project_kernel, EARLY),
+            out_shape=jax.ShapeDtypeStruct((count * SIDE * ROWS, 4 * HEAD), BF),
+            in_specs=[SMEM] + [ANY] * (count + 4),
+            out_specs=VMEM,
+            scratch_shapes=scratch,
+            compiler_params=params(24),
+            cost_estimate=cost(count * SIDE * ROWS * WIDTH * 4 * HEAD, 6),
+        )(place, *[block_at[d] for d in EARLY], *weights)
         projected = pl.pallas_call(
-            project_kernel,
+            functools.partial(project_rest_kernel, LATE),
             out_shape=jax.ShapeDtypeStruct((CHIPS, ROWS, 4 * HEAD), BF),
-            in_specs=[SMEM] + [ANY] * (SIDE + 2),
+            in_specs=[SMEM, VMEM] + [ANY] * (count + 4),
             out_specs=VMEM,
-            scratch_shapes=[
-                pltpu.VMEM((SIDE, CHIPS * ROWS, WIDTH // SIDE), BF),
-                pltpu.VMEM((SIDE, 2, WIDTH // SIDE, 2 * HEAD), BF),
-                pltpu.VMEM((CHIPS * ROWS, 4 * HEAD), F32),
-                pltpu.SemaphoreType.DMA((SIDE, 2 + SIDE)),
-            ],
-            compiler_params=params(40),
-        )(place, *blocks, own_weight, other_weight)
+            scratch_shapes=scratch + [pltpu.VMEM((count * SIDE * ROWS, 4 * HEAD), BF)],
+            compiler_params=params(24),
+            cost_estimate=cost(count * SIDE * ROWS * WIDTH * 4 * HEAD, 6),
+        )(place, early, *[block_at[d] for d in LATE], *weights)
 
     with jax.named_scope("rows_to_slots"):
         slot_rows = lax.all_to_all(projected, PLANE, 0, 0, tiled=True)
@@ -326,25 +368,34 @@
         groups = WIDTH // (GROUP * HEAD)
         wide = pl.BlockSpec((2, TGT, GROUP * HEAD), lambda g: (0, 0, g))
         narrow = pl.BlockSpec((GROUP // 2, ROWS, 4 * HEAD), lambda g: (g, 0, 0))
-        context, grad_queries, slot_grads = pl.pallas_call(
+        tall = pl.BlockSpec((2, GROUP * SRC, TGT), lambda g: (0, g, 0))
+        diagonal = [pltpu.VMEM((2, GROUP * SRC, GROUP * HEAD), BF)] * 2
+        slot_grads, attention, grad_scores = pl.pallas_call(
             attend_kernel,
             grid=(groups,),
-            out_shape=(
-                jax.ShapeDtypeStruct((2, TGT, WIDTH), BF),
-                jax.ShapeDtypeStruct((2, TGT, WIDTH), BF),
-                jax.ShapeDtypeStruct((CHIPS, ROWS, 4 * HEAD), BF),
-            ),
+            out_shape=(jax.ShapeDtypeStruct((CHIPS, ROWS, 4 * HEAD), BF),)
+            + (jax.ShapeDtypeStruct((2, groups * GROUP * SRC, TGT), BF),) * 2,
             in_specs=[SMEM, VMEM, wide, wide, narrow],
-            out_specs=(wide, wide, narrow),
-            scratch_shapes=[
-                pltpu.VMEM((2, GROUP * SRC, GROUP * HEAD), BF),
-                pltpu.VMEM((2, GROUP * SRC, GROUP * HEAD), BF),
-            ],
+            out_specs=(narrow, tall, tall),
+            scratch_shapes=diagonal,
             compiler_params=params(58),
+            cost_estimate=cost(1 << 29, 6),
         )(place, lens, queries[0], grad_context[0], slot_rows)
 
     with jax.named_scope("grads_to_heads"):
         head_grads = lax.all_to_all(slot_grads, PLANE, 0, 0, tiled=True)
+
+    with jax.named_scope("attend"):
+        context, grad_queries = pl.pallas_call(
+            outputs_kernel,
+            grid=(groups,),
+            out_shape=(jax.ShapeDtypeStruct((2, TGT, WIDTH), BF),) * 2,
+            in_specs=[SMEM, VMEM, tall, tall, narrow],
+            out_specs=(wide, wide),
+            scratch_shapes=diagonal,
+            compiler_params=params(32),
+            cost_estimate=cost(1 << 30, 16),
+        )(place, lens, attention, grad_scores, slot_rows)
 
     with jax.named_scope("sum_rows"):
         tile = WIDTH // SIDE
@@ -355,14 +406,17 @@
                 functools.partial(partial_kernel, distances),
                 grid=(WIDTH // tile,),
                 out_shape=(jax.ShapeDtypeStruct((SIDE * ROWS, WIDTH), BF),) * count,
-                in_specs=[SMEM, VMEM] + [pl.BlockSpec((tile, 2 * HEAD), lambda t: (t, 0))] * 2,
+                in_specs=[SMEM, VMEM] + [pl.BlockSpec((tile, HEAD), lambda t: (t, 0))] * 4,
                 out_specs=(pl.BlockSpec((SIDE * ROWS, tile), lambda t: (0, t)),) * count,
                 scratch_shapes=[pltpu.VMEM((count * SIDE * ROWS, 4 * HEAD), BF)],
                 compiler_params=params(24),
                 cost_estimate=cost(count * SIDE * ROWS * WIDTH * 4 * HEAD, 7),
-            )(place, head_grads, own_weight, other_weight)
+            )(place, head_grads, *weights)
             terms.update(zip(distances, found))
         arrived = [terms[0]] + [shift_plane(terms[d], 0, -d) for d in LINE[1:]]
+        arrived[1], context, grad_queries = lax.optimization_barrier(
+            (arrived[1], context, grad_queries)
+        )
         line = sum(term.astype(F32) for term in arrived).astype(BF)
 
     with jax.named_scope("weight_grads"):
@@ -388,6 +442,7 @@
     with jax.named_scope("sum_rows"):
         pieces = {d: line[d * ROWS : (d + 1) * ROWS] for d in LINE}
         arrived = [pieces[0]] + [shift_plane(pieces[d], 1, -d) for d in LINE[1:]]
+        arrived[1], weight_grads = lax.optimization_barrier((arrived[1], weight_grads))
         summed = sum(term.astype(F32) for term in arrived).astype(BF)
 
     with jax.named_scope("sentences_back"):
@@ -398,8 +453,6 @@
             out_specs=(VMEM,) * PLANES,
             compiler_params=params(16),
         )(rank, summed)
-        late, weight_grads = lax.optimization_barrier((sends[5:], weight_grads))
-        sends = [*sends[:5], *late]
         candidates = [sends[0]] + [shift_lang(sends[i], -FAR_FIRST[i]) for i in range(1, PLANES)]
         grad_memory = pl.pallas_call(
             pick_kernel,

time: 195 us -> 186 us (0.954)
  starting transfers between devices: 60.4 us -> 54.4 us
  local copies, waits for them, and re-layouts: 3.75 us -> 0.21 us
  waiting for transfers between devices: 68.9 us -> 66.2 us
  Pallas kernels: 26.8 us -> 29.4 us
    pallas_call x1 -> x3, Pallas kernels: 3.86 us -> 10 us  [the longest x1 3.89 us: local(): pl.pallas_call(outputs_kernel, grid=(groups,), out_shape=(jax.ShapeDtypeS...]
    ppermute x14, starting transfers between devices: 42.2 us -> 37.1 us  [shift_lang(): return lax.ppermute(value, ('lang', 'core'), pairs)]
    ppermute x12, waiting for transfers between devices: 56.1 us -> 51.6 us  [shift_plane(): return lax.ppermute(value, ('y', 'x', 'core'), pairs)]
    pallas_call x1, Pallas kernels: 10.2 us -> 6.66 us  [local(): pl.pallas_call(attend_kernel, grid=(groups,), out_shape=(jax.ShapeDtypeSt...]
    unnamed x25 -> x30, local copies, waits for them, and re-layouts: 3.37 us -> 0.07 us
  transfers between devices with their start and end apart: 28 -> 29, of which waited for: 15 -> 17; matrix products, arithmetic and copies ran while one was open for 1% -> 1% of each run, Pallas kernels for 4% -> 8%
where the time goes in v2:
time: 186 us; the launch traced here: 185 us
  waiting for transfers between devices  66.2 us (36%)
  starting transfers between devices  54.4 us (29%)
  Pallas kernels  29.4 us (16%)
  blocking collectives  28.1 us (15%)
  other arithmetic  3.59 us (2%)
  between operations  3.02 us (2%)
    ppermute x12, waiting for transfers between devices, shift_plane(): return lax.ppermute(value, ('y', 'x', 'core'), pairs)  51.6 us
    ppermute x14, starting transfers between devices, shift_lang(): return lax.ppermute(value, ('lang', 'core'), pairs)  37.1 us
    ppermute x12, starting transfers between devices, shift_plane(): return lax.ppermute(value, ('y', 'x', 'core'), pairs)  16.7 us
    ppermute x14, waiting for transfers between devices, shift_lang(): return lax.ppermute(value, ('lang', 'core'), pairs)  14.5 us
    all_to_all x1, blocking collectives, local(): slot_rows = lax.all_to_all(projected, PLANE, 0, 0, tiled=True)  14.4 us
    all_to_all x1, blocking collectives, local(): head_grads = lax.all_to_all(slot_grads, PLANE, 0, 0, tiled=True)  13.7 us
    pallas_call x1, Pallas kernels, local(): pl.pallas_call(attend_kernel, grid=(groups,), out_shape=(jax.ShapeDtypeSt...  6.66 us
    pallas_call x2, Pallas kernels, local(): pl.pallas_call(functools.partial(partial_kernel, distances), grid=(WIDTH...  5.38 us
  transfers between devices with their start and end apart: 29, of which 17 were waited for; matrix products, arithmetic and copies ran while one was open for 1% of the time, Pallas kernels for 8%

profile of v2, /device:TPU:32, one launch (start us, length us, event | category | flops | bytes accessed | tf_op | source)
XLA Modules:
  0.0 185.0 jit_solution(14208499079331176423)
XLA Ops:
  2.8 0.9 pad_maximum_fusion.refs_0_
  3.7 6.4 %collective-permute-start.6 = (bf16[16,4224]{1,0:T(8,128)(2,1)S(1)}, bf16[16,4224]{1,0:T(8,128)(2,1)S(1)}, u32[]{:S(2)}, u32[]{:S(2)}) collective-permute-start(bf16[16,4224]{1,0:T(8,128)(2,1)S(1)} %pad_maximum_fusion.refs_0_), channel_id=1, source_target_pairs={{0,128},{1,129},{32,160},{33,161},{64,192},{65,193},{96,224},{97,2... | collective-permute-start | bytes 405512 | tf_op jit(solution)/shard_map/sentences_over_lang/ppermute | solution.py:50
  10.1 5.0 %collective-permute-start.4 = (bf16[16,4224]{1,0:T(8,128)(2,1)S(1)}, bf16[16,4224]{1,0:T(8,128)(2,1)S(1)}, u32[]{:S(2)}, u32[]{:S(2)}) collective-permute-start(bf16[16,4224]{1,0:T(8,128)(2,1)S(1)} %pad_maximum_fusion.refs_0_), channel_id=1, source_target_pairs={{0,160},{1,97},{32,192},{33,129},{64,224},{65,161},{96,0},{97,193}... | collective-permute-start | bytes 405512 | tf_op jit(solution)/shard_map/sentences_over_lang/ppermute | solution.py:50
  15.4 3.9 %collective-permute-start.2 = (bf16[16,4224]{1,0:T(8,128)(2,1)S(1)}, bf16[16,4224]{1,0:T(8,128)(2,1)S(1)}, u32[]{:S(2)}, u32[]{:S(2)}) collective-permute-start(bf16[16,4224]{1,0:T(8,128)(2,1)S(1)} %pad_maximum_fusion.refs_0_), channel_id=1, source_target_pairs={{0,192},{1,65},{32,224},{33,97},{64,0},{65,129},{96,32},{97,161},{... | collective-permute-start | bytes 405512 | tf_op jit(solution)/shard_map/sentences_over_lang/ppermute | solution.py:50
  19.2 2.4 %collective-permute-start.1 = (bf16[16,4224]{1,0:T(8,128)(2,1)S(1)}, bf16[16,4224]{1,0:T(8,128)(2,1)S(1)}, u32[]{:S(2)}, u32[]{:S(2)}) collective-permute-start(bf16[16,4224]{1,0:T(8,128)(2,1)S(1)} %pad_maximum_fusion.refs_0_), channel_id=1, source_target_pairs={{0,32},{1,225},{32,64},{33,1},{64,96},{65,33},{96,128},{97,65},{12... | collective-permute-start | bytes 405512 | tf_op jit(solution)/shard_map/sentences_over_lang/ppermute | solution.py:50
  21.7 3.9 %collective-permute-done.5.refs_6_ = bf16[16,4224]{1,0:T(8,128)(2,1)S(1)} collective-permute-done((bf16[16,4224]{1,0:T(8,128)(2,1)S(1)}, bf16[16,4224]{1,0:T(8,128)(2,1)S(1)}, u32[]{:S(2)}, u32[]{:S(2)}) %collective-permute-start.5) | collective-permute-done | bytes 135200 | tf_op jit(solution)/shard_map/sentences_over_lang/ppermute | solution.py:50
  25.5 4.9 %collective-permute-start = (bf16[16,4224]{1,0:T(8,128)(2,1)S(1)}, bf16[16,4224]{1,0:T(8,128)(2,1)S(1)}, u32[]{:S(2)}, u32[]{:S(2)}) collective-permute-start(bf16[16,4224]{1,0:T(8,128)(2,1)S(1)} %pad_maximum_fusion.refs_0_), channel_id=1, source_target_pairs={{0,224},{1,33},{32,0},{33,65},{64,32},{65,97},{96,64},{97,129},{12... | collective-permute-start | bytes 405512 | tf_op jit(solution)/shard_map/sentences_over_lang/ppermute | solution.py:50
  31.1 2.9 %collective-permute-done.1.refs_2_ = bf16[16,4224]{1,0:T(8,128)(2,1)S(1)} collective-permute-done((bf16[16,4224]{1,0:T(8,128)(2,1)S(1)}, bf16[16,4224]{1,0:T(8,128)(2,1)S(1)}, u32[]{:S(2)}, u32[]{:S(2)}) %collective-permute-start.1) | collective-permute-done | bytes 135200 | tf_op jit(solution)/shard_map/sentences_over_lang/ppermute | solution.py:50
  34.1 0.8 route.1
  34.9 2.8 %collective-permute-start.9 = (bf16[32,4096]{1,0:T(8,128)(2,1)S(1)}, bf16[32,4096]{1,0:T(8,128)(2,1)S(1)}, u32[]{:S(2)}, u32[]{:S(2)}) collective-permute-start(bf16[32,4096]{1,0:T(8,128)(2,1)S(1)} %get-tuple-element.39.refs_0_), channel_id=1, source_target_pairs={{0,6},{1,25},{2,0},{3,27},{4,2},{5,29},{6,4},{7,31},{8,14},{9,1},{... | collective-permute-start | bytes 786440 | tf_op jit(solution)/shard_map/gather_rows/ppermute | solution.py:62
  37.7 2.3 %collective-permute-start.7 = (bf16[32,4096]{1,0:T(8,128)(2,1)S(1)}, bf16[32,4096]{1,0:T(8,128)(2,1)S(1)}, u32[]{:S(2)}, u32[]{:S(2)}) collective-permute-start(bf16[32,4096]{1,0:T(8,128)(2,1)S(1)} %get-tuple-element.39.refs_0_), channel_id=1, source_target_pairs={{0,4},{1,17},{2,6},{3,19},{4,0},{5,21},{6,2},{7,23},{8,12},{9,25},... | collective-permute-start | bytes 786440 | tf_op jit(solution)/shard_map/gather_rows/ppermute | solution.py:62
  40.5 1.1 collective-permute-done.9.refs_3_
  41.6 6.5 %collective-permute-done.8.refs_2_ = bf16[32,4096]{1,0:T(8,128)(2,1)S(1)} collective-permute-done((bf16[32,4096]{1,0:T(8,128)(2,1)S(1)}, bf16[32,4096]{1,0:T(8,128)(2,1)S(1)}, u32[]{:S(2)}, u32[]{:S(2)}) %collective-permute-start.8) | collective-permute-done | bytes 262176 | tf_op jit(solution)/shard_map/gather_rows/ppermute | solution.py:62
  48.3 3.1 %collective-permute-start.10 = (bf16[128,4096]{1,0:T(8,128)(2,1)S(1)}, bf16[128,4096]{1,0:T(8,128)(2,1)S(1)}, u32[]{:S(2)}, u32[]{:S(2)}) collective-permute-start(bf16[128,4096]{1,0:T(8,128)(2,1)S(1)} %gather_rows.1.refs_0_), channel_id=1, source_target_pairs={{0,24},{1,7},{2,26},{3,1},{4,28},{5,3},{6,30},{7,5},{8,0},{9,15},{... | collective-permute-start | bytes 3145736 | tf_op jit(solution)/shard_map/gather_rows/ppermute | solution.py:62
  51.4 0.6 collective-permute-start.14
  52.0 1.0 collective-permute-start.13
  53.0 21.9 %collective-permute-done.10.refs_1_.refs_3_ = bf16[128,4096]{1,0:T(8,128)(2,1)S(1)} collective-permute-done((bf16[128,4096]{1,0:T(8,128)(2,1)S(1)}, bf16[128,4096]{1,0:T(8,128)(2,1)S(1)}, u32[]{:S(2)}, u32[]{:S(2)}) %collective-permute-start.10) | collective-permute-done | bytes 1048608 | tf_op jit(solution)/shard_map/gather_rows/ppermute | solution.py:62
  74.9 3.1 %project.2.early_ref = bf16[256,512]{1,0:T(8,128)(2,1)S(1)} custom-call(s32[5]{0:T(128)S(1)} %stack.23.place_ref, bf16[128,4096]{1,0:T(8,128)(2,1)S(1)} %gather_rows.1.refs_0_, bf16[128,4096]{1,0:T(8,128)(2,1)S(1)} %collective-permute-done.10.refs_1_.refs_3_, bf16[4096,128]{1,0:T(8,128)(2,1)S(1)} %bitcast.24, bf16[4096,128]{1,0:T(8,128)(2,1)S(1)} %bitcast.29, ...), custom_call_target="tpu_custom_call" | custom-call | flops 1073741824 | bytes 6291456 | tf_op jit(solution)/shard_map/project/pallas_call | solution.py:345
  78.0 0.9 collective-permute-done.13.refs_0_.refs_2_
  78.9 3.1 %project.3 = bf16[16,32,512]{2,1,0:T(8,128)(2,1)S(1)} custom-call(s32[5]{0:T(128)S(1)} %stack.23.place_ref, bf16[256,512]{1,0:T(8,128)(2,1)S(1)} %project.2.early_ref, bf16[128,4096]{1,0:T(8,128)(2,1)S(1)} %collective-permute-done.13.refs_0_.refs_2_, bf16[128,4096]{1,0:T(8,128)(2,1)S(1)} %collective-permute-done.14.refs_1_, bf16[4096,128]{1,0:T(8,128)(2,1)S(1)} %bitcast.25, ...), custom_call_target="tpu_custom_call" | custom-call | flops 1073741824 | bytes 6291456 | tf_op jit(solution)/shard_map/project/pallas_call | solution.py:354
  82.0 14.4 %all_to_all.10.kv_ref = bf16[16,32,512]{2,1,0:T(8,128)(2,1)} all-to-all(bf16[16,32,512]{2,1,0:T(8,128)(2,1)S(1)} %project.3), channel_id=1, replica_groups=mesh['lang'=8,'y'=4,'x'=4,'core'=2] {'y','x'}, dimensions={0} | all-to-all | bytes 1048576 | tf_op jit(solution)/shard_map/rows_to_slots/all_to_all | solution.py:365
  96.4 6.7 %attend.2 = (bf16[16,32,512]{2,1,0:T(8,128)(2,1)}, bf16[2,512,128]{2,1,0:T(8,128)(2,1)}, bf16[2,512,128]{2,1,0:T(8,128)(2,1)}) custom-call(s32[5]{0:T(128)} %copy-done.9, f32[4,8,128]{2,1,0:T(8,128)} %copy-done.11, bf16[2,128,4096]{2,1,0:T(8,128)(2,1)} %bitcast.33, bf16[2,128,4096]{2,1,0:T(8,128)(2,1)} %bitcast.34, bf16[16,32,512]{2,1,0:T(8,128)(2,1)} %all_to_all.10.kv_ref), custom_call_target="tpu_custom_call" | custom-call | flops 1073741824 | bytes 6291456 | tf_op jit(solution)/shard_map/attend/pallas_call | solution.py:373
  103.1 13.7 %all_to_all.11.grads_ref = bf16[16,32,512]{2,1,0:T(8,128)(2,1)S(1)} all-to-all(bf16[16,32,512]{2,1,0:T(8,128)(2,1)} %get-tuple-element.42), channel_id=1, replica_groups=mesh['lang'=8,'y'=4,'x'=4,'core'=2] {'y','x'}, dimensions={0} | all-to-all | bytes 1048576 | tf_op jit(solution)/shard_map/grads_to_heads/all_to_all | solution.py:386
  116.8 2.7 %sum_rows.2 = (bf16[128,4096]{1,0:T(8,128)(2,1)S(1)}, bf16[128,4096]{1,0:T(8,128)(2,1)S(1)}) custom-call(s32[5]{0:T(128)S(1)} %copy-done.10, bf16[16,32,512]{2,1,0:T(8,128)(2,1)S(1)} %all_to_all.11.grads_ref, bf16[4096,128]{1,0:T(8,128)(2,1)S(1)} %bitcast.26, bf16[4096,128]{1,0:T(8,128)(2,1)S(1)} %bitcast.31, ...), custom_call_target="tpu_custom_call" | custom-call | flops 1073741824 | bytes 7340032 | tf_op jit(solution)/shard_map/sum_rows/pallas_call | solution.py:405
  119.5 0.9 collective-permute-start.15
  120.3 2.5 %collective-permute-start.16 = (bf16[128,4096]{1,0:T(8,128)(2,1)S(1)}, bf16[128,4096]{1,0:T(8,128)(2,1)S(1)}, u32[]{:S(2)}, u32[]{:S(2)}) collective-permute-start(bf16[128,4096]{1,0:T(8,128)(2,1)S(1)} %get-tuple-element.53), channel_id=1, source_target_pairs={{0,6},{1,25},{2,0},{3,27},{4,2},{5,29},{6,4},{7,31},{8,14},{9,1},{... | collective-permute-start | bytes 3145736 | tf_op jit(solution)/shard_map/sum_rows/ppermute | solution.py:62
  122.8 2.7 %sum_rows.3 = (bf16[128,4096]{1,0:T(8,128)(2,1)S(1)}, bf16[128,4096]{1,0:T(8,128)(2,1)S(1)}) custom-call(s32[5]{0:T(128)S(1)} %copy-done.10, bf16[16,32,512]{2,1,0:T(8,128)(2,1)S(1)} %all_to_all.11.grads_ref, bf16[4096,128]{1,0:T(8,128)(2,1)S(1)} %bitcast.27, bf16[4096,128]{1,0:T(8,128)(2,1)S(1)} %bitcast.32, ...), custom_call_target="tpu_custom_call" | custom-call | flops 1073741824 | bytes 7340032 | tf_op jit(solution)/shard_map/sum_rows/pallas_call | solution.py:405
  125.7 5.0 %weight_grads.1 = (bf16[4096,256]{1,0:T(8,128)(2,1)S(1)}, bf16[4096,256]{1,0:T(8,128)(2,1)S(1)}) custom-call(s32[5]{0:T(128)S(1)} %copy-done.10, bf16[16,32,512]{2,1,0:T(8,128)(2,1)S(1)} %all_to_all.11.grads_ref, bf16[128,4096]{1,0:T(8,128)(2,1)S(1)} %gather_rows.1.refs_0_, bf16[128,4096]{1,0:T(8,128)(2,1)S(1)} %copy-done.4, ...), custom_call_target="tpu_custom_call" | custom-call | flops 2147483648 | bytes 16777216 | tf_op jit(solution)/shard_map/weight_grads/pallas_call | solution.py:425
  130.8 3.9 %attend.3 = (bf16[2,128,4096]{2,1,0:T(8,128)(2,1)}, bf16[2,128,4096]{2,1,0:T(8,128)(2,1)}) custom-call(s32[5]{0:T(128)S(1)} %copy-done.10, f32[4,8,128]{2,1,0:T(8,128)S(1)} %copy-done.12, bf16[2,512,128]{2,1,0:T(8,128)(2,1)S(1)} %copy-done.13, bf16[2,512,128]{2,1,0:T(8,128)(2,1)S(1)} %copy-done.14, bf16[16,32,512]{2,1,0:T(8,128)(2,1)S(1)} %copy-done.2), custom_call_target="tpu_custom_call" | custom-call | flops 2147483648 | bytes 16777216 | tf_op jit(solution)/shard_map/attend/pallas_call | solution.py:389
  134.7 1.2 collective-permute-done.15
  136.0 9.7 %collective-permute-done.16 = bf16[128,4096]{1,0:T(8,128)(2,1)S(1)} collective-permute-done((bf16[128,4096]{1,0:T(8,128)(2,1)S(1)}, bf16[128,4096]{1,0:T(8,128)(2,1)S(1)}, u32[]{:S(2)}, u32[]{:S(2)}) %collective-permute-start.16) | collective-permute-done | bytes 1048608 | tf_op jit(solution)/shard_map/sum_rows/ppermute | solution.py:62
  145.7 5.0 %collective-permute-done.17 = bf16[128,4096]{1,0:T(8,128)(2,1)S(1)} collective-permute-done((bf16[128,4096]{1,0:T(8,128)(2,1)S(1)}, bf16[128,4096]{1,0:T(8,128)(2,1)S(1)}, u32[]{:S(2)}, u32[]{:S(2)}) %collective-permute-start.17) | collective-permute-done | bytes 1048608 | tf_op jit(solution)/shard_map/sum_rows/ppermute | solution.py:62
  150.7 0.7 add_convert_fusion.2
  151.7 1.2 collective-permute-start.21
  152.9 2.0 %collective-permute-start.20 = (bf16[32,4096]{1,0:T(8,128)(2,1)S(1)}, bf16[32,4096]{1,0:T(8,128)(2,1)S(1)}, u32[]{:S(2)}, u32[]{:S(2)}) collective-permute-start(bf16[32,4096]{1,0:T(8,128)(2,1)S(1)} %get-tuple-element.73), channel_id=1, source_target_pairs={{0,24},{1,7},{2,26},{3,1},{4,28},{5,3},{6,30},{7,5},{8,0},{9,15},{... | collective-permute-start | bytes 786440 | tf_op jit(solution)/shard_map/sum_rows/ppermute | solution.py:62
  154.9 1.9 %add_convert_fusion = (bf16[4096,128]{1,0:T(8,128)(2,1)}, bf16[4096,128]{1,0:T(8,128)(2,1)}) fusion(bf16[4096,256]{1,0:T(8,128)(2,1)S(1)} %collective-permute-done.19, bf16[4096,256]{1,0:T(8,128)(2,1)S(1)} %get-tuple-element.56), kind=kLoop, calls=%fused_computation | loop fusion | flops 4194304 | bytes 6291456 | tf_op jit(solution)/shard_map/weight_grads/convert_element_type | solution.py:438
  156.8 2.7 %collective-permute-done.18 = bf16[32,4096]{1,0:T(8,128)(2,1)S(1)} collective-permute-done((bf16[32,4096]{1,0:T(8,128)(2,1)S(1)}, bf16[32,4096]{1,0:T(8,128)(2,1)S(1)}, u32[]{:S(2)}, u32[]{:S(2)}) %collective-permute-start.18) | collective-permute-done | bytes 262176 | tf_op jit(solution)/shard_map/sum_rows/ppermute | solution.py:62
  159.5 2.6 %collective-permute-done.21 = bf16[32,4096]{1,0:T(8,128)(2,1)S(1)} collective-permute-done((bf16[32,4096]{1,0:T(8,128)(2,1)S(1)}, bf16[32,4096]{1,0:T(8,128)(2,1)S(1)}, u32[]{:S(2)}, u32[]{:S(2)}) %collective-permute-start.21) | collective-permute-done | bytes 262176 | tf_op jit(solution)/shard_map/sum_rows/ppermute | solution.py:62
  162.3 3.1 %collective-permute-start.22 = (bf16[16,4096]{1,0:T(8,128)(2,1)S(1)}, bf16[16,4096]{1,0:T(8,128)(2,1)S(1)}, u32[]{:S(2)}, u32[]{:S(2)}) collective-permute-start(bf16[16,4096]{1,0:T(8,128)(2,1)S(1)} %get-tuple-element.60), channel_id=1, source_target_pairs={{0,128},{1,129},{32,160},{33,161},{64,192},{65,193},{96,224},{97,2... | collective-permute-start | bytes 393224 | tf_op jit(solution)/shard_map/sentences_back/ppermute | solution.py:50
  165.4 2.7 %collective-permute-start.23 = (bf16[16,4096]{1,0:T(8,128)(2,1)S(1)}, bf16[16,4096]{1,0:T(8,128)(2,1)S(1)}, u32[]{:S(2)}, u32[]{:S(2)}) collective-permute-start(bf16[16,4096]{1,0:T(8,128)(2,1)S(1)} %get-tuple-element.61), channel_id=1, source_target_pairs={{0,160},{1,97},{32,192},{33,129},{64,224},{65,161},{96,0},{97,193}... | collective-permute-start | bytes 393224 | tf_op jit(solution)/shard_map/sentences_back/ppermute | solution.py:50
  168.1 2.3 %collective-permute-start.24 = (bf16[16,4096]{1,0:T(8,128)(2,1)S(1)}, bf16[16,4096]{1,0:T(8,128)(2,1)S(1)}, u32[]{:S(2)}, u32[]{:S(2)}) collective-permute-start(bf16[16,4096]{1,0:T(8,128)(2,1)S(1)} %get-tuple-element.62), channel_id=1, source_target_pairs={{0,96},{1,161},{32,128},{33,193},{64,160},{65,225},{96,192},{97,1}... | collective-permute-start | bytes 393224 | tf_op jit(solution)/shard_map/sentences_back/ppermute | solution.py:50
  170.4 2.5 %collective-permute-start.25 = (bf16[16,4096]{1,0:T(8,128)(2,1)S(1)}, bf16[16,4096]{1,0:T(8,128)(2,1)S(1)}, u32[]{:S(2)}, u32[]{:S(2)}) collective-permute-start(bf16[16,4096]{1,0:T(8,128)(2,1)S(1)} %get-tuple-element.63), channel_id=1, source_target_pairs={{0,192},{1,65},{32,224},{33,97},{64,0},{65,129},{96,32},{97,161},{... | collective-permute-start | bytes 393224 | tf_op jit(solution)/shard_map/sentences_back/ppermute | solution.py:50
  173.6 1.4 collective-permute-done.22.refs_1_
  175.5 3.2 %collective-permute-done.23.refs_2_ = bf16[16,4096]{1,0:T(8,128)(2,1)S(1)} collective-permute-done((bf16[16,4096]{1,0:T(8,128)(2,1)S(1)}, bf16[16,4096]{1,0:T(8,128)(2,1)S(1)}, u32[]{:S(2)}, u32[]{:S(2)}) %collective-permute-start.23) | collective-permute-done | bytes 131104 | tf_op jit(solution)/shard_map/sentences_back/ppermute | solution.py:50
  178.7 2.5 %collective-permute-start.28 = (bf16[16,4096]{1,0:T(8,128)(2,1)S(1)}, bf16[16,4096]{1,0:T(8,128)(2,1)S(1)}, u32[]{:S(2)}, u32[]{:S(2)}) collective-permute-start(bf16[16,4096]{1,0:T(8,128)(2,1)S(1)} %get-tuple-element.66), channel_id=1, source_target_pairs={{0,32},{1,225},{32,64},{33,1},{64,96},{65,33},{96,128},{97,65},{12... | collective-permute-start | bytes 393224 | tf_op jit(solution)/shard_map/sentences_back/ppermute | solution.py:50
  181.2 0.9 collective-permute-done.25.refs_4_
  182.1 1.6 collective-permute-done.28.refs_7_
  183.7 1.3 sentences_back.3
  (62 shorter events, 3.7 us)
Async XLA Ops:
  0.6 74.3 %copy-start.1 = (bf16[1,4096,128]{2,1,0:T(8,128)(2,1)S(1)}, bf16[1,4096,128]{2,1,0:T(8,128)(2,1)}, u32[]{:S(2)}) copy-start(bf16[1,4096,128]{2,1,0:T(8,128)(2,1)} %param.14) | copy-start | bytes 3145732
  0.6 74.3 %copy-start = (bf16[1,4096,128]{2,1,0:T(8,128)(2,1)S(1)}, bf16[1,4096,128]{2,1,0:T(8,128)(2,1)}, u32[]{:S(2)}) copy-start(bf16[1,4096,128]{2,1,0:T(8,128)(2,1)} %param.13) | copy-start | bytes 3145732
  3.7 15.6 %collective-permute-start.6 = (bf16[16,4224]{1,0:T(8,128)(2,1)S(1)}, bf16[16,4224]{1,0:T(8,128)(2,1)S(1)}, u32[]{:S(2)}, u32[]{:S(2)}) collective-permute-start(bf16[16,4224]{1,0:T(8,128)(2,1)S(1)} %pad_maximum_fusion.refs_0_), channel_id=1, source_target_pairs={{0,128},{1,129},{32,160},{33,161},{64,192},{65,193},{96,224},{97,2... | collective-permute-start | bytes 405512 | tf_op jit(solution)/shard_map/sentences_over_lang/ppermute | solution.py:50
  10.1 15.5 %collective-permute-start.5 = (bf16[16,4224]{1,0:T(8,128)(2,1)S(1)}, bf16[16,4224]{1,0:T(8,128)(2,1)S(1)}, u32[]{:S(2)}, u32[]{:S(2)}) collective-permute-start(bf16[16,4224]{1,0:T(8,128)(2,1)S(1)} %pad_maximum_fusion.refs_0_), channel_id=1, source_target_pairs={{0,96},{1,161},{32,128},{33,193},{64,160},{65,225},{96,192},{97,1}... | collective-permute-start | bytes 405512 | tf_op jit(solution)/shard_map/sentences_over_lang/ppermute | solution.py:50
  10.1 20.4 %collective-permute-start.4 = (bf16[16,4224]{1,0:T(8,128)(2,1)S(1)}, bf16[16,4224]{1,0:T(8,128)(2,1)S(1)}, u32[]{:S(2)}, u32[]{:S(2)}) collective-permute-start(bf16[16,4224]{1,0:T(8,128)(2,1)S(1)} %pad_maximum_fusion.refs_0_), channel_id=1, source_target_pairs={{0,160},{1,97},{32,192},{33,129},{64,224},{65,161},{96,0},{97,193}... | collective-permute-start | bytes 405512 | tf_op jit(solution)/shard_map/sentences_over_lang/ppermute | solution.py:50
  15.1 15.8 %collective-permute-start.3 = (bf16[16,4224]{1,0:T(8,128)(2,1)S(1)}, bf16[16,4224]{1,0:T(8,128)(2,1)S(1)}, u32[]{:S(2)}, u32[]{:S(2)}) collective-permute-start(bf16[16,4224]{1,0:T(8,128)(2,1)S(1)} %pad_maximum_fusion.refs_0_), channel_id=1, source_target_pairs={{0,64},{1,193},{32,96},{33,225},{64,128},{65,1},{96,160},{97,33},{... | collective-permute-start | bytes 405512 | tf_op jit(solution)/shard_map/sentences_over_lang/ppermute | solution.py:50
  15.4 15.8 %collective-permute-start.2 = (bf16[16,4224]{1,0:T(8,128)(2,1)S(1)}, bf16[16,4224]{1,0:T(8,128)(2,1)S(1)}, u32[]{:S(2)}, u32[]{:S(2)}) collective-permute-start(bf16[16,4224]{1,0:T(8,128)(2,1)S(1)} %pad_maximum_fusion.refs_0_), channel_id=1, source_target_pairs={{0,192},{1,65},{32,224},{33,97},{64,0},{65,129},{96,32},{97,161},{... | collective-permute-start | bytes 405512 | tf_op jit(solution)/shard_map/sentences_over_lang/ppermute | solution.py:50
  19.2 14.8 %collective-permute-start.1 = (bf16[16,4224]{1,0:T(8,128)(2,1)S(1)}, bf16[16,4224]{1,0:T(8,128)(2,1)S(1)}, u32[]{:S(2)}, u32[]{:S(2)}) collective-permute-start(bf16[16,4224]{1,0:T(8,128)(2,1)S(1)} %pad_maximum_fusion.refs_0_), channel_id=1, source_target_pairs={{0,32},{1,225},{32,64},{33,1},{64,96},{65,33},{96,128},{97,65},{12... | collective-permute-start | bytes 405512 | tf_op jit(solution)/shard_map/sentences_over_lang/ppermute | solution.py:50
  25.5 8.5 %collective-permute-start = (bf16[16,4224]{1,0:T(8,128)(2,1)S(1)}, bf16[16,4224]{1,0:T(8,128)(2,1)S(1)}, u32[]{:S(2)}, u32[]{:S(2)}) collective-permute-start(bf16[16,4224]{1,0:T(8,128)(2,1)S(1)} %pad_maximum_fusion.refs_0_), channel_id=1, source_target_pairs={{0,224},{1,33},{32,0},{33,65},{64,32},{65,97},{96,64},{97,129},{12... | collective-permute-start | bytes 405512 | tf_op jit(solution)/shard_map/sentences_over_lang/ppermute | solution.py:50
  30.5 48.4 %copy-start.9 = (s32[5]{0:T(128)}, s32[5]{0:T(128)S(1)}, u32[]{:S(2)}) copy-start(s32[5]{0:T(128)S(1)} %stack.23.place_ref) | copy-start | bytes 64
  34.9 18.1 %copy-start.11 = (f32[4,8,128]{2,1,0:T(8,128)}, f32[4,8,128]{2,1,0:T(8,128)S(1)}, u32[]{:S(2)}) copy-start(f32[4,8,128]{2,1,0:T(8,128)S(1)} %get-tuple-element.37.lens_ref) | copy-start | bytes 49156
  34.9 6.7 %collective-permute-start.9 = (bf16[32,4096]{1,0:T(8,128)(2,1)S(1)}, bf16[32,4096]{1,0:T(8,128)(2,1)S(1)}, u32[]{:S(2)}, u32[]{:S(2)}) collective-permute-start(bf16[32,4096]{1,0:T(8,128)(2,1)S(1)} %get-tuple-element.39.refs_0_), channel_id=1, source_target_pairs={{0,6},{1,25},{2,0},{3,27},{4,2},{5,29},{6,4},{7,31},{8,14},{9,1},{... | collective-permute-start | bytes 786440 | tf_op jit(solution)/shard_map/gather_rows/ppermute | solution.py:62
  37.7 10.4 %collective-permute-start.8 = (bf16[32,4096]{1,0:T(8,128)(2,1)S(1)}, bf16[32,4096]{1,0:T(8,128)(2,1)S(1)}, u32[]{:S(2)}, u32[]{:S(2)}) collective-permute-start(bf16[32,4096]{1,0:T(8,128)(2,1)S(1)} %get-tuple-element.39.refs_0_), channel_id=1, source_target_pairs={{0,2},{1,9},{2,4},{3,11},{4,6},{5,13},{6,0},{7,15},{8,10},{9,17},{... | collective-permute-start | bytes 786440 | tf_op jit(solution)/shard_map/gather_rows/ppermute | solution.py:62
  37.7 10.4 %collective-permute-start.7 = (bf16[32,4096]{1,0:T(8,128)(2,1)S(1)}, bf16[32,4096]{1,0:T(8,128)(2,1)S(1)}, u32[]{:S(2)}, u32[]{:S(2)}) collective-permute-start(bf16[32,4096]{1,0:T(8,128)(2,1)S(1)} %get-tuple-element.39.refs_0_), channel_id=1, source_target_pairs={{0,4},{1,17},{2,6},{3,19},{4,0},{5,21},{6,2},{7,23},{8,12},{9,25},... | collective-permute-start | bytes 786440 | tf_op jit(solution)/shard_map/gather_rows/ppermute | solution.py:62
  40.0 12.9 %collective-permute-start.11 = (bf16[4096,128]{1,0:T(8,128)(2,1)}, bf16[4096,128]{1,0:T(8,128)(2,1)S(1)}, u32[]{:S(2)}, u32[]{:S(2)}) collective-permute-start(bf16[4096,128]{1,0:T(8,128)(2,1)} %bitcast.23), channel_id=1, source_target_pairs={{0,1},{1,0},{2,3},{3,2},{4,5},{5,4},{6,7},{7,6},{8,9},{9,8},{10,11... | collective-permute-start | bytes 3145736 | tf_op jit(solution)/shard_map/weights_of_chip/ppermute | solution.py:41
  40.0 12.9 %collective-permute-start.12 = (bf16[4096,128]{1,0:T(8,128)(2,1)}, bf16[4096,128]{1,0:T(8,128)(2,1)S(1)}, u32[]{:S(2)}, u32[]{:S(2)}) collective-permute-start(bf16[4096,128]{1,0:T(8,128)(2,1)} %bitcast.28), channel_id=1, source_target_pairs={{0,1},{1,0},{2,3},{3,2},{4,5},{5,4},{6,7},{7,6},{8,9},{9,8},{10,11... | collective-permute-start | bytes 3145736 | tf_op jit(solution)/shard_map/weights_of_chip/ppermute | solution.py:41
  48.3 26.6 %collective-permute-start.10 = (bf16[128,4096]{1,0:T(8,128)(2,1)S(1)}, bf16[128,4096]{1,0:T(8,128)(2,1)S(1)}, u32[]{:S(2)}, u32[]{:S(2)}) collective-permute-start(bf16[128,4096]{1,0:T(8,128)(2,1)S(1)} %gather_rows.1.refs_0_), channel_id=1, source_target_pairs={{0,24},{1,7},{2,26},{3,1},{4,28},{5,3},{6,30},{7,5},{8,0},{9,15},{... | collective-permute-start | bytes 3145736 | tf_op jit(solution)/shard_map/gather_rows/ppermute | solution.py:62
  51.4 26.7 %collective-permute-start.14 = (bf16[128,4096]{1,0:T(8,128)(2,1)S(1)}, bf16[128,4096]{1,0:T(8,128)(2,1)S(1)}, u32[]{:S(2)}, u32[]{:S(2)}) collective-permute-start(bf16[128,4096]{1,0:T(8,128)(2,1)S(1)} %gather_rows.1.refs_0_), channel_id=1, source_target_pairs={{0,16},{1,5},{2,18},{3,7},{4,20},{5,1},{6,22},{7,3},{8,24},{9,13},... | collective-permute-start | bytes 3145736 | tf_op jit(solution)/shard_map/gather_rows/ppermute | solution.py:62
  52.0 26.9 %collective-permute-start.13 = (bf16[128,4096]{1,0:T(8,128)(2,1)S(1)}, bf16[128,4096]{1,0:T(8,128)(2,1)S(1)}, u32[]{:S(2)}, u32[]{:S(2)}) collective-permute-start(bf16[128,4096]{1,0:T(8,128)(2,1)S(1)} %gather_rows.1.refs_0_), channel_id=1, source_target_pairs={{0,8},{1,3},{2,10},{3,5},{4,12},{5,7},{6,14},{7,1},{8,16},{9,11},{... | collective-permute-start | bytes 3145736 | tf_op jit(solution)/shard_map/gather_rows/ppermute | solution.py:62
  74.9 3.1 %copy-start.7 = (bf16[128,4096]{1,0:T(8,128)(2,1)}, bf16[128,4096]{1,0:T(8,128)(2,1)S(1)}, u32[]{:S(2)}) copy-start(bf16[128,4096]{1,0:T(8,128)(2,1)S(1)} %collective-permute-done.10.refs_1_.refs_3_) | copy-start | bytes 3145732
  78.0 4.0 %copy-start.3 = (bf16[128,4096]{1,0:T(8,128)(2,1)}, bf16[128,4096]{1,0:T(8,128)(2,1)S(1)}, u32[]{:S(2)}) copy-start(bf16[128,4096]{1,0:T(8,128)(2,1)S(1)} %collective-permute-done.14.refs_1_) | copy-start | bytes 3145732
  78.9 3.1 %copy-start.5 = (bf16[128,4096]{1,0:T(8,128)(2,1)}, bf16[128,4096]{1,0:T(8,128)(2,1)S(1)}, u32[]{:S(2)}) copy-start(bf16[128,4096]{1,0:T(8,128)(2,1)S(1)} %collective-permute-done.13.refs_0_.refs_2_) | copy-start | bytes 3145732
  96.4 20.3 %copy-start.10 = (s32[5]{0:T(128)S(1)}, s32[5]{0:T(128)}, u32[]{:S(2)}) copy-start(s32[5]{0:T(128)} %copy-done.9) | copy-start | bytes 64
  119.5 16.5 %collective-permute-start.15 = (bf16[128,4096]{1,0:T(8,128)(2,1)S(1)}, bf16[128,4096]{1,0:T(8,128)(2,1)S(1)}, u32[]{:S(2)}, u32[]{:S(2)}) collective-permute-start(bf16[128,4096]{1,0:T(8,128)(2,1)S(1)} %get-tuple-element.43), channel_id=1, source_target_pairs={{0,4},{1,17},{2,6},{3,19},{4,0},{5,21},{6,2},{7,23},{8,12},{9,25},... | collective-permute-start | bytes 3145736 | tf_op jit(solution)/shard_map/sum_rows/ppermute | solution.py:62
  120.3 5.3 %copy-start.4 = (bf16[128,4096]{1,0:T(8,128)(2,1)S(1)}, bf16[128,4096]{1,0:T(8,128)(2,1)}, u32[]{:S(2)}) copy-start(bf16[128,4096]{1,0:T(8,128)(2,1)} %copy-done.3) | copy-start | bytes 3145732
  120.3 5.3 %copy-start.6 = (bf16[128,4096]{1,0:T(8,128)(2,1)S(1)}, bf16[128,4096]{1,0:T(8,128)(2,1)}, u32[]{:S(2)}) copy-start(bf16[128,4096]{1,0:T(8,128)(2,1)} %copy-done.5) | copy-start | bytes 3145732
  120.3 5.3 %copy-start.8 = (bf16[128,4096]{1,0:T(8,128)(2,1)S(1)}, bf16[128,4096]{1,0:T(8,128)(2,1)}, u32[]{:S(2)}) copy-start(bf16[128,4096]{1,0:T(8,128)(2,1)} %copy-done.7) | copy-start | bytes 3145732
  120.3 25.4 %collective-permute-start.16 = (bf16[128,4096]{1,0:T(8,128)(2,1)S(1)}, bf16[128,4096]{1,0:T(8,128)(2,1)S(1)}, u32[]{:S(2)}, u32[]{:S(2)}) collective-permute-start(bf16[128,4096]{1,0:T(8,128)(2,1)S(1)} %get-tuple-element.53), channel_id=1, source_target_pairs={{0,6},{1,25},{2,0},{3,27},{4,2},{5,29},{6,4},{7,31},{8,14},{9,1},{... | collective-permute-start | bytes 3145736 | tf_op jit(solution)/shard_map/sum_rows/ppermute | solution.py:62
  125.5 25.2 %collective-permute-start.17 = (bf16[128,4096]{1,0:T(8,128)(2,1)S(1)}, bf16[128,4096]{1,0:T(8,128)(2,1)S(1)}, u32[]{:S(2)}, u32[]{:S(2)}) collective-permute-start(bf16[128,4096]{1,0:T(8,128)(2,1)S(1)} %get-tuple-element.54), channel_id=1, source_target_pairs={{0,2},{1,9},{2,4},{3,11},{4,6},{5,13},{6,0},{7,15},{8,10},{9,17},{... | collective-permute-start | bytes 3145736 | tf_op jit(solution)/shard_map/sum_rows/ppermute | solution.py:62
  125.6 5.2 %copy-start.2 = (bf16[16,32,512]{2,1,0:T(8,128)(2,1)S(1)}, bf16[16,32,512]{2,1,0:T(8,128)(2,1)}, u32[]{:S(2)}) copy-start(bf16[16,32,512]{2,1,0:T(8,128)(2,1)} %all_to_all.10.kv_ref) | copy-start | bytes 1572868
  125.6 5.2 %copy-start.12 = (f32[4,8,128]{2,1,0:T(8,128)S(1)}, f32[4,8,128]{2,1,0:T(8,128)}, u32[]{:S(2)}) copy-start(f32[4,8,128]{2,1,0:T(8,128)} %copy-done.11) | copy-start | bytes 49156
  125.6 5.2 %copy-start.13 = (bf16[2,512,128]{2,1,0:T(8,128)(2,1)S(1)}, bf16[2,512,128]{2,1,0:T(8,128)(2,1)}, u32[]{:S(2)}) copy-start(bf16[2,512,128]{2,1,0:T(8,128)(2,1)} %get-tuple-element.44.attention_ref) | copy-start | bytes 786436
  125.7 5.2 %copy-start.14 = (bf16[2,512,128]{2,1,0:T(8,128)(2,1)S(1)}, bf16[2,512,128]{2,1,0:T(8,128)(2,1)}, u32[]{:S(2)}) copy-start(bf16[2,512,128]{2,1,0:T(8,128)(2,1)} %get-tuple-element.45.grad_scores_ref) | copy-start | bytes 786436
  130.7 24.2 %collective-permute-start.19 = (bf16[4096,256]{1,0:T(8,128)(2,1)S(1)}, bf16[4096,256]{1,0:T(8,128)(2,1)S(1)}, u32[]{:S(2)}, u32[]{:S(2)}) collective-permute-start(bf16[4096,256]{1,0:T(8,128)(2,1)S(1)} %get-tuple-element.57), channel_id=1, source_target_pairs={{0,1},{1,0},{2,3},{3,2},{4,5},{5,4},{6,7},{7,6},{8,9},{9,8},{10,11... | collective-permute-start | bytes 6291464 | tf_op jit(solution)/shard_map/weight_grads/ppermute | solution.py:41
  151.4 8.1 %collective-permute-start.18 = (bf16[32,4096]{1,0:T(8,128)(2,1)S(1)}, bf16[32,4096]{1,0:T(8,128)(2,1)S(1)}, u32[]{:S(2)}, u32[]{:S(2)}) collective-permute-start(bf16[32,4096]{1,0:T(8,128)(2,1)S(1)} %get-tuple-element.71), channel_id=1, source_target_pairs={{0,16},{1,5},{2,18},{3,7},{4,20},{5,1},{6,22},{7,3},{8,24},{9,13},... | collective-permute-start | bytes 786440 | tf_op jit(solution)/shard_map/sum_rows/ppermute | solution.py:62
  151.7 10.4 %collective-permute-start.21 = (bf16[32,4096]{1,0:T(8,128)(2,1)S(1)}, bf16[32,4096]{1,0:T(8,128)(2,1)S(1)}, u32[]{:S(2)}, u32[]{:S(2)}) collective-permute-start(bf16[32,4096]{1,0:T(8,128)(2,1)S(1)} %get-tuple-element.72), channel_id=1, source_target_pairs={{0,8},{1,3},{2,10},{3,5},{4,12},{5,7},{6,14},{7,1},{8,16},{9,11},{... | collective-permute-start | bytes 786440 | tf_op jit(solution)/shard_map/sum_rows/ppermute | solution.py:62
  152.9 9.2 %collective-permute-start.20 = (bf16[32,4096]{1,0:T(8,128)(2,1)S(1)}, bf16[32,4096]{1,0:T(8,128)(2,1)S(1)}, u32[]{:S(2)}, u32[]{:S(2)}) collective-permute-start(bf16[32,4096]{1,0:T(8,128)(2,1)S(1)} %get-tuple-element.73), channel_id=1, source_target_pairs={{0,24},{1,7},{2,26},{3,1},{4,28},{5,3},{6,30},{7,5},{8,0},{9,15},{... | collective-permute-start | bytes 786440 | tf_op jit(solution)/shard_map/sum_rows/ppermute | solution.py:62
  162.3 12.6 %collective-permute-start.22 = (bf16[16,4096]{1,0:T(8,128)(2,1)S(1)}, bf16[16,4096]{1,0:T(8,128)(2,1)S(1)}, u32[]{:S(2)}, u32[]{:S(2)}) collective-permute-start(bf16[16,4096]{1,0:T(8,128)(2,1)S(1)} %get-tuple-element.60), channel_id=1, source_target_pairs={{0,128},{1,129},{32,160},{33,161},{64,192},{65,193},{96,224},{97,2... | collective-permute-start | bytes 393224 | tf_op jit(solution)/shard_map/sentences_back/ppermute | solution.py:50
  165.4 13.3 %collective-permute-start.23 = (bf16[16,4096]{1,0:T(8,128)(2,1)S(1)}, bf16[16,4096]{1,0:T(8,128)(2,1)S(1)}, u32[]{:S(2)}, u32[]{:S(2)}) collective-permute-start(bf16[16,4096]{1,0:T(8,128)(2,1)S(1)} %get-tuple-element.61), channel_id=1, source_target_pairs={{0,160},{1,97},{32,192},{33,129},{64,224},{65,161},{96,0},{97,193}... | collective-permute-start | bytes 393224 | tf_op jit(solution)/shard_map/sentences_back/ppermute | solution.py:50
  168.1 13.0 %collective-permute-start.24 = (bf16[16,4096]{1,0:T(8,128)(2,1)S(1)}, bf16[16,4096]{1,0:T(8,128)(2,1)S(1)}, u32[]{:S(2)}, u32[]{:S(2)}) collective-permute-start(bf16[16,4096]{1,0:T(8,128)(2,1)S(1)} %get-tuple-element.62), channel_id=1, source_target_pairs={{0,96},{1,161},{32,128},{33,193},{64,160},{65,225},{96,192},{97,1}... | collective-permute-start | bytes 393224 | tf_op jit(solution)/shard_map/sentences_back/ppermute | solution.py:50
  170.4 11.6 %collective-permute-start.25 = (bf16[16,4096]{1,0:T(8,128)(2,1)S(1)}, bf16[16,4096]{1,0:T(8,128)(2,1)S(1)}, u32[]{:S(2)}, u32[]{:S(2)}) collective-permute-start(bf16[16,4096]{1,0:T(8,128)(2,1)S(1)} %get-tuple-element.63), channel_id=1, source_target_pairs={{0,192},{1,65},{32,224},{33,97},{64,0},{65,129},{96,32},{97,161},{... | collective-permute-start | bytes 393224 | tf_op jit(solution)/shard_map/sentences_back/ppermute | solution.py:50
  173.0 9.1 %collective-permute-start.26 = (bf16[16,4096]{1,0:T(8,128)(2,1)S(1)}, bf16[16,4096]{1,0:T(8,128)(2,1)S(1)}, u32[]{:S(2)}, u32[]{:S(2)}) collective-permute-start(bf16[16,4096]{1,0:T(8,128)(2,1)S(1)} %get-tuple-element.64), channel_id=1, source_target_pairs={{0,64},{1,193},{32,96},{33,225},{64,128},{65,1},{96,160},{97,33},{... | collective-permute-start | bytes 393224 | tf_op jit(solution)/shard_map/sentences_back/ppermute | solution.py:50
  175.0 7.1 %collective-permute-start.27 = (bf16[16,4096]{1,0:T(8,128)(2,1)S(1)}, bf16[16,4096]{1,0:T(8,128)(2,1)S(1)}, u32[]{:S(2)}, u32[]{:S(2)}) collective-permute-start(bf16[16,4096]{1,0:T(8,128)(2,1)S(1)} %get-tuple-element.65), channel_id=1, source_target_pairs={{0,224},{1,33},{32,0},{33,65},{64,32},{65,97},{96,64},{97,129},{12... | collective-permute-start | bytes 393224 | tf_op jit(solution)/shard_map/sentences_back/ppermute | solution.py:50
  178.7 5.0 %collective-permute-start.28 = (bf16[16,4096]{1,0:T(8,128)(2,1)S(1)}, bf16[16,4096]{1,0:T(8,128)(2,1)S(1)}, u32[]{:S(2)}, u32[]{:S(2)}) collective-permute-start(bf16[16,4096]{1,0:T(8,128)(2,1)S(1)} %get-tuple-element.66), channel_id=1, source_target_pairs={{0,32},{1,225},{32,64},{33,1},{64,96},{65,33},{96,128},{97,65},{12... | collective-permute-start | bytes 393224 | tf_op jit(solution)/shard_map/sentences_back/ppermute | solution.py:50

commit v3 on v2

--- a/solution.py
+++ b/solution.py
@@ -71,6 +71,13 @@
     dy = jnp.where(core == 0, second, first)
     dx = jnp.where(core == 0, first, second)
     return lax.rem(y - dy + SIDE, SIDE) * SIDE + lax.rem(x - dx + SIDE, SIDE)
+
+
+def label_kernel(memory_ref, lang_ref, src_ref, tgt_ref, out_ref):
+    lane = lax.broadcasted_iota(jnp.int32, (SRC, HEAD), 1)
+    numbers = jnp.where(lane == 0, lang_ref[...], jnp.where(lane == 1, src_ref[...], tgt_ref[...]))
+    out_ref[:, :WIDTH] = memory_ref[...]
+    out_ref[:, WIDTH:] = numbers.astype(F32).astype(BF)
 
 
 def route_kernel(place_ref, *refs):
@@ -281,12 +288,14 @@
 
 
 def pick_kernel(place_ref, *refs):
-    candidates, out_ref = refs[:PLANES], refs[PLANES]
+    candidates, out_ref, sem = refs[:PLANES], refs[PLANES], refs[PLANES + 1]
     for d, ref in zip(FAR_FIRST, candidates):
 
         @pl.when(place_ref[3] == d)
         def _():
-            out_ref[...] = ref[...]
+            copy = pltpu.make_async_copy(ref, out_ref, sem)
+            copy.start()
+            copy.wait()
 
 
 def local(memory, lang_id, src_len, tgt_len, queries, key_weight, value_weight, grad_context):
@@ -297,10 +306,13 @@
     place = jnp.stack([plane, y, x, ahead, core]).astype(jnp.int32)
 
     with jax.named_scope("sentences_over_lang"):
-        lane = lax.broadcasted_iota(jnp.int32, (SRC, HEAD), 1)
-        numbers = jnp.where(lane == 0, lang_id[0], jnp.where(lane == 1, src_len[0], tgt_len[0]))
-        sentence = jnp.concatenate([memory[0], numbers.astype(BF)], axis=1)
-
+        sentence = pl.pallas_call(
+            label_kernel,
+            out_shape=jax.ShapeDtypeStruct((SRC, WIDTH + HEAD), BF),
+            in_specs=[VMEM] * 4,
+            out_specs=VMEM,
+            compiler_params=params(4),
+        )(memory[0], *(number.reshape(1, 1) for number in (lang_id, src_len, tgt_len)))
         column = [sentence] + [shift_lang(sentence, d) for d in FAR_FIRST[1:]]
 
     with jax.named_scope("route"):
@@ -457,8 +469,9 @@
         grad_memory = pl.pallas_call(
             pick_kernel,
             out_shape=jax.ShapeDtypeStruct((SRC, WIDTH), BF),
-            in_specs=[SMEM] + [VMEM] * PLANES,
-            out_specs=VMEM,
+            in_specs=[SMEM] + [ANY] * PLANES,
+            out_specs=ANY,
+            scratch_shapes=[pltpu.SemaphoreType.DMA],
             compiler_params=params(16),
         )(place, *candidates)
 

time: 186 us -> 186 us (level)
  no operation moved by 1% of the time
where the time goes in v3:
time: 186 us; the launch traced here: 185 us
  waiting for transfers between devices  66.6 us (36%)
  starting transfers between devices  54 us (29%)
  Pallas kernels  29.5 us (16%)
  blocking collectives  28.1 us (15%)
  between operations  3.19 us (2%)
  other arithmetic  2.66 us (1%)
    ppermute x12, waiting for transfers between devices, shift_plane(): return lax.ppermute(value, ('y', 'x', 'core'), pairs)  51.7 us
    ppermute x14, starting transfers between devices, shift_lang(): return lax.ppermute(value, ('lang', 'core'), pairs)  36.7 us
    ppermute x12, starting transfers between devices, shift_plane(): return lax.ppermute(value, ('y', 'x', 'core'), pairs)  16.7 us
    ppermute x14, waiting for transfers between devices, shift_lang(): return lax.ppermute(value, ('lang', 'core'), pairs)  14.9 us
    all_to_all x1, blocking collectives, local(): slot_rows = lax.all_to_all(projected, PLANE, 0, 0, tiled=True)  14.4 us
    all_to_all x1, blocking collectives, local(): head_grads = lax.all_to_all(slot_grads, PLANE, 0, 0, tiled=True)  13.7 us
    pallas_call x1, Pallas kernels, local(): pl.pallas_call(attend_kernel, grid=(groups,), out_shape=(jax.ShapeDtypeSt...  6.67 us
    pallas_call x2, Pallas kernels, local(): pl.pallas_call(functools.partial(partial_kernel, distances), grid=(WIDTH...  5.38 us
  transfers between devices with their start and end apart: 29, of which 17 were waited for; matrix products, arithmetic and copies ran while one was open for 1% of the time, Pallas kernels for 8%

profile of v3, /device:TPU:32, one launch (start us, length us, event | category | flops | bytes accessed | tf_op | source)
XLA Modules:
  0.0 185.2 jit_solution(14787484249463473962)
XLA Ops:
  2.7 0.9 copy-done.9
  3.7 6.3 %collective-permute-start.6 = (bf16[16,4224]{1,0:T(8,128)(2,1)S(1)}, bf16[16,4224]{1,0:T(8,128)(2,1)S(1)}, u32[]{:S(2)}, u32[]{:S(2)}) collective-permute-start(bf16[16,4224]{1,0:T(8,128)(2,1)S(1)} %sentences_over_lang.1.refs_0_), channel_id=1, source_target_pairs={{0,128},{1,129},{32,160},{33,161},{64,192},{65,193},{96,224},{97,2... | collective-permute-start | bytes 405512 | tf_op jit(solution)/shard_map/sentences_over_lang/ppermute | solution.py:50
  10.1 5.0 %collective-permute-start.4 = (bf16[16,4224]{1,0:T(8,128)(2,1)S(1)}, bf16[16,4224]{1,0:T(8,128)(2,1)S(1)}, u32[]{:S(2)}, u32[]{:S(2)}) collective-permute-start(bf16[16,4224]{1,0:T(8,128)(2,1)S(1)} %sentences_over_lang.1.refs_0_), channel_id=1, source_target_pairs={{0,160},{1,97},{32,192},{33,129},{64,224},{65,161},{96,0},{97,193}... | collective-permute-start | bytes 405512 | tf_op jit(solution)/shard_map/sentences_over_lang/ppermute | solution.py:50
  15.3 3.9 %collective-permute-start.2 = (bf16[16,4224]{1,0:T(8,128)(2,1)S(1)}, bf16[16,4224]{1,0:T(8,128)(2,1)S(1)}, u32[]{:S(2)}, u32[]{:S(2)}) collective-permute-start(bf16[16,4224]{1,0:T(8,128)(2,1)S(1)} %sentences_over_lang.1.refs_0_), channel_id=1, source_target_pairs={{0,192},{1,65},{32,224},{33,97},{64,0},{65,129},{96,32},{97,161},{... | collective-permute-start | bytes 405512 | tf_op jit(solution)/shard_map/sentences_over_lang/ppermute | solution.py:50
  19.2 2.4 %collective-permute-start.1 = (bf16[16,4224]{1,0:T(8,128)(2,1)S(1)}, bf16[16,4224]{1,0:T(8,128)(2,1)S(1)}, u32[]{:S(2)}, u32[]{:S(2)}) collective-permute-start(bf16[16,4224]{1,0:T(8,128)(2,1)S(1)} %sentences_over_lang.1.refs_0_), channel_id=1, source_target_pairs={{0,32},{1,225},{32,64},{33,1},{64,96},{65,33},{96,128},{97,65},{12... | collective-permute-start | bytes 405512 | tf_op jit(solution)/shard_map/sentences_over_lang/ppermute | solution.py:50
  21.6 3.9 %collective-permute-done.5.refs_6_ = bf16[16,4224]{1,0:T(8,128)(2,1)S(1)} collective-permute-done((bf16[16,4224]{1,0:T(8,128)(2,1)S(1)}, bf16[16,4224]{1,0:T(8,128)(2,1)S(1)}, u32[]{:S(2)}, u32[]{:S(2)}) %collective-permute-start.5) | collective-permute-done | bytes 135200 | tf_op jit(solution)/shard_map/sentences_over_lang/ppermute | solution.py:50
  25.5 4.9 %collective-permute-start = (bf16[16,4224]{1,0:T(8,128)(2,1)S(1)}, bf16[16,4224]{1,0:T(8,128)(2,1)S(1)}, u32[]{:S(2)}, u32[]{:S(2)}) collective-permute-start(bf16[16,4224]{1,0:T(8,128)(2,1)S(1)} %sentences_over_lang.1.refs_0_), channel_id=1, source_target_pairs={{0,224},{1,33},{32,0},{33,65},{64,32},{65,97},{96,64},{97,129},{12... | collective-permute-start | bytes 405512 | tf_op jit(solution)/shard_map/sentences_over_lang/ppermute | solution.py:50
  31.1 2.9 %collective-permute-done.1.refs_2_ = bf16[16,4224]{1,0:T(8,128)(2,1)S(1)} collective-permute-done((bf16[16,4224]{1,0:T(8,128)(2,1)S(1)}, bf16[16,4224]{1,0:T(8,128)(2,1)S(1)}, u32[]{:S(2)}, u32[]{:S(2)}) %collective-permute-start.1) | collective-permute-done | bytes 135200 | tf_op jit(solution)/shard_map/sentences_over_lang/ppermute | solution.py:50
  34.0 0.8 route.1
  34.9 2.8 %collective-permute-start.9 = (bf16[32,4096]{1,0:T(8,128)(2,1)S(1)}, bf16[32,4096]{1,0:T(8,128)(2,1)S(1)}, u32[]{:S(2)}, u32[]{:S(2)}) collective-permute-start(bf16[32,4096]{1,0:T(8,128)(2,1)S(1)} %get-tuple-element.39.refs_0_), channel_id=1, source_target_pairs={{0,6},{1,25},{2,0},{3,27},{4,2},{5,29},{6,4},{7,31},{8,14},{9,1},{... | collective-permute-start | bytes 786440 | tf_op jit(solution)/shard_map/gather_rows/ppermute | solution.py:62
  37.7 2.3 %collective-permute-start.7 = (bf16[32,4096]{1,0:T(8,128)(2,1)S(1)}, bf16[32,4096]{1,0:T(8,128)(2,1)S(1)}, u32[]{:S(2)}, u32[]{:S(2)}) collective-permute-start(bf16[32,4096]{1,0:T(8,128)(2,1)S(1)} %get-tuple-element.39.refs_0_), channel_id=1, source_target_pairs={{0,4},{1,17},{2,6},{3,19},{4,0},{5,21},{6,2},{7,23},{8,12},{9,25},... | collective-permute-start | bytes 786440 | tf_op jit(solution)/shard_map/gather_rows/ppermute | solution.py:62
  40.5 1.1 collective-permute-done.9.refs_3_
  41.6 6.5 %collective-permute-done.8.refs_2_ = bf16[32,4096]{1,0:T(8,128)(2,1)S(1)} collective-permute-done((bf16[32,4096]{1,0:T(8,128)(2,1)S(1)}, bf16[32,4096]{1,0:T(8,128)(2,1)S(1)}, u32[]{:S(2)}, u32[]{:S(2)}) %collective-permute-start.8) | collective-permute-done | bytes 262176 | tf_op jit(solution)/shard_map/gather_rows/ppermute | solution.py:62
  48.2 3.1 %collective-permute-start.10 = (bf16[128,4096]{1,0:T(8,128)(2,1)S(1)}, bf16[128,4096]{1,0:T(8,128)(2,1)S(1)}, u32[]{:S(2)}, u32[]{:S(2)}) collective-permute-start(bf16[128,4096]{1,0:T(8,128)(2,1)S(1)} %gather_rows.1.refs_0_), channel_id=1, source_target_pairs={{0,24},{1,7},{2,26},{3,1},{4,28},{5,3},{6,30},{7,5},{8,0},{9,15},{... | collective-permute-start | bytes 3145736 | tf_op jit(solution)/shard_map/gather_rows/ppermute | solution.py:62
  51.3 0.6 collective-permute-start.14
  51.9 1.0 collective-permute-start.13
  52.9 21.9 %collective-permute-done.10.refs_1_.refs_3_ = bf16[128,4096]{1,0:T(8,128)(2,1)S(1)} collective-permute-done((bf16[128,4096]{1,0:T(8,128)(2,1)S(1)}, bf16[128,4096]{1,0:T(8,128)(2,1)S(1)}, u32[]{:S(2)}, u32[]{:S(2)}) %collective-permute-start.10) | collective-permute-done | bytes 1048608 | tf_op jit(solution)/shard_map/gather_rows/ppermute | solution.py:62
  74.9 3.1 %project.2.early_ref = bf16[256,512]{1,0:T(8,128)(2,1)S(1)} custom-call(s32[5]{0:T(128)S(1)} %stack.23.place_ref, bf16[128,4096]{1,0:T(8,128)(2,1)S(1)} %gather_rows.1.refs_0_, bf16[128,4096]{1,0:T(8,128)(2,1)S(1)} %collective-permute-done.10.refs_1_.refs_3_, bf16[4096,128]{1,0:T(8,128)(2,1)S(1)} %bitcast.25, bf16[4096,128]{1,0:T(8,128)(2,1)S(1)} %bitcast.30, ...), custom_call_target="tpu_custom_call" | custom-call | flops 1073741824 | bytes 6291456 | tf_op jit(solution)/shard_map/project/pallas_call | solution.py:357
  78.0 0.9 collective-permute-done.13.refs_0_.refs_2_
  78.9 3.1 %project.3 = bf16[16,32,512]{2,1,0:T(8,128)(2,1)S(1)} custom-call(s32[5]{0:T(128)S(1)} %stack.23.place_ref, bf16[256,512]{1,0:T(8,128)(2,1)S(1)} %project.2.early_ref, bf16[128,4096]{1,0:T(8,128)(2,1)S(1)} %collective-permute-done.13.refs_0_.refs_2_, bf16[128,4096]{1,0:T(8,128)(2,1)S(1)} %collective-permute-done.14.refs_1_, bf16[4096,128]{1,0:T(8,128)(2,1)S(1)} %bitcast.26, ...), custom_call_target="tpu_custom_call" | custom-call | flops 1073741824 | bytes 6291456 | tf_op jit(solution)/shard_map/project/pallas_call | solution.py:366
  82.0 14.4 %all_to_all.10.kv_ref = bf16[16,32,512]{2,1,0:T(8,128)(2,1)} all-to-all(bf16[16,32,512]{2,1,0:T(8,128)(2,1)S(1)} %project.3), channel_id=1, replica_groups=mesh['lang'=8,'y'=4,'x'=4,'core'=2] {'y','x'}, dimensions={0} | all-to-all | bytes 1048576 | tf_op jit(solution)/shard_map/rows_to_slots/all_to_all | solution.py:377
  96.4 6.7 %attend.2 = (bf16[16,32,512]{2,1,0:T(8,128)(2,1)}, bf16[2,512,128]{2,1,0:T(8,128)(2,1)}, bf16[2,512,128]{2,1,0:T(8,128)(2,1)}) custom-call(s32[5]{0:T(128)} %copy-done.10, f32[4,8,128]{2,1,0:T(8,128)} %copy-done.12, bf16[2,128,4096]{2,1,0:T(8,128)(2,1)} %bitcast.35, bf16[2,128,4096]{2,1,0:T(8,128)(2,1)} %bitcast.36, bf16[16,32,512]{2,1,0:T(8,128)(2,1)} %all_to_all.10.kv_ref), custom_call_target="tpu_custom_call" | custom-call | flops 1073741824 | bytes 6291456 | tf_op jit(solution)/shard_map/attend/pallas_call | solution.py:385
  103.1 13.7 %all_to_all.11.grads_ref = bf16[16,32,512]{2,1,0:T(8,128)(2,1)S(1)} all-to-all(bf16[16,32,512]{2,1,0:T(8,128)(2,1)} %get-tuple-element.42), channel_id=1, replica_groups=mesh['lang'=8,'y'=4,'x'=4,'core'=2] {'y','x'}, dimensions={0} | all-to-all | bytes 1048576 | tf_op jit(solution)/shard_map/grads_to_heads/all_to_all | solution.py:398
  116.7 2.7 %sum_rows.2 = (bf16[128,4096]{1,0:T(8,128)(2,1)S(1)}, bf16[128,4096]{1,0:T(8,128)(2,1)S(1)}) custom-call(s32[5]{0:T(128)S(1)} %copy-done.11, bf16[16,32,512]{2,1,0:T(8,128)(2,1)S(1)} %all_to_all.11.grads_ref, bf16[4096,128]{1,0:T(8,128)(2,1)S(1)} %bitcast.27, bf16[4096,128]{1,0:T(8,128)(2,1)S(1)} %bitcast.32, ...), custom_call_target="tpu_custom_call" | custom-call | flops 1073741824 | bytes 7340032 | tf_op jit(solution)/shard_map/sum_rows/pallas_call | solution.py:417
  119.4 0.9 collective-permute-start.15
  120.3 2.5 %collective-permute-start.16 = (bf16[128,4096]{1,0:T(8,128)(2,1)S(1)}, bf16[128,4096]{1,0:T(8,128)(2,1)S(1)}, u32[]{:S(2)}, u32[]{:S(2)}) collective-permute-start(bf16[128,4096]{1,0:T(8,128)(2,1)S(1)} %get-tuple-element.53), channel_id=1, source_target_pairs={{0,6},{1,25},{2,0},{3,27},{4,2},{5,29},{6,4},{7,31},{8,14},{9,1},{... | collective-permute-start | bytes 3145736 | tf_op jit(solution)/shard_map/sum_rows/ppermute | solution.py:62
  122.8 2.7 %sum_rows.3 = (bf16[128,4096]{1,0:T(8,128)(2,1)S(1)}, bf16[128,4096]{1,0:T(8,128)(2,1)S(1)}) custom-call(s32[5]{0:T(128)S(1)} %copy-done.11, bf16[16,32,512]{2,1,0:T(8,128)(2,1)S(1)} %all_to_all.11.grads_ref, bf16[4096,128]{1,0:T(8,128)(2,1)S(1)} %bitcast.28, bf16[4096,128]{1,0:T(8,128)(2,1)S(1)} %bitcast.33, ...), custom_call_target="tpu_custom_call" | custom-call | flops 1073741824 | bytes 7340032 | tf_op jit(solution)/shard_map/sum_rows/pallas_call | solution.py:417
  125.6 5.0 %weight_grads.1 = (bf16[4096,256]{1,0:T(8,128)(2,1)S(1)}, bf16[4096,256]{1,0:T(8,128)(2,1)S(1)}) custom-call(s32[5]{0:T(128)S(1)} %copy-done.11, bf16[16,32,512]{2,1,0:T(8,128)(2,1)S(1)} %all_to_all.11.grads_ref, bf16[128,4096]{1,0:T(8,128)(2,1)S(1)} %gather_rows.1.refs_0_, bf16[128,4096]{1,0:T(8,128)(2,1)S(1)} %copy-done.4, ...), custom_call_target="tpu_custom_call" | custom-call | flops 2147483648 | bytes 16777216 | tf_op jit(solution)/shard_map/weight_grads/pallas_call | solution.py:437
  130.8 3.9 %attend.3 = (bf16[2,128,4096]{2,1,0:T(8,128)(2,1)}, bf16[2,128,4096]{2,1,0:T(8,128)(2,1)}) custom-call(s32[5]{0:T(128)S(1)} %copy-done.11, f32[4,8,128]{2,1,0:T(8,128)S(1)} %copy-done.13, bf16[2,512,128]{2,1,0:T(8,128)(2,1)S(1)} %copy-done.14, bf16[2,512,128]{2,1,0:T(8,128)(2,1)S(1)} %copy-done.15, bf16[16,32,512]{2,1,0:T(8,128)(2,1)S(1)} %copy-done.2), custom_call_target="tpu_custom_call" | custom-call | flops 2147483648 | bytes 16777216 | tf_op jit(solution)/shard_map/attend/pallas_call | solution.py:401
  134.7 1.2 collective-permute-done.15
  135.9 9.7 %collective-permute-done.16 = bf16[128,4096]{1,0:T(8,128)(2,1)S(1)} collective-permute-done((bf16[128,4096]{1,0:T(8,128)(2,1)S(1)}, bf16[128,4096]{1,0:T(8,128)(2,1)S(1)}, u32[]{:S(2)}, u32[]{:S(2)}) %collective-permute-start.16) | collective-permute-done | bytes 1048608 | tf_op jit(solution)/shard_map/sum_rows/ppermute | solution.py:62
  145.7 5.0 %collective-permute-done.17 = bf16[128,4096]{1,0:T(8,128)(2,1)S(1)} collective-permute-done((bf16[128,4096]{1,0:T(8,128)(2,1)S(1)}, bf16[128,4096]{1,0:T(8,128)(2,1)S(1)}, u32[]{:S(2)}, u32[]{:S(2)}) %collective-permute-start.17) | collective-permute-done | bytes 1048608 | tf_op jit(solution)/shard_map/sum_rows/ppermute | solution.py:62
  150.7 0.7 add_convert_fusion.2
  151.7 1.2 collective-permute-start.21
  152.9 2.0 %collective-permute-start.20 = (bf16[32,4096]{1,0:T(8,128)(2,1)S(1)}, bf16[32,4096]{1,0:T(8,128)(2,1)S(1)}, u32[]{:S(2)}, u32[]{:S(2)}) collective-permute-start(bf16[32,4096]{1,0:T(8,128)(2,1)S(1)} %get-tuple-element.73), channel_id=1, source_target_pairs={{0,24},{1,7},{2,26},{3,1},{4,28},{5,3},{6,30},{7,5},{8,0},{9,15},{... | collective-permute-start | bytes 786440 | tf_op jit(solution)/shard_map/sum_rows/ppermute | solution.py:62
  154.9 1.9 %add_convert_fusion = (bf16[4096,128]{1,0:T(8,128)(2,1)}, bf16[4096,128]{1,0:T(8,128)(2,1)}) fusion(bf16[4096,256]{1,0:T(8,128)(2,1)S(1)} %collective-permute-done.19, bf16[4096,256]{1,0:T(8,128)(2,1)S(1)} %get-tuple-element.56), kind=kLoop, calls=%fused_computation | loop fusion | flops 4194304 | bytes 6291456 | tf_op jit(solution)/shard_map/weight_grads/convert_element_type | solution.py:450
  156.8 2.7 %collective-permute-done.18 = bf16[32,4096]{1,0:T(8,128)(2,1)S(1)} collective-permute-done((bf16[32,4096]{1,0:T(8,128)(2,1)S(1)}, bf16[32,4096]{1,0:T(8,128)(2,1)S(1)}, u32[]{:S(2)}, u32[]{:S(2)}) %collective-permute-start.18) | collective-permute-done | bytes 262176 | tf_op jit(solution)/shard_map/sum_rows/ppermute | solution.py:62
  159.5 2.6 %collective-permute-done.21 = bf16[32,4096]{1,0:T(8,128)(2,1)S(1)} collective-permute-done((bf16[32,4096]{1,0:T(8,128)(2,1)S(1)}, bf16[32,4096]{1,0:T(8,128)(2,1)S(1)}, u32[]{:S(2)}, u32[]{:S(2)}) %collective-permute-start.21) | collective-permute-done | bytes 262176 | tf_op jit(solution)/shard_map/sum_rows/ppermute | solution.py:62
  162.3 3.1 %collective-permute-start.22 = (bf16[16,4096]{1,0:T(8,128)(2,1)S(1)}, bf16[16,4096]{1,0:T(8,128)(2,1)S(1)}, u32[]{:S(2)}, u32[]{:S(2)}) collective-permute-start(bf16[16,4096]{1,0:T(8,128)(2,1)S(1)} %get-tuple-element.60), channel_id=1, source_target_pairs={{0,128},{1,129},{32,160},{33,161},{64,192},{65,193},{96,224},{97,2... | collective-permute-start | bytes 393224 | tf_op jit(solution)/shard_map/sentences_back/ppermute | solution.py:50
  165.5 2.6 %collective-permute-start.23 = (bf16[16,4096]{1,0:T(8,128)(2,1)S(1)}, bf16[16,4096]{1,0:T(8,128)(2,1)S(1)}, u32[]{:S(2)}, u32[]{:S(2)}) collective-permute-start(bf16[16,4096]{1,0:T(8,128)(2,1)S(1)} %get-tuple-element.61), channel_id=1, source_target_pairs={{0,160},{1,97},{32,192},{33,129},{64,224},{65,161},{96,0},{97,193}... | collective-permute-start | bytes 393224 | tf_op jit(solution)/shard_map/sentences_back/ppermute | solution.py:50
  168.1 2.4 %collective-permute-start.24 = (bf16[16,4096]{1,0:T(8,128)(2,1)S(1)}, bf16[16,4096]{1,0:T(8,128)(2,1)S(1)}, u32[]{:S(2)}, u32[]{:S(2)}) collective-permute-start(bf16[16,4096]{1,0:T(8,128)(2,1)S(1)} %get-tuple-element.62), channel_id=1, source_target_pairs={{0,96},{1,161},{32,128},{33,193},{64,160},{65,225},{96,192},{97,1}... | collective-permute-start | bytes 393224 | tf_op jit(solution)/shard_map/sentences_back/ppermute | solution.py:50
  170.5 2.4 %collective-permute-start.25 = (bf16[16,4096]{1,0:T(8,128)(2,1)S(1)}, bf16[16,4096]{1,0:T(8,128)(2,1)S(1)}, u32[]{:S(2)}, u32[]{:S(2)}) collective-permute-start(bf16[16,4096]{1,0:T(8,128)(2,1)S(1)} %get-tuple-element.63), channel_id=1, source_target_pairs={{0,192},{1,65},{32,224},{33,97},{64,0},{65,129},{96,32},{97,161},{... | collective-permute-start | bytes 393224 | tf_op jit(solution)/shard_map/sentences_back/ppermute | solution.py:50
  173.5 1.6 collective-permute-done.22.refs_1_
  175.5 3.3 %collective-permute-done.23.refs_2_ = bf16[16,4096]{1,0:T(8,128)(2,1)S(1)} collective-permute-done((bf16[16,4096]{1,0:T(8,128)(2,1)S(1)}, bf16[16,4096]{1,0:T(8,128)(2,1)S(1)}, u32[]{:S(2)}, u32[]{:S(2)}) %collective-permute-start.23) | collective-permute-done | bytes 131104 | tf_op jit(solution)/shard_map/sentences_back/ppermute | solution.py:50
  178.8 2.4 %collective-permute-start.28 = (bf16[16,4096]{1,0:T(8,128)(2,1)S(1)}, bf16[16,4096]{1,0:T(8,128)(2,1)S(1)}, u32[]{:S(2)}, u32[]{:S(2)}) collective-permute-start(bf16[16,4096]{1,0:T(8,128)(2,1)S(1)} %get-tuple-element.66), channel_id=1, source_target_pairs={{0,32},{1,225},{32,64},{33,1},{64,96},{65,33},{96,128},{97,65},{12... | collective-permute-start | bytes 393224 | tf_op jit(solution)/shard_map/sentences_back/ppermute | solution.py:50
  181.2 0.9 collective-permute-done.25.refs_4_
  182.1 1.7 collective-permute-done.28.refs_7_
  183.7 1.2 sentences_back.3
  (61 shorter events, 3.6 us)
Async XLA Ops:
  0.6 74.2 %copy-start.1 = (bf16[1,4096,128]{2,1,0:T(8,128)(2,1)S(1)}, bf16[1,4096,128]{2,1,0:T(8,128)(2,1)}, u32[]{:S(2)}) copy-start(bf16[1,4096,128]{2,1,0:T(8,128)(2,1)} %param.14) | copy-start | bytes 3145732
  0.6 74.2 %copy-start = (bf16[1,4096,128]{2,1,0:T(8,128)(2,1)S(1)}, bf16[1,4096,128]{2,1,0:T(8,128)(2,1)}, u32[]{:S(2)}) copy-start(bf16[1,4096,128]{2,1,0:T(8,128)(2,1)} %param.13) | copy-start | bytes 3145732
  2.7 0.9 copy-start.9
  3.7 15.5 %collective-permute-start.6 = (bf16[16,4224]{1,0:T(8,128)(2,1)S(1)}, bf16[16,4224]{1,0:T(8,128)(2,1)S(1)}, u32[]{:S(2)}, u32[]{:S(2)}) collective-permute-start(bf16[16,4224]{1,0:T(8,128)(2,1)S(1)} %sentences_over_lang.1.refs_0_), channel_id=1, source_target_pairs={{0,128},{1,129},{32,160},{33,161},{64,192},{65,193},{96,224},{97,2... | collective-permute-start | bytes 405512 | tf_op jit(solution)/shard_map/sentences_over_lang/ppermute | solution.py:50
  10.0 15.5 %collective-permute-start.5 = (bf16[16,4224]{1,0:T(8,128)(2,1)S(1)}, bf16[16,4224]{1,0:T(8,128)(2,1)S(1)}, u32[]{:S(2)}, u32[]{:S(2)}) collective-permute-start(bf16[16,4224]{1,0:T(8,128)(2,1)S(1)} %sentences_over_lang.1.refs_0_), channel_id=1, source_target_pairs={{0,96},{1,161},{32,128},{33,193},{64,160},{65,225},{96,192},{97,1}... | collective-permute-start | bytes 405512 | tf_op jit(solution)/shard_map/sentences_over_lang/ppermute | solution.py:50
  10.1 20.4 %collective-permute-start.4 = (bf16[16,4224]{1,0:T(8,128)(2,1)S(1)}, bf16[16,4224]{1,0:T(8,128)(2,1)S(1)}, u32[]{:S(2)}, u32[]{:S(2)}) collective-permute-start(bf16[16,4224]{1,0:T(8,128)(2,1)S(1)} %sentences_over_lang.1.refs_0_), channel_id=1, source_target_pairs={{0,160},{1,97},{32,192},{33,129},{64,224},{65,161},{96,0},{97,193}... | collective-permute-start | bytes 405512 | tf_op jit(solution)/shard_map/sentences_over_lang/ppermute | solution.py:50
  15.1 15.8 %collective-permute-start.3 = (bf16[16,4224]{1,0:T(8,128)(2,1)S(1)}, bf16[16,4224]{1,0:T(8,128)(2,1)S(1)}, u32[]{:S(2)}, u32[]{:S(2)}) collective-permute-start(bf16[16,4224]{1,0:T(8,128)(2,1)S(1)} %sentences_over_lang.1.refs_0_), channel_id=1, source_target_pairs={{0,64},{1,193},{32,96},{33,225},{64,128},{65,1},{96,160},{97,33},{... | collective-permute-start | bytes 405512 | tf_op jit(solution)/shard_map/sentences_over_lang/ppermute | solution.py:50
  15.3 15.8 %collective-permute-start.2 = (bf16[16,4224]{1,0:T(8,128)(2,1)S(1)}, bf16[16,4224]{1,0:T(8,128)(2,1)S(1)}, u32[]{:S(2)}, u32[]{:S(2)}) collective-permute-start(bf16[16,4224]{1,0:T(8,128)(2,1)S(1)} %sentences_over_lang.1.refs_0_), channel_id=1, source_target_pairs={{0,192},{1,65},{32,224},{33,97},{64,0},{65,129},{96,32},{97,161},{... | collective-permute-start | bytes 405512 | tf_op jit(solution)/shard_map/sentences_over_lang/ppermute | solution.py:50
  19.2 14.8 %collective-permute-start.1 = (bf16[16,4224]{1,0:T(8,128)(2,1)S(1)}, bf16[16,4224]{1,0:T(8,128)(2,1)S(1)}, u32[]{:S(2)}, u32[]{:S(2)}) collective-permute-start(bf16[16,4224]{1,0:T(8,128)(2,1)S(1)} %sentences_over_lang.1.refs_0_), channel_id=1, source_target_pairs={{0,32},{1,225},{32,64},{33,1},{64,96},{65,33},{96,128},{97,65},{12... | collective-permute-start | bytes 405512 | tf_op jit(solution)/shard_map/sentences_over_lang/ppermute | solution.py:50
  25.5 8.5 %collective-permute-start = (bf16[16,4224]{1,0:T(8,128)(2,1)S(1)}, bf16[16,4224]{1,0:T(8,128)(2,1)S(1)}, u32[]{:S(2)}, u32[]{:S(2)}) collective-permute-start(bf16[16,4224]{1,0:T(8,128)(2,1)S(1)} %sentences_over_lang.1.refs_0_), channel_id=1, source_target_pairs={{0,224},{1,33},{32,0},{33,65},{64,32},{65,97},{96,64},{97,129},{12... | collective-permute-start | bytes 405512 | tf_op jit(solution)/shard_map/sentences_over_lang/ppermute | solution.py:50
  30.5 48.4 %copy-start.10 = (s32[5]{0:T(128)}, s32[5]{0:T(128)S(1)}, u32[]{:S(2)}) copy-start(s32[5]{0:T(128)S(1)} %stack.23.place_ref) | copy-start | bytes 64
  34.9 18.1 %copy-start.12 = (f32[4,8,128]{2,1,0:T(8,128)}, f32[4,8,128]{2,1,0:T(8,128)S(1)}, u32[]{:S(2)}) copy-start(f32[4,8,128]{2,1,0:T(8,128)S(1)} %get-tuple-element.37.lens_ref) | copy-start | bytes 49156
  34.9 6.7 %collective-permute-start.9 = (bf16[32,4096]{1,0:T(8,128)(2,1)S(1)}, bf16[32,4096]{1,0:T(8,128)(2,1)S(1)}, u32[]{:S(2)}, u32[]{:S(2)}) collective-permute-start(bf16[32,4096]{1,0:T(8,128)(2,1)S(1)} %get-tuple-element.39.refs_0_), channel_id=1, source_target_pairs={{0,6},{1,25},{2,0},{3,27},{4,2},{5,29},{6,4},{7,31},{8,14},{9,1},{... | collective-permute-start | bytes 786440 | tf_op jit(solution)/shard_map/gather_rows/ppermute | solution.py:62
  37.7 10.4 %collective-permute-start.8 = (bf16[32,4096]{1,0:T(8,128)(2,1)S(1)}, bf16[32,4096]{1,0:T(8,128)(2,1)S(1)}, u32[]{:S(2)}, u32[]{:S(2)}) collective-permute-start(bf16[32,4096]{1,0:T(8,128)(2,1)S(1)} %get-tuple-element.39.refs_0_), channel_id=1, source_target_pairs={{0,2},{1,9},{2,4},{3,11},{4,6},{5,13},{6,0},{7,15},{8,10},{9,17},{... | collective-permute-start | bytes 786440 | tf_op jit(solution)/shard_map/gather_rows/ppermute | solution.py:62
  37.7 10.4 %collective-permute-start.7 = (bf16[32,4096]{1,0:T(8,128)(2,1)S(1)}, bf16[32,4096]{1,0:T(8,128)(2,1)S(1)}, u32[]{:S(2)}, u32[]{:S(2)}) collective-permute-start(bf16[32,4096]{1,0:T(8,128)(2,1)S(1)} %get-tuple-element.39.refs_0_), channel_id=1, source_target_pairs={{0,4},{1,17},{2,6},{3,19},{4,0},{5,21},{6,2},{7,23},{8,12},{9,25},... | collective-permute-start | bytes 786440 | tf_op jit(solution)/shard_map/gather_rows/ppermute | solution.py:62
  40.0 12.9 %collective-permute-start.11 = (bf16[4096,128]{1,0:T(8,128)(2,1)}, bf16[4096,128]{1,0:T(8,128)(2,1)S(1)}, u32[]{:S(2)}, u32[]{:S(2)}) collective-permute-start(bf16[4096,128]{1,0:T(8,128)(2,1)} %bitcast.24), channel_id=1, source_target_pairs={{0,1},{1,0},{2,3},{3,2},{4,5},{5,4},{6,7},{7,6},{8,9},{9,8},{10,11... | collective-permute-start | bytes 3145736 | tf_op jit(solution)/shard_map/weights_of_chip/ppermute | solution.py:41
  40.0 12.9 %collective-permute-start.12 = (bf16[4096,128]{1,0:T(8,128)(2,1)}, bf16[4096,128]{1,0:T(8,128)(2,1)S(1)}, u32[]{:S(2)}, u32[]{:S(2)}) collective-permute-start(bf16[4096,128]{1,0:T(8,128)(2,1)} %bitcast.29), channel_id=1, source_target_pairs={{0,1},{1,0},{2,3},{3,2},{4,5},{5,4},{6,7},{7,6},{8,9},{9,8},{10,11... | collective-permute-start | bytes 3145736 | tf_op jit(solution)/shard_map/weights_of_chip/ppermute | solution.py:41
  48.2 26.6 %collective-permute-start.10 = (bf16[128,4096]{1,0:T(8,128)(2,1)S(1)}, bf16[128,4096]{1,0:T(8,128)(2,1)S(1)}, u32[]{:S(2)}, u32[]{:S(2)}) collective-permute-start(bf16[128,4096]{1,0:T(8,128)(2,1)S(1)} %gather_rows.1.refs_0_), channel_id=1, source_target_pairs={{0,24},{1,7},{2,26},{3,1},{4,28},{5,3},{6,30},{7,5},{8,0},{9,15},{... | collective-permute-start | bytes 3145736 | tf_op jit(solution)/shard_map/gather_rows/ppermute | solution.py:62
  51.3 26.7 %collective-permute-start.14 = (bf16[128,4096]{1,0:T(8,128)(2,1)S(1)}, bf16[128,4096]{1,0:T(8,128)(2,1)S(1)}, u32[]{:S(2)}, u32[]{:S(2)}) collective-permute-start(bf16[128,4096]{1,0:T(8,128)(2,1)S(1)} %gather_rows.1.refs_0_), channel_id=1, source_target_pairs={{0,16},{1,5},{2,18},{3,7},{4,20},{5,1},{6,22},{7,3},{8,24},{9,13},... | collective-permute-start | bytes 3145736 | tf_op jit(solution)/shard_map/gather_rows/ppermute | solution.py:62
  51.9 26.9 %collective-permute-start.13 = (bf16[128,4096]{1,0:T(8,128)(2,1)S(1)}, bf16[128,4096]{1,0:T(8,128)(2,1)S(1)}, u32[]{:S(2)}, u32[]{:S(2)}) collective-permute-start(bf16[128,4096]{1,0:T(8,128)(2,1)S(1)} %gather_rows.1.refs_0_), channel_id=1, source_target_pairs={{0,8},{1,3},{2,10},{3,5},{4,12},{5,7},{6,14},{7,1},{8,16},{9,11},{... | collective-permute-start | bytes 3145736 | tf_op jit(solution)/shard_map/gather_rows/ppermute | solution.py:62
  74.9 3.1 %copy-start.7 = (bf16[128,4096]{1,0:T(8,128)(2,1)}, bf16[128,4096]{1,0:T(8,128)(2,1)S(1)}, u32[]{:S(2)}) copy-start(bf16[128,4096]{1,0:T(8,128)(2,1)S(1)} %collective-permute-done.10.refs_1_.refs_3_) | copy-start | bytes 3145732
  78.0 4.0 %copy-start.3 = (bf16[128,4096]{1,0:T(8,128)(2,1)}, bf16[128,4096]{1,0:T(8,128)(2,1)S(1)}, u32[]{:S(2)}) copy-start(bf16[128,4096]{1,0:T(8,128)(2,1)S(1)} %collective-permute-done.14.refs_1_) | copy-start | bytes 3145732
  78.9 3.1 %copy-start.5 = (bf16[128,4096]{1,0:T(8,128)(2,1)}, bf16[128,4096]{1,0:T(8,128)(2,1)S(1)}, u32[]{:S(2)}) copy-start(bf16[128,4096]{1,0:T(8,128)(2,1)S(1)} %collective-permute-done.13.refs_0_.refs_2_) | copy-start | bytes 3145732
  96.4 20.3 %copy-start.11 = (s32[5]{0:T(128)S(1)}, s32[5]{0:T(128)}, u32[]{:S(2)}) copy-start(s32[5]{0:T(128)} %copy-done.10) | copy-start | bytes 64
  119.4 16.5 %collective-permute-start.15 = (bf16[128,4096]{1,0:T(8,128)(2,1)S(1)}, bf16[128,4096]{1,0:T(8,128)(2,1)S(1)}, u32[]{:S(2)}, u32[]{:S(2)}) collective-permute-start(bf16[128,4096]{1,0:T(8,128)(2,1)S(1)} %get-tuple-element.43), channel_id=1, source_target_pairs={{0,4},{1,17},{2,6},{3,19},{4,0},{5,21},{6,2},{7,23},{8,12},{9,25},... | collective-permute-start | bytes 3145736 | tf_op jit(solution)/shard_map/sum_rows/ppermute | solution.py:62
  120.3 5.3 %copy-start.4 = (bf16[128,4096]{1,0:T(8,128)(2,1)S(1)}, bf16[128,4096]{1,0:T(8,128)(2,1)}, u32[]{:S(2)}) copy-start(bf16[128,4096]{1,0:T(8,128)(2,1)} %copy-done.3) | copy-start | bytes 3145732
  120.3 5.3 %copy-start.6 = (bf16[128,4096]{1,0:T(8,128)(2,1)S(1)}, bf16[128,4096]{1,0:T(8,128)(2,1)}, u32[]{:S(2)}) copy-start(bf16[128,4096]{1,0:T(8,128)(2,1)} %copy-done.5) | copy-start | bytes 3145732
  120.3 5.3 %copy-start.8 = (bf16[128,4096]{1,0:T(8,128)(2,1)S(1)}, bf16[128,4096]{1,0:T(8,128)(2,1)}, u32[]{:S(2)}) copy-start(bf16[128,4096]{1,0:T(8,128)(2,1)} %copy-done.7) | copy-start | bytes 3145732
  120.3 25.4 %collective-permute-start.16 = (bf16[128,4096]{1,0:T(8,128)(2,1)S(1)}, bf16[128,4096]{1,0:T(8,128)(2,1)S(1)}, u32[]{:S(2)}, u32[]{:S(2)}) collective-permute-start(bf16[128,4096]{1,0:T(8,128)(2,1)S(1)} %get-tuple-element.53), channel_id=1, source_target_pairs={{0,6},{1,25},{2,0},{3,27},{4,2},{5,29},{6,4},{7,31},{8,14},{9,1},{... | collective-permute-start | bytes 3145736 | tf_op jit(solution)/shard_map/sum_rows/ppermute | solution.py:62
  125.5 25.2 %collective-permute-start.17 = (bf16[128,4096]{1,0:T(8,128)(2,1)S(1)}, bf16[128,4096]{1,0:T(8,128)(2,1)S(1)}, u32[]{:S(2)}, u32[]{:S(2)}) collective-permute-start(bf16[128,4096]{1,0:T(8,128)(2,1)S(1)} %get-tuple-element.54), channel_id=1, source_target_pairs={{0,2},{1,9},{2,4},{3,11},{4,6},{5,13},{6,0},{7,15},{8,10},{9,17},{... | collective-permute-start | bytes 3145736 | tf_op jit(solution)/shard_map/sum_rows/ppermute | solution.py:62
  125.6 5.2 %copy-start.2 = (bf16[16,32,512]{2,1,0:T(8,128)(2,1)S(1)}, bf16[16,32,512]{2,1,0:T(8,128)(2,1)}, u32[]{:S(2)}) copy-start(bf16[16,32,512]{2,1,0:T(8,128)(2,1)} %all_to_all.10.kv_ref) | copy-start | bytes 1572868
  125.6 5.2 %copy-start.13 = (f32[4,8,128]{2,1,0:T(8,128)S(1)}, f32[4,8,128]{2,1,0:T(8,128)}, u32[]{:S(2)}) copy-start(f32[4,8,128]{2,1,0:T(8,128)} %copy-done.12) | copy-start | bytes 49156
  125.6 5.2 %copy-start.14 = (bf16[2,512,128]{2,1,0:T(8,128)(2,1)S(1)}, bf16[2,512,128]{2,1,0:T(8,128)(2,1)}, u32[]{:S(2)}) copy-start(bf16[2,512,128]{2,1,0:T(8,128)(2,1)} %get-tuple-element.44.attention_ref) | copy-start | bytes 786436
  125.6 5.2 %copy-start.15 = (bf16[2,512,128]{2,1,0:T(8,128)(2,1)S(1)}, bf16[2,512,128]{2,1,0:T(8,128)(2,1)}, u32[]{:S(2)}) copy-start(bf16[2,512,128]{2,1,0:T(8,128)(2,1)} %get-tuple-element.45.grad_scores_ref) | copy-start | bytes 786436
  130.7 24.2 %collective-permute-start.19 = (bf16[4096,256]{1,0:T(8,128)(2,1)S(1)}, bf16[4096,256]{1,0:T(8,128)(2,1)S(1)}, u32[]{:S(2)}, u32[]{:S(2)}) collective-permute-start(bf16[4096,256]{1,0:T(8,128)(2,1)S(1)} %get-tuple-element.57), channel_id=1, source_target_pairs={{0,1},{1,0},{2,3},{3,2},{4,5},{5,4},{6,7},{7,6},{8,9},{9,8},{10,11... | collective-permute-start | bytes 6291464 | tf_op jit(solution)/shard_map/weight_grads/ppermute | solution.py:41
  151.4 8.1 %collective-permute-start.18 = (bf16[32,4096]{1,0:T(8,128)(2,1)S(1)}, bf16[32,4096]{1,0:T(8,128)(2,1)S(1)}, u32[]{:S(2)}, u32[]{:S(2)}) collective-permute-start(bf16[32,4096]{1,0:T(8,128)(2,1)S(1)} %get-tuple-element.71), channel_id=1, source_target_pairs={{0,16},{1,5},{2,18},{3,7},{4,20},{5,1},{6,22},{7,3},{8,24},{9,13},... | collective-permute-start | bytes 786440 | tf_op jit(solution)/shard_map/sum_rows/ppermute | solution.py:62
  151.7 10.4 %collective-permute-start.21 = (bf16[32,4096]{1,0:T(8,128)(2,1)S(1)}, bf16[32,4096]{1,0:T(8,128)(2,1)S(1)}, u32[]{:S(2)}, u32[]{:S(2)}) collective-permute-start(bf16[32,4096]{1,0:T(8,128)(2,1)S(1)} %get-tuple-element.72), channel_id=1, source_target_pairs={{0,8},{1,3},{2,10},{3,5},{4,12},{5,7},{6,14},{7,1},{8,16},{9,11},{... | collective-permute-start | bytes 786440 | tf_op jit(solution)/shard_map/sum_rows/ppermute | solution.py:62
  152.9 9.2 %collective-permute-start.20 = (bf16[32,4096]{1,0:T(8,128)(2,1)S(1)}, bf16[32,4096]{1,0:T(8,128)(2,1)S(1)}, u32[]{:S(2)}, u32[]{:S(2)}) collective-permute-start(bf16[32,4096]{1,0:T(8,128)(2,1)S(1)} %get-tuple-element.73), channel_id=1, source_target_pairs={{0,24},{1,7},{2,26},{3,1},{4,28},{5,3},{6,30},{7,5},{8,0},{9,15},{... | collective-permute-start | bytes 786440 | tf_op jit(solution)/shard_map/sum_rows/ppermute | solution.py:62
  162.3 12.8 %collective-permute-start.22 = (bf16[16,4096]{1,0:T(8,128)(2,1)S(1)}, bf16[16,4096]{1,0:T(8,128)(2,1)S(1)}, u32[]{:S(2)}, u32[]{:S(2)}) collective-permute-start(bf16[16,4096]{1,0:T(8,128)(2,1)S(1)} %get-tuple-element.60), channel_id=1, source_target_pairs={{0,128},{1,129},{32,160},{33,161},{64,192},{65,193},{96,224},{97,2... | collective-permute-start | bytes 393224 | tf_op jit(solution)/shard_map/sentences_back/ppermute | solution.py:50
  165.5 13.3 %collective-permute-start.23 = (bf16[16,4096]{1,0:T(8,128)(2,1)S(1)}, bf16[16,4096]{1,0:T(8,128)(2,1)S(1)}, u32[]{:S(2)}, u32[]{:S(2)}) collective-permute-start(bf16[16,4096]{1,0:T(8,128)(2,1)S(1)} %get-tuple-element.61), channel_id=1, source_target_pairs={{0,160},{1,97},{32,192},{33,129},{64,224},{65,161},{96,0},{97,193}... | collective-permute-start | bytes 393224 | tf_op jit(solution)/shard_map/sentences_back/ppermute | solution.py:50
  168.1 13.1 %collective-permute-start.24 = (bf16[16,4096]{1,0:T(8,128)(2,1)S(1)}, bf16[16,4096]{1,0:T(8,128)(2,1)S(1)}, u32[]{:S(2)}, u32[]{:S(2)}) collective-permute-start(bf16[16,4096]{1,0:T(8,128)(2,1)S(1)} %get-tuple-element.62), channel_id=1, source_target_pairs={{0,96},{1,161},{32,128},{33,193},{64,160},{65,225},{96,192},{97,1}... | collective-permute-start | bytes 393224 | tf_op jit(solution)/shard_map/sentences_back/ppermute | solution.py:50
  170.5 11.6 %collective-permute-start.25 = (bf16[16,4096]{1,0:T(8,128)(2,1)S(1)}, bf16[16,4096]{1,0:T(8,128)(2,1)S(1)}, u32[]{:S(2)}, u32[]{:S(2)}) collective-permute-start(bf16[16,4096]{1,0:T(8,128)(2,1)S(1)} %get-tuple-element.63), channel_id=1, source_target_pairs={{0,192},{1,65},{32,224},{33,97},{64,0},{65,129},{96,32},{97,161},{... | collective-permute-start | bytes 393224 | tf_op jit(solution)/shard_map/sentences_back/ppermute | solution.py:50
  172.9 9.2 %collective-permute-start.26 = (bf16[16,4096]{1,0:T(8,128)(2,1)S(1)}, bf16[16,4096]{1,0:T(8,128)(2,1)S(1)}, u32[]{:S(2)}, u32[]{:S(2)}) collective-permute-start(bf16[16,4096]{1,0:T(8,128)(2,1)S(1)} %get-tuple-element.64), channel_id=1, source_target_pairs={{0,64},{1,193},{32,96},{33,225},{64,128},{65,1},{96,160},{97,33},{... | collective-permute-start | bytes 393224 | tf_op jit(solution)/shard_map/sentences_back/ppermute | solution.py:50
  175.1 6.9 %collective-permute-start.27 = (bf16[16,4096]{1,0:T(8,128)(2,1)S(1)}, bf16[16,4096]{1,0:T(8,128)(2,1)S(1)}, u32[]{:S(2)}, u32[]{:S(2)}) collective-permute-start(bf16[16,4096]{1,0:T(8,128)(2,1)S(1)} %get-tuple-element.65), channel_id=1, source_target_pairs={{0,224},{1,33},{32,0},{33,65},{64,32},{65,97},{96,64},{97,129},{12... | collective-permute-start | bytes 393224 | tf_op jit(solution)/shard_map/sentences_back/ppermute | solution.py:50
  178.8 5.0 %collective-permute-start.28 = (bf16[16,4096]{1,0:T(8,128)(2,1)S(1)}, bf16[16,4096]{1,0:T(8,128)(2,1)S(1)}, u32[]{:S(2)}, u32[]{:S(2)}) collective-permute-start(bf16[16,4096]{1,0:T(8,128)(2,1)S(1)} %get-tuple-element.66), channel_id=1, source_target_pairs={{0,32},{1,225},{32,64},{33,1},{64,96},{65,33},{96,128},{97,65},{12... | collective-permute-start | bytes 393224 | tf_op jit(solution)/shard_map/sentences_back/ppermute | solution.py:50
